TPU v7x, 32 devices: a whole 2x2x4 slice. The times are simulated.
32 devices in a mesh: row: 8 (over z, x), col: 2 (over y), seq: 2 (over core).
Axes of the slice: x: 2, y: 2, z: 4, core: 2. Of those that a mesh axis runs over, the one named last changes fastest.
Arguments:
- out_grads: bfloat16 [1, 2048, 32768], P(None, 'seq', 'row'), may hold values from -0.125 to 0.125
- layer_inputs: bfloat16 [1, 2048, 8192], P(None, 'seq', 'col'), may hold values from -6 to 6
- row_bits: int32 [32768], P('row'), may hold values from 0 to 1
- col_bits: int32 [8192], P('col'), may hold values from 0 to 1
- row_blocks: int32 [16], replicated, may hold values from 0 to 511
- col_blocks: int32 [8], replicated, may hold values from 0 to 63
Outputs:
- sketch: float32 [1, 1024, 1024], P(None, 'row', 'col')
Inputs may be any that keep to these rules, and one draw needn't show every extreme that they name: `row_blocks`: blocks may repeat. `col_blocks`: blocks may repeat.
All inputs are finite; a program needn't handle non-finite values.
Results may differ from a plain program's by a relative error of at most 0.0003.
Values sent between devices are 32-bit elements; how exact they have to be, the bound alone decides.
No kernel may reach another device: no remote copies, remote signals or barrier semaphores. Data moves between devices by JAX's collectives and lax.ppermute only.
A program may use at most 128 MiB of HBM per device.

v0:
```python
import functools
import math

import jax
import jax.numpy as jnp
import numpy as np
from jax import lax
from jax.experimental import pallas as pl
from jax.experimental.pallas import tpu as pltpu
from jax.sharding import PartitionSpec as P

FF = 28672
BR = 64
BC = 128
CHUNK = 256
TILE = 256
VMEM_LIMIT = 56 << 20


def scalar_parity(first, second):
    joined = first & second
    for shift in (8, 4, 2, 1):
        joined = joined ^ (joined >> shift)
    return joined & 1


def hadamard_table(order):
    index = np.arange(order)
    joined = index[:, None] & index[None, :]
    parity = sum((joined >> position) & 1 for position in range(order.bit_length()))
    return jnp.asarray(1 - 2 * (parity % 2), dtype=jnp.bfloat16)


def mix_group(parts):
    first, second = parts[0] + parts[1], parts[0] - parts[1]
    third, fourth = parts[2] + parts[3], parts[2] - parts[3]
    return first + third, second + fourth, first - third, second - fourth


def kept_sum(source, slot, sign, width, length, axis):
    per_chunk = CHUNK // width
    inside = slot % per_chunk
    chunk = slot // per_chunk
    low, high = chunk % 4, chunk // 4
    start = pl.multiple_of(inside * width, width)
    total = None
    for group in range(source.shape[0] // 4):
        weight = sign * (1 - 2 * scalar_parity(high, jnp.int32(group))).astype(jnp.float32)
        if axis == 0:
            piece = source[4 * group + low, pl.ds(start, width), :]
        else:
            piece = source[4 * group + low, :, pl.ds(start, width)]
        total = piece * weight if total is None else total + piece * weight
    return total


def store_pieces(values, high_ref, low_ref, where):
    high = values.astype(jnp.bfloat16)
    high_ref[where] = high
    low_ref[where] = (values - high.astype(jnp.float32)).astype(jnp.bfloat16)


def product_blocks(plan, here, left_high, left_low, right_high, right_low, out_ref, first_row, orders):
    rows, width = out_ref.shape[1], out_ref.shape[2]
    tile = min(CHUNK, width)
    span = pl.ds(first_row, plan.rows * rows)
    seq = here[2] % 2
    for start in range(0, plan.cols * width, tile):
        lanes = pl.ds(start, tile)
        total = jnp.dot(left_high[span, :], right_high[:, lanes], preferred_element_type=jnp.float32)
        total += jnp.dot(left_high[span, :], right_low[:, lanes], preferred_element_type=jnp.float32)
        total += jnp.dot(left_low[span, :], right_high[:, lanes], preferred_element_type=jnp.float32)
        col = start // width
        for row in range(plan.rows):
            places = [plan.place(order, row, col) for order in orders]
            place = jnp.where(seq == 0, places[0], places[1]) if places[0] != places[1] else places[0]
            out_ref[place, :, pl.ds(start % width, tile)] = total[row * rows : (row + 1) * rows, :]


def mix_kernel(
    plan, scale, here, row_blocks, col_blocks, grads, inputs, row_bits, col_bits, table,
    out, left_high, left_low, right_high, right_low, row_mixed, col_mixed,
):
    step = pl.program_id(0)
    tokens, row_local = grads.shape
    col_local = inputs.shape[1]
    mixing = table[...]
    index = lax.broadcasted_iota(jnp.int32, (1, row_local), 1) + here[0] * row_local
    row_sign = jnp.where(index < FF, 1 - 2 * row_bits[...], 0).astype(jnp.float32).astype(jnp.bfloat16)
    col_sign = (1 - 2 * col_bits[...]).astype(jnp.float32).astype(jnp.bfloat16)

    for group in range(row_local // CHUNK // 4):
        parts = []
        for chunk in range(4 * group, 4 * group + 4):
            lanes = slice(chunk * CHUNK, (chunk + 1) * CHUNK)
            signed = grads[:, lanes] * row_sign[:, lanes]
            parts.append(
                lax.dot_general(mixing, signed, (((1,), (1,)), ((), ())), preferred_element_type=jnp.float32)
            )
        for at, part in enumerate(mix_group(parts)):
            row_mixed[4 * group + at] = part
    for group in range(col_local // CHUNK // 4):
        parts = []
        for chunk in range(4 * group, 4 * group + 4):
            lanes = slice(chunk * CHUNK, (chunk + 1) * CHUNK)
            signed = inputs[:, lanes] * col_sign[:, lanes]
            parts.append(jnp.dot(signed, mixing, preferred_element_type=jnp.float32))
        for at, part in enumerate(mix_group(parts)):
            col_mixed[4 * group + at] = part

    now = pl.ds(pl.multiple_of(step * tokens, tokens), tokens)
    row_slots = row_local // BR
    inner = plan.per_row // plan.split
    cut = BR * 3 // 4
    for part in range(plan.split):
        base = part * plan.rows * inner * BR
        for row in range(plan.rows):
            for at in range(inner):
                kept = (here[0] ^ row) * plan.per_row + at * plan.split
                if plan.split == 2:
                    kept = kept + (here[2] ^ part)
                block = row_blocks[kept]
                sign = (1 - 2 * scalar_parity(block // row_slots, here[0])).astype(jnp.float32) * scale
                values = kept_sum(row_mixed, block % row_slots, sign, BR, tokens, 0)
                spot = row * inner + at
                first = base + spot * cut
                store_pieces(values[:cut], left_high, left_low, (pl.ds(first, cut), now))
                first = base + plan.rows * inner * cut + spot * (BR - cut)
                store_pieces(values[cut:], left_high, left_low, (pl.ds(first, BR - cut), now))
    col_slots = col_local // BC
    for col in range(plan.cols):
        for at in range(plan.per_col):
            block = col_blocks[(here[1] ^ col) * plan.per_col + at]
            sign = (1 - 2 * scalar_parity(block // col_slots, here[1])).astype(jnp.float32)
            values = kept_sum(col_mixed, block % col_slots, sign, BC, tokens, 1)
            store_pieces(values, right_high, right_low, (now, pl.ds((col * plan.per_col + at) * BC, BC)))

    @pl.when(step == pl.num_programs(0) - 1)
    def _():
        first, orders = plan.first_product()
        product_blocks(plan, here, left_high, left_low, right_high, right_low, out, first, orders)


def product_kernel(plan, wanted, here, left_high, left_low, right_high, right_low, *outs):
    for (first, orders), out in zip(wanted, outs):
        product_blocks(plan, here, left_high, left_low, right_high, right_low, out, first, orders)


class Plan:
    def __init__(self, mesh, row_kept, col_kept):
        self.rows, self.cols, self.seqs = mesh.shape["row"], mesh.shape["col"], mesh.shape["seq"]
        self.split = self.seqs if self.seqs == 2 and (row_kept // self.rows) % 2 == 0 else 1
        self.per_row = row_kept // self.rows
        self.per_col = col_kept // self.cols
        row_bits = [("row", 1 << bit) for bit in range(self.rows.bit_length() - 1)]
        col_bits = [("col", 1 << bit) for bit in range(self.cols.bit_length() - 1)]
        last = row_bits[-1:]
        early = col_bits + row_bits[:-1]
        turn = len(early) - 1 if early else 0
        first = early
        second = early[1:] + early[:1]
        third = early[turn:] + early[:turn]
        self.main = (first + last, second + last)
        self.rest = (third + last, third + last)

    def pairs(self, bits):
        found = []
        for row in range(self.rows):
            for col in range(self.cols):
                for seq in range(self.seqs):
                    axis, mask = bits[seq % 2]
                    other_row = row ^ mask if axis == "row" else row
                    other_col = col ^ mask if axis == "col" else col
                    found.append(
                        (
                            (row * self.cols + col) * self.seqs + seq,
                            (other_row * self.cols + other_col) * self.seqs + seq,
                        )
                    )
        return found

    def place(self, order, row, col):
        spot = 0
        for axis, mask in order:
            spot = spot * 2 + int(bool((row if axis == "row" else col) & mask))
        return spot

    def first_product(self):
        if self.split == 1:
            return 0, self.main
        return self.rows * self.per_row // 2 * BR, self.main[1:] + self.main[:1]

    def halve(self, part, orders, step):
        half = part.shape[0] // 2
        bits = (orders[0][step], orders[1][step])
        return part[:half] + lax.ppermute(part[half:], ("row", "col", "seq"), self.pairs(bits))


def body(plan, out_grads, layer_inputs, row_bits, col_bits, row_blocks, col_blocks):
    tokens, row_local = out_grads.shape[1:]
    col_local = layer_inputs.shape[2]
    tile = min(TILE, tokens)
    here = jnp.stack([lax.axis_index(name) for name in ("row", "col", "seq")]).astype(jnp.int32)
    scale = 1.0 / math.sqrt(row_local * plan.rows * col_local * plan.cols)
    left_rows = plan.rows * plan.per_row * BR
    right_cols = plan.cols * plan.per_col * BC
    inner = plan.per_row // plan.split
    cut = BR * 3 // 4
    cols_each = plan.per_col * BC
    blocks = plan.rows * plan.cols
    smem = pl.BlockSpec(memory_space=pltpu.SMEM)
    vmem = pl.BlockSpec(memory_space=pltpu.VMEM)
    main_shape = jax.ShapeDtypeStruct((blocks, inner * cut, cols_each), jnp.float32)
    rest_shape = jax.ShapeDtypeStruct((blocks, inner * (BR - cut), cols_each), jnp.float32)
    first_out, *factors = pl.pallas_call(
        functools.partial(mix_kernel, plan, scale),
        grid=(tokens // tile,),
        in_specs=[
            smem,
            smem,
            smem,
            pl.BlockSpec((tile, row_local), lambda step: (step, 0)),
            pl.BlockSpec((tile, col_local), lambda step: (step, 0)),
            vmem,
            vmem,
            vmem,
        ],
        out_specs=[vmem] * 5,
        out_shape=[
            main_shape,
            jax.ShapeDtypeStruct((left_rows, tokens), jnp.bfloat16),
            jax.ShapeDtypeStruct((left_rows, tokens), jnp.bfloat16),
            jax.ShapeDtypeStruct((tokens, right_cols), jnp.bfloat16),
            jax.ShapeDtypeStruct((tokens, right_cols), jnp.bfloat16),
        ],
        scratch_shapes=[
            pltpu.VMEM((row_local // CHUNK, CHUNK, tile), jnp.float32),
            pltpu.VMEM((col_local // CHUNK, tile, CHUNK), jnp.float32),
        ],
        compiler_params=pltpu.CompilerParams(vmem_limit_bytes=VMEM_LIMIT),
        name="mix",
    )(
        here,
        row_blocks,
        col_blocks,
        out_grads[0],
        layer_inputs[0],
        row_bits[None],
        col_bits[None],
        hadamard_table(CHUNK),
    )

    def products(wanted, shapes, name):
        return pl.pallas_call(
            functools.partial(product_kernel, plan, wanted),
            in_specs=[smem] + [vmem] * 4,
            out_specs=[vmem] * len(shapes),
            out_shape=shapes,
            compiler_params=pltpu.CompilerParams(vmem_limit_bytes=VMEM_LIMIT),
            name=name,
        )(here, *factors)

    swap = [(0, 1), (1, 0)]
    half_rows = plan.rows * inner * BR
    main_rows = plan.rows * inner * cut
    if plan.split == 2:
        arrived = lax.ppermute(first_out, "seq", swap)
        (mine,) = products([(0, plan.main)], [main_shape], "main_product")
        rest_mine, rest_other = products(
            [(main_rows, plan.rest), (half_rows + main_rows, plan.rest)], [rest_shape] * 2, "rest_products"
        )
        main = mine + arrived
        rest = rest_mine + lax.ppermute(rest_other, "seq", swap)
    else:
        main = first_out
        (rest,) = products([(main_rows, plan.rest)], [rest_shape], "rest_product")
    steps = len(plan.main[0])
    for step in range(steps - 1):
        main = plan.halve(main, plan.main, step)
        rest = plan.halve(rest, plan.rest, step)
    both = plan.halve(jnp.concatenate([main, rest], axis=1), plan.rest, steps - 1)[0]

    def in_rows(values):
        first = values[..., : inner * cut, :].reshape(*values.shape[:-2], inner, cut, cols_each)
        second = values[..., inner * cut :, :].reshape(*values.shape[:-2], inner, BR - cut, cols_each)
        return jnp.concatenate([first, second], axis=-2)

    if plan.split == 2:
        both = in_rows(lax.all_gather(both, "seq", axis=0))
        return both.transpose(1, 0, 2, 3).reshape(1, plan.per_row * BR, cols_each)
    return in_rows(lax.psum(both, "seq")).reshape(1, plan.per_row * BR, cols_each)


def solution(mesh):
    def run(out_grads, layer_inputs, row_bits, col_bits, row_blocks, col_blocks):
        plan = Plan(mesh, row_blocks.shape[0], col_blocks.shape[0])
        in_specs = (P(None, "seq", "row"), P(None, "seq", "col"), P("row"), P("col"), P(), P())
        return jax.shard_map(
            lambda *args: body(plan, *args),
            mesh=mesh,
            in_specs=in_specs,
            out_specs=P(None, "row", "col"),
            check_vma=False,
        )(out_grads, layer_inputs, row_bits, col_bits, row_blocks, col_blocks)

    return run
```

profile of v0, /device:TPU:0, one launch (start us, length us, event | category | flops | bytes accessed | tf_op | source)
XLA Modules:
  0.0 74.2 jit_solution(8375086433511301742)
XLA Ops:
  0.0 0.6 pad_add_fusion.here
  0.6 18.9 %mix.1 = (f32[16,48,512]{2,1,0:T(8,128)}, bf16[1024,1024]{1,0:T(8,128)(2,1)}, bf16[1024,1024]{1,0:T(8,128)(2,1)}, bf16[1024,1024]{1,0:T(8,128)(2,1)}, bf16[1024,1024]{1,0:T(8,128)(2,1)}) custom-call(s32[3]{0:T(128)} %pad_add_fusion.here, s32[16]{0:T(128)} %row_blocks.1, s32[8]{0:T(128)} %col_blocks.1, bf16[1024,4096]{1,0:T(8,128)(2,1)} %bitcast.12, ...), custom_call_target="tpu_custom_call" | custom-call | tf_op jit(solution)/shard_map/mix/pallas_call | solution.py:215
  19.5 0.5 collective-permute-start
  20.0 7.2 %main_product.1 = f32[16,48,512]{2,1,0:T(8,128)} custom-call(s32[3]{0:T(128)} %pad_add_fusion.here, bf16[1024,1024]{1,0:T(8,128)(2,1)} %get-tuple-element.12.left_high, bf16[1024,1024]{1,0:T(8,128)(2,1)} %get-tuple-element.13.left_low, bf16[1024,1024]{1,0:T(8,128)(2,1)} %get-tuple-element.14.right_high, bf16[1024,1024]{1,0:T(8,128)(2,1)} %get-tuple-element.15.right_low), custom_call_target="tpu_custom_call" | custom-call | tf_op jit(solution)/shard_map/main_product/pallas_call | solution.py:254
  27.2 0.0 collective-permute-done
  27.2 1.8 %add.27 = f32[16,48,512]{2,1,0:T(8,128)S(1)} add(f32[16,48,512]{2,1,0:T(8,128)} %main_product.1, f32[16,48,512]{2,1,0:T(8,128)S(1)} %collective-permute-done) | non-fusion elementwise | flops 393216 | bytes 4718592 | tf_op jit(solution)/shard_map/add | solution.py:272
  29.0 0.1 slice.65
  29.1 2.6 %collective-permute-start.1 = (f32[8,48,512]{2,1,0:T(8,128)S(1)}, f32[8,48,512]{2,1,0:T(8,128)S(1)}, u32[]{:S(2)}, u32[]{:S(2)}) collective-permute-start(f32[8,48,512]{2,1,0:T(8,128)S(1)} %slice.65), channel_id=1, source_target_pairs={{0,2},{1,5},{2,0},{3,7},{4,6},{5,1},{6,4},{7,3},{8,10},{9,13},{10,... | collective-permute-start | bytes 2359304 | tf_op jit(solution)/shard_map/ppermute | solution.py:196
  31.7 6.1 %rest_products.1 = (f32[16,16,512]{2,1,0:T(8,128)}, f32[16,16,512]{2,1,0:T(8,128)}) custom-call(s32[3]{0:T(128)} %pad_add_fusion.here, bf16[1024,1024]{1,0:T(8,128)(2,1)} %get-tuple-element.12.left_high, bf16[1024,1024]{1,0:T(8,128)(2,1)} %get-tuple-element.13.left_low, bf16[1024,1024]{1,0:T(8,128)(2,1)} %get-tuple-element.14.right_high, ...), custom_call_target="tpu_custom_call" | custom-call | tf_op jit(solution)/shard_map/rest_products/pallas_call | solution.py:254
  37.8 0.2 collective-permute-start.4
  38.0 1.9 %collective-permute-done.4 = f32[16,16,512]{2,1,0:T(8,128)S(1)} collective-permute-done((f32[16,16,512]{2,1,0:T(8,128)}, f32[16,16,512]{2,1,0:T(8,128)S(1)}, u32[]{:S(2)}, u32[]{:S(2)}) %collective-permute-start.4) | collective-permute-done | bytes 524320 | tf_op jit(solution)/shard_map/ppermute | solution.py:273
  39.9 1.1 %add.31 = f32[16,16,512]{2,1,0:T(8,128)S(1)} add(f32[16,16,512]{2,1,0:T(8,128)} %get-tuple-element.17, f32[16,16,512]{2,1,0:T(8,128)S(1)} %collective-permute-done.4) | non-fusion elementwise | flops 131072 | bytes 1572864 | tf_op jit(solution)/shard_map/add | solution.py:273
  41.1 1.7 %collective-permute-start.5 = (f32[8,16,512]{2,1,0:T(8,128)S(1)}, f32[8,16,512]{2,1,0:T(8,128)S(1)}, u32[]{:S(2)}, u32[]{:S(2)}) collective-permute-start(f32[8,16,512]{2,1,0:T(8,128)S(1)} %slice.71), channel_id=1, source_target_pairs={{0,8},{1,9},{2,10},{3,11},{4,12},{5,13},{6,14},{7,15},{8,0},{9,1},... | collective-permute-start | bytes 786440 | tf_op jit(solution)/shard_map/ppermute | solution.py:196
  42.7 0.0 collective-permute-done.1
  42.7 0.1 slice_add_fusion
  42.9 1.5 %collective-permute-start.2 = (f32[4,48,512]{2,1,0:T(8,128)S(1)}, f32[4,48,512]{2,1,0:T(8,128)S(1)}, u32[]{:S(2)}, u32[]{:S(2)}) collective-permute-start(f32[4,48,512]{2,1,0:T(8,128)S(1)} %slice.67), channel_id=1, source_target_pairs={{0,4},{1,9},{2,6},{3,11},{4,0},{5,13},{6,2},{7,15},{8,12},{9,1},{1... | collective-permute-start | bytes 1179656 | tf_op jit(solution)/shard_map/ppermute | solution.py:196
  44.5 5.8 %collective-permute-done.5 = f32[8,16,512]{2,1,0:T(8,128)S(1)} collective-permute-done((f32[8,16,512]{2,1,0:T(8,128)S(1)}, f32[8,16,512]{2,1,0:T(8,128)S(1)}, u32[]{:S(2)}, u32[]{:S(2)}) %collective-permute-start.5) | collective-permute-done | bytes 262176 | tf_op jit(solution)/shard_map/ppermute | solution.py:196
  50.4 1.4 %collective-permute-start.6 = (f32[4,16,512]{2,1,0:T(8,128)S(1)}, f32[4,16,512]{2,1,0:T(8,128)S(1)}, u32[]{:S(2)}, u32[]{:S(2)}) collective-permute-start(f32[4,16,512]{2,1,0:T(8,128)S(1)} %slice.73), channel_id=1, source_target_pairs={{0,2},{1,3},{2,0},{3,1},{4,6},{5,7},{6,4},{7,5},{8,10},{9,11},{10,... | collective-permute-start | bytes 393224 | tf_op jit(solution)/shard_map/ppermute | solution.py:196
  51.7 3.6 %collective-permute-done.6 = f32[4,16,512]{2,1,0:T(8,128)S(1)} collective-permute-done((f32[4,16,512]{2,1,0:T(8,128)S(1)}, f32[4,16,512]{2,1,0:T(8,128)S(1)}, u32[]{:S(2)}, u32[]{:S(2)}) %collective-permute-start.6) | collective-permute-done | bytes 131104 | tf_op jit(solution)/shard_map/ppermute | solution.py:196
  55.4 1.6 %collective-permute-start.7 = (f32[2,16,512]{2,1,0:T(8,128)S(1)}, f32[2,16,512]{2,1,0:T(8,128)S(1)}, u32[]{:S(2)}, u32[]{:S(2)}) collective-permute-start(f32[2,16,512]{2,1,0:T(8,128)S(1)} %slice.75), channel_id=1, source_target_pairs={{0,4},{1,5},{2,6},{3,7},{4,0},{5,1},{6,2},{7,3},{8,12},{9,13},{10,... | collective-permute-start | bytes 196616 | tf_op jit(solution)/shard_map/ppermute | solution.py:196
  57.0 0.0 collective-permute-done.2
  57.0 0.1 slice_add_fusion.1
  57.1 1.6 %collective-permute-start.3 = (f32[2,48,512]{2,1,0:T(8,128)S(1)}, f32[2,48,512]{2,1,0:T(8,128)S(1)}, u32[]{:S(2)}, u32[]{:S(2)}) collective-permute-start(f32[2,48,512]{2,1,0:T(8,128)S(1)} %slice.69), channel_id=1, source_target_pairs={{0,8},{1,3},{2,10},{3,1},{4,12},{5,7},{6,14},{7,5},{8,0},{9,11},{1... | collective-permute-start | bytes 589832 | tf_op jit(solution)/shard_map/ppermute | solution.py:196
  58.7 1.0 %collective-permute-done.7 = f32[2,16,512]{2,1,0:T(8,128)S(1)} collective-permute-done((f32[2,16,512]{2,1,0:T(8,128)S(1)}, f32[2,16,512]{2,1,0:T(8,128)S(1)}, u32[]{:S(2)}, u32[]{:S(2)}) %collective-permute-start.7) | collective-permute-done | bytes 65568 | tf_op jit(solution)/shard_map/ppermute | solution.py:196
  59.8 4.4 %collective-permute-done.3 = f32[2,48,512]{2,1,0:T(8,128)S(1)} collective-permute-done((f32[2,48,512]{2,1,0:T(8,128)S(1)}, f32[2,48,512]{2,1,0:T(8,128)S(1)}, u32[]{:S(2)}, u32[]{:S(2)}) %collective-permute-start.3) | collective-permute-done | bytes 196640 | tf_op jit(solution)/shard_map/ppermute | solution.py:196
  64.2 2.7 %collective-permute-start.8 = (f32[1,64,512]{2,1,0:T(8,128)S(1)}, f32[1,64,512]{2,1,0:T(8,128)S(1)}, u32[]{:S(2)}, u32[]{:S(2)}) collective-permute-start(f32[1,64,512]{2,1,0:T(8,128)S(1)} %pad_maximum_fusion.1), channel_id=1, source_target_pairs={{0,16},{1,17},{2,18},{3,19},{4,20},{5,21},{6,22},{7,23},{8,24},{9,... | collective-permute-start | bytes 393224 | tf_op jit(solution)/shard_map/ppermute | solution.py:196
  66.9 4.6 %collective-permute-done.8 = f32[1,64,512]{2,1,0:T(8,128)S(1)} collective-permute-done((f32[1,64,512]{2,1,0:T(8,128)S(1)}, f32[1,64,512]{2,1,0:T(8,128)S(1)}, u32[]{:S(2)}, u32[]{:S(2)}) %collective-permute-start.8) | collective-permute-done | bytes 131104 | tf_op jit(solution)/shard_map/ppermute | solution.py:196
  71.5 2.0 %all_gather.3 = f32[2,64,512]{2,1,0:T(8,128)S(1)} all-gather(f32[1,64,512]{2,1,0:T(8,128)S(1)} %fusion.1), channel_id=1, replica_groups=mesh['row'=8,'col'=2,'seq'=2] {'seq'}, dimensions={0}, use_global_device_ids=true | all-gather | bytes 393216 | tf_op jit(solution)/shard_map/all_gather | solution.py:289
  73.5 0.7 pad_maximum_fusion
  (13 shorter events, 0.2 us)
Async XLA Ops:
  19.5 7.7 %collective-permute-start = (f32[16,48,512]{2,1,0:T(8,128)}, f32[16,48,512]{2,1,0:T(8,128)S(1)}, u32[]{:S(2)}, u32[]{:S(2)}) collective-permute-start(f32[16,48,512]{2,1,0:T(8,128)} %get-tuple-element.16), channel_id=1, source_target_pairs={{0,1},{1,0},{2,3},{3,2},{4,5},{5,4},{6,7},{7,6},{8,9},{9,8},{10,11... | collective-permute-start | bytes 4718600 | tf_op jit(solution)/shard_map/ppermute | solution.py:267
  29.1 13.6 %collective-permute-start.1 = (f32[8,48,512]{2,1,0:T(8,128)S(1)}, f32[8,48,512]{2,1,0:T(8,128)S(1)}, u32[]{:S(2)}, u32[]{:S(2)}) collective-permute-start(f32[8,48,512]{2,1,0:T(8,128)S(1)} %slice.65), channel_id=1, source_target_pairs={{0,2},{1,5},{2,0},{3,7},{4,6},{5,1},{6,4},{7,3},{8,10},{9,13},{10,... | collective-permute-start | bytes 2359304 | tf_op jit(solution)/shard_map/ppermute | solution.py:196
  37.8 2.1 %collective-permute-start.4 = (f32[16,16,512]{2,1,0:T(8,128)}, f32[16,16,512]{2,1,0:T(8,128)S(1)}, u32[]{:S(2)}, u32[]{:S(2)}) collective-permute-start(f32[16,16,512]{2,1,0:T(8,128)} %get-tuple-element.18), channel_id=1, source_target_pairs={{0,1},{1,0},{2,3},{3,2},{4,5},{5,4},{6,7},{7,6},{8,9},{9,8},{10,11... | collective-permute-start | bytes 1572872 | tf_op jit(solution)/shard_map/ppermute | solution.py:273
  41.1 9.2 %collective-permute-start.5 = (f32[8,16,512]{2,1,0:T(8,128)S(1)}, f32[8,16,512]{2,1,0:T(8,128)S(1)}, u32[]{:S(2)}, u32[]{:S(2)}) collective-permute-start(f32[8,16,512]{2,1,0:T(8,128)S(1)} %slice.71), channel_id=1, source_target_pairs={{0,8},{1,9},{2,10},{3,11},{4,12},{5,13},{6,14},{7,15},{8,0},{9,1},... | collective-permute-start | bytes 786440 | tf_op jit(solution)/shard_map/ppermute | solution.py:196
  42.9 14.1 %collective-permute-start.2 = (f32[4,48,512]{2,1,0:T(8,128)S(1)}, f32[4,48,512]{2,1,0:T(8,128)S(1)}, u32[]{:S(2)}, u32[]{:S(2)}) collective-permute-start(f32[4,48,512]{2,1,0:T(8,128)S(1)} %slice.67), channel_id=1, source_target_pairs={{0,4},{1,9},{2,6},{3,11},{4,0},{5,13},{6,2},{7,15},{8,12},{9,1},{1... | collective-permute-start | bytes 1179656 | tf_op jit(solution)/shard_map/ppermute | solution.py:196
  50.4 5.0 %collective-permute-start.6 = (f32[4,16,512]{2,1,0:T(8,128)S(1)}, f32[4,16,512]{2,1,0:T(8,128)S(1)}, u32[]{:S(2)}, u32[]{:S(2)}) collective-permute-start(f32[4,16,512]{2,1,0:T(8,128)S(1)} %slice.73), channel_id=1, source_target_pairs={{0,2},{1,3},{2,0},{3,1},{4,6},{5,7},{6,4},{7,5},{8,10},{9,11},{10,... | collective-permute-start | bytes 393224 | tf_op jit(solution)/shard_map/ppermute | solution.py:196
  55.4 4.3 %collective-permute-start.7 = (f32[2,16,512]{2,1,0:T(8,128)S(1)}, f32[2,16,512]{2,1,0:T(8,128)S(1)}, u32[]{:S(2)}, u32[]{:S(2)}) collective-permute-start(f32[2,16,512]{2,1,0:T(8,128)S(1)} %slice.75), channel_id=1, source_target_pairs={{0,4},{1,5},{2,6},{3,7},{4,0},{5,1},{6,2},{7,3},{8,12},{9,13},{10,... | collective-permute-start | bytes 196616 | tf_op jit(solution)/shard_map/ppermute | solution.py:196
  57.1 7.1 %collective-permute-start.3 = (f32[2,48,512]{2,1,0:T(8,128)S(1)}, f32[2,48,512]{2,1,0:T(8,128)S(1)}, u32[]{:S(2)}, u32[]{:S(2)}) collective-permute-start(f32[2,48,512]{2,1,0:T(8,128)S(1)} %slice.69), channel_id=1, source_target_pairs={{0,8},{1,3},{2,10},{3,1},{4,12},{5,7},{6,14},{7,5},{8,0},{9,11},{1... | collective-permute-start | bytes 589832 | tf_op jit(solution)/shard_map/ppermute | solution.py:196
  64.2 7.3 %collective-permute-start.8 = (f32[1,64,512]{2,1,0:T(8,128)S(1)}, f32[1,64,512]{2,1,0:T(8,128)S(1)}, u32[]{:S(2)}, u32[]{:S(2)}) collective-permute-start(f32[1,64,512]{2,1,0:T(8,128)S(1)} %pad_maximum_fusion.1), channel_id=1, source_target_pairs={{0,16},{1,17},{2,18},{3,19},{4,20},{5,21},{6,22},{7,23},{8,24},{9,... | collective-permute-start | bytes 393224 | tf_op jit(solution)/shard_map/ppermute | solution.py:196
where the time goes:
time: 74.4 us; the launch traced here: 74.2 us
  Pallas kernels  32.2 us (43%)
  waiting for transfers between devices  21.4 us (29%)
  starting transfers between devices  13.8 us (19%)
  other arithmetic  4.61 us (6%)
  blocking collectives  1.99 us (3%)
    ppermute x7, waiting for transfers between devices, halve(): lax.ppermute(part[half:], ('row', 'col', 'seq'), self.pairs(bits))  19.4 us
    pallas_call x1, Pallas kernels, body(): pl.pallas_call(functools.partial(mix_kernel, plan, scale), grid=(tokens /...  18.9 us
    pallas_call x2, Pallas kernels, products(): pl.pallas_call(functools.partial(product_kernel, plan, wanted), in_specs=...  13.3 us
    ppermute x7, starting transfers between devices, halve(): lax.ppermute(part[half:], ('row', 'col', 'seq'), self.pairs(bits))  13.1 us
    all_gather x1, blocking collectives, body(): both = in_rows(lax.all_gather(both, 'seq', axis=0))  1.99 us
    ppermute x1, waiting for transfers between devices, body(): rest = rest_mine + lax.ppermute(rest_other, 'seq', swap)  1.93 us
    add x1, other arithmetic, body(): main = mine + arrived  1.8 us
  transfers between devices with their start and end apart: 9, of which 6 were waited for; matrix products, arithmetic and copies ran while one was open for 2% of the time, Pallas kernels for 18%

commit v1 on v0

--- a/solution.py
+++ b/solution.py
@@ -14,7 +14,8 @@
 BC = 128
 CHUNK = 256
 TILE = 256
-VMEM_LIMIT = 56 << 20
+MIX_VMEM = 30 << 20
+PRODUCT_VMEM = 16 << 20
 
 
 def scalar_parity(first, second):
@@ -228,16 +229,16 @@
         out_specs=[vmem] * 5,
         out_shape=[
             main_shape,
-            jax.ShapeDtypeStruct((left_rows, tokens), jnp.bfloat16),
-            jax.ShapeDtypeStruct((left_rows, tokens), jnp.bfloat16),
-            jax.ShapeDtypeStruct((tokens, right_cols), jnp.bfloat16),
-            jax.ShapeDtypeStruct((tokens, right_cols), jnp.bfloat16),
+            pltpu.VMEM((left_rows, tokens), jnp.bfloat16),
+            pltpu.VMEM((left_rows, tokens), jnp.bfloat16),
+            pltpu.VMEM((tokens, right_cols), jnp.bfloat16),
+            pltpu.VMEM((tokens, right_cols), jnp.bfloat16),
         ],
         scratch_shapes=[
             pltpu.VMEM((row_local // CHUNK, CHUNK, tile), jnp.float32),
             pltpu.VMEM((col_local // CHUNK, tile, CHUNK), jnp.float32),
         ],
-        compiler_params=pltpu.CompilerParams(vmem_limit_bytes=VMEM_LIMIT),
+        compiler_params=pltpu.CompilerParams(vmem_limit_bytes=MIX_VMEM),
         name="mix",
     )(
         here,
@@ -256,7 +257,7 @@
             in_specs=[smem] + [vmem] * 4,
             out_specs=[vmem] * len(shapes),
             out_shape=shapes,
-            compiler_params=pltpu.CompilerParams(vmem_limit_bytes=VMEM_LIMIT),
+            compiler_params=pltpu.CompilerParams(vmem_limit_bytes=PRODUCT_VMEM),
             name=name,
         )(here, *factors)
 

time: 74.4 us -> 64.6 us (0.87)
  Pallas kernels: 32.2 us -> 20.1 us
  local copies, waits for them, and re-layouts: 0.15 us -> 7.18 us
  other arithmetic: 4.61 us -> 1.55 us
  waiting for transfers between devices: 21.4 us -> 19.1 us
    pallas_call x2, Pallas kernels: 13.3 us -> 5.49 us  [products(): pl.pallas_call(functools.partial(product_kernel, plan, wanted), in_specs=...]
    unnamed x0 -> x12, local copies, waits for them, and re-layouts: none -> 7.03 us
    pallas_call x1, Pallas kernels: 18.9 us -> 14.7 us  [body(): pl.pallas_call(functools.partial(mix_kernel, plan, scale), grid=(tokens /...]
    ppermute x7, waiting for transfers between devices: 19.4 us -> 17.2 us  [halve(): lax.ppermute(part[half:], ('row', 'col', 'seq'), self.pairs(bits))]
    add x1, other arithmetic: 1.8 us -> 0.34 us  [body(): main = mine + arrived]
    add x1, other arithmetic: 1.12 us -> 0.08 us  [body(): rest = rest_mine + lax.ppermute(rest_other, 'seq', swap)]
  transfers between devices with their start and end apart: 9 -> 9, of which waited for: 6 -> 7; matrix products, arithmetic and copies ran while one was open for 2% -> 1% of each run, Pallas kernels for 18% -> 9%
where the time goes in v1:
time: 64.6 us; the launch traced here: 64.3 us
  Pallas kernels  20.1 us (31%)
  waiting for transfers between devices  19.1 us (30%)
  starting transfers between devices  14.2 us (22%)
  local copies, waits for them, and re-layouts  7.18 us (11%)
  blocking collectives  1.99 us (3%)
  other arithmetic  1.55 us (2%)
    ppermute x7, waiting for transfers between devices, halve(): lax.ppermute(part[half:], ('row', 'col', 'seq'), self.pairs(bits))  17.2 us
    pallas_call x1, Pallas kernels, body(): pl.pallas_call(functools.partial(mix_kernel, plan, scale), grid=(tokens /...  14.7 us
    ppermute x7, starting transfers between devices, halve(): lax.ppermute(part[half:], ('row', 'col', 'seq'), self.pairs(bits))  13.6 us
    unnamed x12, local copies, waits for them, and re-layouts  7.03 us
    pallas_call x2, Pallas kernels, products(): pl.pallas_call(functools.partial(product_kernel, plan, wanted), in_specs=...  5.49 us
    all_gather x1, blocking collectives, body(): both = in_rows(lax.all_gather(both, 'seq', axis=0))  1.99 us
    ppermute x1, waiting for transfers between devices, body(): rest = rest_mine + lax.ppermute(rest_other, 'seq', swap)  1.9 us
  transfers between devices with their start and end apart: 9, of which 7 were waited for; matrix products, arithmetic and copies ran while one was open for 1% of the time, Pallas kernels for 9%

profile of v1, /device:TPU:0, one launch (start us, length us, event | category | flops | bytes accessed | tf_op | source)
XLA Modules:
  0.0 64.3 jit_solution(11945761854285454364)
XLA Ops:
  0.0 0.1 pad_add_fusion.here
  0.1 3.4 %copy-done = bf16[1,1024,4096]{2,1,0:T(8,128)(2,1)S(1)} copy-done((bf16[1,1024,4096]{2,1,0:T(8,128)(2,1)S(1)}, bf16[1,1024,4096]{2,1,0:T(8,128)(2,1)}, u32[]{:S(2)}) %copy-start) | copy-done | bytes 8388632
  3.5 0.9 %copy-done.1 = bf16[256,256]{1,0:T(8,128)(2,1)S(1)} copy-done((bf16[256,256]{1,0:T(8,128)(2,1)S(1)}, bf16[256,256]{1,0:T(8,128)(2,1)}, u32[]{:S(2)}) %copy-start.1) | copy-done | bytes 131096
  4.4 0.7 %copy-done.2 = s32[4096]{0:T(1024)S(1)} copy-done((s32[4096]{0:T(1024)S(1)}, s32[4096]{0:T(1024)}, u32[]{:S(2)}) %copy-start.2) | copy-done | bytes 16408
  5.1 0.7 %copy-done.3 = s32[4096]{0:T(1024)S(1)} copy-done((s32[4096]{0:T(1024)S(1)}, s32[4096]{0:T(1024)}, u32[]{:S(2)}) %copy-start.3) | copy-done | bytes 16408
  5.8 0.7 %copy-done.4 = s32[16]{0:T(128)S(1)} copy-done((s32[16]{0:T(128)S(1)}, s32[16]{0:T(128)}, u32[]{:S(2)}) %copy-start.4) | copy-done | bytes 88
  6.5 0.7 %copy-done.5 = s32[8]{0:T(128)S(1)} copy-done((s32[8]{0:T(128)S(1)}, s32[8]{0:T(128)}, u32[]{:S(2)}) %copy-start.5) | copy-done | bytes 56
  7.1 14.7 %mix.1 = (f32[16,48,512]{2,1,0:T(8,128)S(1)}, bf16[1024,1024]{1,0:T(8,128)(2,1)S(1)}, bf16[1024,1024]{1,0:T(8,128)(2,1)S(1)}, bf16[1024,1024]{1,0:T(8,128)(2,1)S(1)}, bf16[1024,1024]{1,0:T(8,128)(2,1)S(1)}) custom-call(s32[3]{0:T(128)S(1)} %pad_add_fusion.here, s32[16]{0:T(128)S(1)} %copy-done.4, s32[8]{0:T(128)S(1)} %copy-done.5, ...), custom_call_target="tpu_custom_call" | custom-call | tf_op jit(solution)/shard_map/mix/pallas_call | solution.py:216
  21.8 0.5 collective-permute-start
  22.3 3.1 %main_product.1 = f32[16,48,512]{2,1,0:T(8,128)S(1)} custom-call(s32[3]{0:T(128)S(1)} %pad_add_fusion.here, bf16[1024,1024]{1,0:T(8,128)(2,1)S(1)} %get-tuple-element.12.left_high, bf16[1024,1024]{1,0:T(8,128)(2,1)S(1)} %get-tuple-element.13.left_low, bf16[1024,1024]{1,0:T(8,128)(2,1)S(1)} %get-tuple-element.14.right_high, ...), custom_call_target="tpu_custom_call" | custom-call | tf_op jit(solution)/shard_map/main_product/pallas_call | solution.py:255
  25.5 0.3 add.27
  25.9 2.8 %collective-permute-start.1 = (f32[8,48,512]{2,1,0:T(8,128)S(1)}, f32[8,48,512]{2,1,0:T(8,128)S(1)}, u32[]{:S(2)}, u32[]{:S(2)}) collective-permute-start(f32[8,48,512]{2,1,0:T(8,128)S(1)} %slice.65), channel_id=1, source_target_pairs={{0,2},{1,5},{2,0},{3,7},{4,6},{5,1},{6,4},{7,3},{8,10},{9,13},{10,... | collective-permute-start | bytes 2359304 | tf_op jit(solution)/shard_map/ppermute | solution.py:197
  28.7 2.3 %rest_products.1 = (f32[16,16,512]{2,1,0:T(8,128)S(1)}, f32[16,16,512]{2,1,0:T(8,128)S(1)}) custom-call(s32[3]{0:T(128)S(1)} %pad_add_fusion.here, bf16[1024,1024]{1,0:T(8,128)(2,1)S(1)} %get-tuple-element.12.left_high, bf16[1024,1024]{1,0:T(8,128)(2,1)S(1)} %get-tuple-element.13.left_low, bf16[1024,1024]{1,0:T(8,128)(2,1)S(1)} %get-tuple-element.14.right_high, ...), custom_call_target="tpu_custom_call" | custom-call | tf_op jit(solution)/shard_map/rest_products/pallas_call | solution.py:255
  31.1 0.1 collective-permute-start.4
  31.1 1.9 %collective-permute-done.4 = f32[16,16,512]{2,1,0:T(8,128)S(1)} collective-permute-done((f32[16,16,512]{2,1,0:T(8,128)S(1)}, f32[16,16,512]{2,1,0:T(8,128)S(1)}, u32[]{:S(2)}, u32[]{:S(2)}) %collective-permute-start.4) | collective-permute-done | bytes 524320 | tf_op jit(solution)/shard_map/ppermute | solution.py:274
  33.0 0.1 add.31
  33.1 1.6 %collective-permute-start.5 = (f32[8,16,512]{2,1,0:T(8,128)S(1)}, f32[8,16,512]{2,1,0:T(8,128)S(1)}, u32[]{:S(2)}, u32[]{:S(2)}) collective-permute-start(f32[8,16,512]{2,1,0:T(8,128)S(1)} %slice.71), channel_id=1, source_target_pairs={{0,8},{1,9},{2,10},{3,11},{4,12},{5,13},{6,14},{7,15},{8,0},{9,1},... | collective-permute-start | bytes 786440 | tf_op jit(solution)/shard_map/ppermute | solution.py:197
  34.8 3.9 %collective-permute-done.1 = f32[8,48,512]{2,1,0:T(8,128)S(1)} collective-permute-done((f32[8,48,512]{2,1,0:T(8,128)S(1)}, f32[8,48,512]{2,1,0:T(8,128)S(1)}, u32[]{:S(2)}, u32[]{:S(2)}) %collective-permute-start.1) | collective-permute-done | bytes 786464 | tf_op jit(solution)/shard_map/ppermute | solution.py:197
  38.7 0.1 slice_add_fusion
  38.9 2.1 %collective-permute-start.2 = (f32[4,48,512]{2,1,0:T(8,128)S(1)}, f32[4,48,512]{2,1,0:T(8,128)S(1)}, u32[]{:S(2)}, u32[]{:S(2)}) collective-permute-start(f32[4,48,512]{2,1,0:T(8,128)S(1)} %slice.67), channel_id=1, source_target_pairs={{0,4},{1,9},{2,6},{3,11},{4,0},{5,13},{6,2},{7,15},{8,12},{9,1},{1... | collective-permute-start | bytes 1179656 | tf_op jit(solution)/shard_map/ppermute | solution.py:197
  40.9 0.9 %collective-permute-done.5 = f32[8,16,512]{2,1,0:T(8,128)S(1)} collective-permute-done((f32[8,16,512]{2,1,0:T(8,128)S(1)}, f32[8,16,512]{2,1,0:T(8,128)S(1)}, u32[]{:S(2)}, u32[]{:S(2)}) %collective-permute-start.5) | collective-permute-done | bytes 262176 | tf_op jit(solution)/shard_map/ppermute | solution.py:197
  41.9 1.2 %collective-permute-start.6 = (f32[4,16,512]{2,1,0:T(8,128)S(1)}, f32[4,16,512]{2,1,0:T(8,128)S(1)}, u32[]{:S(2)}, u32[]{:S(2)}) collective-permute-start(f32[4,16,512]{2,1,0:T(8,128)S(1)} %slice.73), channel_id=1, source_target_pairs={{0,2},{1,3},{2,0},{3,1},{4,6},{5,7},{6,4},{7,5},{8,10},{9,11},{10,... | collective-permute-start | bytes 393224 | tf_op jit(solution)/shard_map/ppermute | solution.py:197
  43.0 3.9 %collective-permute-done.6 = f32[4,16,512]{2,1,0:T(8,128)S(1)} collective-permute-done((f32[4,16,512]{2,1,0:T(8,128)S(1)}, f32[4,16,512]{2,1,0:T(8,128)S(1)}, u32[]{:S(2)}, u32[]{:S(2)}) %collective-permute-start.6) | collective-permute-done | bytes 131104 | tf_op jit(solution)/shard_map/ppermute | solution.py:197
  46.9 1.4 %collective-permute-start.7 = (f32[2,16,512]{2,1,0:T(8,128)S(1)}, f32[2,16,512]{2,1,0:T(8,128)S(1)}, u32[]{:S(2)}, u32[]{:S(2)}) collective-permute-start(f32[2,16,512]{2,1,0:T(8,128)S(1)} %slice.75), channel_id=1, source_target_pairs={{0,4},{1,5},{2,6},{3,7},{4,0},{5,1},{6,2},{7,3},{8,12},{9,13},{10,... | collective-permute-start | bytes 196616 | tf_op jit(solution)/shard_map/ppermute | solution.py:197
  48.3 0.1 slice_add_fusion.1
  48.4 1.6 %collective-permute-start.3 = (f32[2,48,512]{2,1,0:T(8,128)S(1)}, f32[2,48,512]{2,1,0:T(8,128)S(1)}, u32[]{:S(2)}, u32[]{:S(2)}) collective-permute-start(f32[2,48,512]{2,1,0:T(8,128)S(1)} %slice.69), channel_id=1, source_target_pairs={{0,8},{1,3},{2,10},{3,1},{4,12},{5,7},{6,14},{7,5},{8,0},{9,11},{1... | collective-permute-start | bytes 589832 | tf_op jit(solution)/shard_map/ppermute | solution.py:197
  50.0 1.2 %collective-permute-done.7 = f32[2,16,512]{2,1,0:T(8,128)S(1)} collective-permute-done((f32[2,16,512]{2,1,0:T(8,128)S(1)}, f32[2,16,512]{2,1,0:T(8,128)S(1)}, u32[]{:S(2)}, u32[]{:S(2)}) %collective-permute-start.7) | collective-permute-done | bytes 65568 | tf_op jit(solution)/shard_map/ppermute | solution.py:197
  51.3 2.9 %collective-permute-done.3 = f32[2,48,512]{2,1,0:T(8,128)S(1)} collective-permute-done((f32[2,48,512]{2,1,0:T(8,128)S(1)}, f32[2,48,512]{2,1,0:T(8,128)S(1)}, u32[]{:S(2)}, u32[]{:S(2)}) %collective-permute-start.3) | collective-permute-done | bytes 196640 | tf_op jit(solution)/shard_map/ppermute | solution.py:197
  54.2 2.9 %collective-permute-start.8 = (f32[1,64,512]{2,1,0:T(8,128)S(1)}, f32[1,64,512]{2,1,0:T(8,128)S(1)}, u32[]{:S(2)}, u32[]{:S(2)}) collective-permute-start(f32[1,64,512]{2,1,0:T(8,128)S(1)} %pad_maximum_fusion.1), channel_id=1, source_target_pairs={{0,16},{1,17},{2,18},{3,19},{4,20},{5,21},{6,22},{7,23},{8,24},{9,... | collective-permute-start | bytes 393224 | tf_op jit(solution)/shard_map/ppermute | solution.py:197
  57.1 4.4 %collective-permute-done.8 = f32[1,64,512]{2,1,0:T(8,128)S(1)} collective-permute-done((f32[1,64,512]{2,1,0:T(8,128)S(1)}, f32[1,64,512]{2,1,0:T(8,128)S(1)}, u32[]{:S(2)}, u32[]{:S(2)}) %collective-permute-start.8) | collective-permute-done | bytes 131104 | tf_op jit(solution)/shard_map/ppermute | solution.py:197
  61.6 2.0 %all_gather.3 = f32[2,64,512]{2,1,0:T(8,128)S(1)} all-gather(f32[1,64,512]{2,1,0:T(8,128)S(1)} %fusion.1), channel_id=1, replica_groups=mesh['row'=8,'col'=2,'seq'=2] {'seq'}, dimensions={0}, use_global_device_ids=true | all-gather | bytes 393216 | tf_op jit(solution)/shard_map/all_gather | solution.py:290
  63.6 0.7 %pad_maximum_fusion = f32[2,1,64,512]{3,2,0,1:T(8,128)} fusion(f32[2,1,16,512]{3,2,0,1:T(8,128)S(1)} %slice_bitcast_fusion.1, f32[2,1,48,512]{3,2,0,1:T(8,128)S(1)} %slice_bitcast_fusion), kind=kLoop, calls=%fused_computation.5 | loop fusion | flops 65536 | bytes 524288 | tf_op jit(solution)/shard_map/concatenate | solution.py:287
  (22 shorter events, 0.3 us)
Async XLA Ops:
  0.1 3.4 %copy-start = (bf16[1,1024,4096]{2,1,0:T(8,128)(2,1)S(1)}, bf16[1,1024,4096]{2,1,0:T(8,128)(2,1)}, u32[]{:S(2)}) copy-start(bf16[1,1024,4096]{2,1,0:T(8,128)(2,1)} %param.7) | copy-start | bytes 25165828
  3.5 0.9 %copy-start.1 = (bf16[256,256]{1,0:T(8,128)(2,1)S(1)}, bf16[256,256]{1,0:T(8,128)(2,1)}, u32[]{:S(2)}) copy-start(bf16[256,256]{1,0:T(8,128)(2,1)} %constant.14.clone.table) | copy-start | bytes 393220
  4.4 0.7 %copy-start.2 = (s32[4096]{0:T(1024)S(1)}, s32[4096]{0:T(1024)}, u32[]{:S(2)}) copy-start(s32[4096]{0:T(1024)} %param.9) | copy-start | bytes 49156
  5.1 0.7 %copy-start.3 = (s32[4096]{0:T(1024)S(1)}, s32[4096]{0:T(1024)}, u32[]{:S(2)}) copy-start(s32[4096]{0:T(1024)} %param.10) | copy-start | bytes 49156
  5.8 0.7 %copy-start.4 = (s32[16]{0:T(128)S(1)}, s32[16]{0:T(128)}, u32[]{:S(2)}) copy-start(s32[16]{0:T(128)} %row_blocks.1) | copy-start | bytes 196
  6.5 0.7 %copy-start.5 = (s32[8]{0:T(128)S(1)}, s32[8]{0:T(128)}, u32[]{:S(2)}) copy-start(s32[8]{0:T(128)} %col_blocks.1) | copy-start | bytes 100
  21.8 3.7 %collective-permute-start = (f32[16,48,512]{2,1,0:T(8,128)S(1)}, f32[16,48,512]{2,1,0:T(8,128)S(1)}, u32[]{:S(2)}, u32[]{:S(2)}) collective-permute-start(f32[16,48,512]{2,1,0:T(8,128)S(1)} %get-tuple-element.16), channel_id=1, source_target_pairs={{0,1},{1,0},{2,3},{3,2},{4,5},{5,4},{6,7},{7,6},{8,9},{9,8},{10,11... | collective-permute-start | bytes 4718600 | tf_op jit(solution)/shard_map/ppermute | solution.py:268
  25.9 12.8 %collective-permute-start.1 = (f32[8,48,512]{2,1,0:T(8,128)S(1)}, f32[8,48,512]{2,1,0:T(8,128)S(1)}, u32[]{:S(2)}, u32[]{:S(2)}) collective-permute-start(f32[8,48,512]{2,1,0:T(8,128)S(1)} %slice.65), channel_id=1, source_target_pairs={{0,2},{1,5},{2,0},{3,7},{4,6},{5,1},{6,4},{7,3},{8,10},{9,13},{10,... | collective-permute-start | bytes 2359304 | tf_op jit(solution)/shard_map/ppermute | solution.py:197
  31.1 2.0 %collective-permute-start.4 = (f32[16,16,512]{2,1,0:T(8,128)S(1)}, f32[16,16,512]{2,1,0:T(8,128)S(1)}, u32[]{:S(2)}, u32[]{:S(2)}) collective-permute-start(f32[16,16,512]{2,1,0:T(8,128)S(1)} %get-tuple-element.18), channel_id=1, source_target_pairs={{0,1},{1,0},{2,3},{3,2},{4,5},{5,4},{6,7},{7,6},{8,9},{9,8},{10,11... | collective-permute-start | bytes 1572872 | tf_op jit(solution)/shard_map/ppermute | solution.py:274
  33.1 8.7 %collective-permute-start.5 = (f32[8,16,512]{2,1,0:T(8,128)S(1)}, f32[8,16,512]{2,1,0:T(8,128)S(1)}, u32[]{:S(2)}, u32[]{:S(2)}) collective-permute-start(f32[8,16,512]{2,1,0:T(8,128)S(1)} %slice.71), channel_id=1, source_target_pairs={{0,8},{1,9},{2,10},{3,11},{4,12},{5,13},{6,14},{7,15},{8,0},{9,1},... | collective-permute-start | bytes 786440 | tf_op jit(solution)/shard_map/ppermute | solution.py:197
  38.9 9.5 %collective-permute-start.2 = (f32[4,48,512]{2,1,0:T(8,128)S(1)}, f32[4,48,512]{2,1,0:T(8,128)S(1)}, u32[]{:S(2)}, u32[]{:S(2)}) collective-permute-start(f32[4,48,512]{2,1,0:T(8,128)S(1)} %slice.67), channel_id=1, source_target_pairs={{0,4},{1,9},{2,6},{3,11},{4,0},{5,13},{6,2},{7,15},{8,12},{9,1},{1... | collective-permute-start | bytes 1179656 | tf_op jit(solution)/shard_map/ppermute | solution.py:197
  41.9 5.0 %collective-permute-start.6 = (f32[4,16,512]{2,1,0:T(8,128)S(1)}, f32[4,16,512]{2,1,0:T(8,128)S(1)}, u32[]{:S(2)}, u32[]{:S(2)}) collective-permute-start(f32[4,16,512]{2,1,0:T(8,128)S(1)} %slice.73), channel_id=1, source_target_pairs={{0,2},{1,3},{2,0},{3,1},{4,6},{5,7},{6,4},{7,5},{8,10},{9,11},{10,... | collective-permute-start | bytes 393224 | tf_op jit(solution)/shard_map/ppermute | solution.py:197
  46.9 4.3 %collective-permute-start.7 = (f32[2,16,512]{2,1,0:T(8,128)S(1)}, f32[2,16,512]{2,1,0:T(8,128)S(1)}, u32[]{:S(2)}, u32[]{:S(2)}) collective-permute-start(f32[2,16,512]{2,1,0:T(8,128)S(1)} %slice.75), channel_id=1, source_target_pairs={{0,4},{1,5},{2,6},{3,7},{4,0},{5,1},{6,2},{7,3},{8,12},{9,13},{10,... | collective-permute-start | bytes 196616 | tf_op jit(solution)/shard_map/ppermute | solution.py:197
  48.4 5.7 %collective-permute-start.3 = (f32[2,48,512]{2,1,0:T(8,128)S(1)}, f32[2,48,512]{2,1,0:T(8,128)S(1)}, u32[]{:S(2)}, u32[]{:S(2)}) collective-permute-start(f32[2,48,512]{2,1,0:T(8,128)S(1)} %slice.69), channel_id=1, source_target_pairs={{0,8},{1,3},{2,10},{3,1},{4,12},{5,7},{6,14},{7,5},{8,0},{9,11},{1... | collective-permute-start | bytes 589832 | tf_op jit(solution)/shard_map/ppermute | solution.py:197
  54.2 7.3 %collective-permute-start.8 = (f32[1,64,512]{2,1,0:T(8,128)S(1)}, f32[1,64,512]{2,1,0:T(8,128)S(1)}, u32[]{:S(2)}, u32[]{:S(2)}) collective-permute-start(f32[1,64,512]{2,1,0:T(8,128)S(1)} %pad_maximum_fusion.1), channel_id=1, source_target_pairs={{0,16},{1,17},{2,18},{3,19},{4,20},{5,21},{6,22},{7,23},{8,24},{9,... | collective-permute-start | bytes 393224 | tf_op jit(solution)/shard_map/ppermute | solution.py:197

commit v2 on v1

--- a/solution.py
+++ b/solution.py
@@ -3,7 +3,6 @@
 
 import jax
 import jax.numpy as jnp
-import numpy as np
 from jax import lax
 from jax.experimental import pallas as pl
 from jax.experimental.pallas import tpu as pltpu
@@ -26,10 +25,9 @@
 
 
 def hadamard_table(order):
-    index = np.arange(order)
-    joined = index[:, None] & index[None, :]
-    parity = sum((joined >> position) & 1 for position in range(order.bit_length()))
-    return jnp.asarray(1 - 2 * (parity % 2), dtype=jnp.bfloat16)
+    first = lax.broadcasted_iota(jnp.int32, (order, order), 0)
+    second = lax.broadcasted_iota(jnp.int32, (order, order), 1)
+    return (1 - 2 * scalar_parity(first, second)).astype(jnp.float32).astype(jnp.bfloat16)
 
 
 def mix_group(parts):
@@ -79,13 +77,13 @@
 
 
 def mix_kernel(
-    plan, scale, here, row_blocks, col_blocks, grads, inputs, row_bits, col_bits, table,
+    plan, scale, here, row_blocks, col_blocks, grads, inputs, row_bits, col_bits,
     out, left_high, left_low, right_high, right_low, row_mixed, col_mixed,
 ):
     step = pl.program_id(0)
     tokens, row_local = grads.shape
     col_local = inputs.shape[1]
-    mixing = table[...]
+    mixing = hadamard_table(CHUNK)
     index = lax.broadcasted_iota(jnp.int32, (1, row_local), 1) + here[0] * row_local
     row_sign = jnp.where(index < FF, 1 - 2 * row_bits[...], 0).astype(jnp.float32).astype(jnp.bfloat16)
     col_sign = (1 - 2 * col_bits[...]).astype(jnp.float32).astype(jnp.bfloat16)
@@ -222,9 +220,8 @@
             smem,
             pl.BlockSpec((tile, row_local), lambda step: (step, 0)),
             pl.BlockSpec((tile, col_local), lambda step: (step, 0)),
-            vmem,
-            vmem,
-            vmem,
+            pl.BlockSpec((1, row_local), lambda step: (0, 0)),
+            pl.BlockSpec((1, col_local), lambda step: (0, 0)),
         ],
         out_specs=[vmem] * 5,
         out_shape=[
@@ -244,11 +241,8 @@
         here,
         row_blocks,
         col_blocks,
-        out_grads[0],
-        layer_inputs[0],
-        row_bits[None],
-        col_bits[None],
-        hadamard_table(CHUNK),
+        *(pltpu.with_memory_space_constraint(array, pltpu.HBM) for array in (out_grads[0], layer_inputs[0])),
+        *(pltpu.with_memory_space_constraint(bits[None], pltpu.HBM) for bits in (row_bits, col_bits)),
     )
 
     def products(wanted, shapes, name):

time: 64.6 us -> 59.5 us (0.921)
  local copies, waits for them, and re-layouts: 7.18 us -> 1.46 us
  Pallas kernels: 20.1 us -> 20.8 us
    unnamed x12 -> x4, local copies, waits for them, and re-layouts: 7.03 us -> 1.31 us
    pallas_call x1, Pallas kernels: 14.7 us -> 15.3 us  [body(): pl.pallas_call(functools.partial(mix_kernel, plan, scale), grid=(tokens /...]
where the time goes in v2:
time: 59.5 us; the launch traced here: 59.2 us
  Pallas kernels  20.8 us (35%)
  waiting for transfers between devices  19 us (32%)
  starting transfers between devices  14.3 us (24%)
  blocking collectives  1.99 us (3%)
  other arithmetic  1.55 us (3%)
  local copies, waits for them, and re-layouts  1.46 us (2%)
    ppermute x7, waiting for transfers between devices, halve(): lax.ppermute(part[half:], ('row', 'col', 'seq'), self.pairs(bits))  17.1 us
    pallas_call x1, Pallas kernels, body(): pl.pallas_call(functools.partial(mix_kernel, plan, scale), grid=(tokens /...  15.3 us
    ppermute x7, starting transfers between devices, halve(): lax.ppermute(part[half:], ('row', 'col', 'seq'), self.pairs(bits))  13.7 us
    pallas_call x2, Pallas kernels, products(): pl.pallas_call(functools.partial(product_kernel, plan, wanted), in_specs=...  5.49 us
    all_gather x1, blocking collectives, body(): both = in_rows(lax.all_gather(both, 'seq', axis=0))  1.99 us
    ppermute x1, waiting for transfers between devices, body(): rest = rest_mine + lax.ppermute(rest_other, 'seq', swap)  1.9 us
    unnamed x4, local copies, waits for them, and re-layouts  1.31 us
  transfers between devices with their start and end apart: 9, of which 7 were waited for; matrix products, arithmetic and copies ran while one was open for 1% of the time, Pallas kernels for 9%

profile of v2, /device:TPU:0, one launch (start us, length us, event | category | flops | bytes accessed | tf_op | source)
XLA Modules:
  0.0 59.2 jit_solution(9178588762266561056)
XLA Ops:
  0.0 0.1 pad_add_fusion.here
  0.1 0.0 copy-start
  0.1 0.7 %copy-done = s32[16]{0:T(128)S(1)} copy-done((s32[16]{0:T(128)S(1)}, s32[16]{0:T(128)}, u32[]{:S(2)}) %copy-start) | copy-done | bytes 88
  0.7 0.7 %copy-done.1 = s32[8]{0:T(128)S(1)} copy-done((s32[8]{0:T(128)S(1)}, s32[8]{0:T(128)}, u32[]{:S(2)}) %copy-start.1) | copy-done | bytes 56
  1.4 15.3 %mix.1 = (f32[16,48,512]{2,1,0:T(8,128)S(1)}, bf16[1024,1024]{1,0:T(8,128)(2,1)S(1)}, bf16[1024,1024]{1,0:T(8,128)(2,1)S(1)}, bf16[1024,1024]{1,0:T(8,128)(2,1)S(1)}, bf16[1024,1024]{1,0:T(8,128)(2,1)S(1)}) custom-call(s32[3]{0:T(128)S(1)} %pad_add_fusion.here, s32[16]{0:T(128)S(1)} %copy-done, s32[8]{0:T(128)S(1)} %copy-done.1, ...), custom_call_target="tpu_custom_call" | custom-call | tf_op jit(solution)/shard_map/mix/pallas_call | solution.py:214
  16.7 0.5 collective-permute-start
  17.3 3.1 %main_product.1 = f32[16,48,512]{2,1,0:T(8,128)S(1)} custom-call(s32[3]{0:T(128)S(1)} %pad_add_fusion.here, bf16[1024,1024]{1,0:T(8,128)(2,1)S(1)} %get-tuple-element.12.left_high, bf16[1024,1024]{1,0:T(8,128)(2,1)S(1)} %get-tuple-element.13.left_low, bf16[1024,1024]{1,0:T(8,128)(2,1)S(1)} %get-tuple-element.14.right_high, ...), custom_call_target="tpu_custom_call" | custom-call | tf_op jit(solution)/shard_map/main_product/pallas_call | solution.py:249
  20.4 0.0 collective-permute-done
  20.4 0.3 add.27
  20.8 0.1 slice.65
  20.8 2.8 %collective-permute-start.1 = (f32[8,48,512]{2,1,0:T(8,128)S(1)}, f32[8,48,512]{2,1,0:T(8,128)S(1)}, u32[]{:S(2)}, u32[]{:S(2)}) collective-permute-start(f32[8,48,512]{2,1,0:T(8,128)S(1)} %slice.65), channel_id=1, source_target_pairs={{0,2},{1,5},{2,0},{3,7},{4,6},{5,1},{6,4},{7,3},{8,10},{9,13},{10,... | collective-permute-start | bytes 2359304 | tf_op jit(solution)/shard_map/ppermute | solution.py:195
  23.6 2.4 %rest_products.1 = (f32[16,16,512]{2,1,0:T(8,128)S(1)}, f32[16,16,512]{2,1,0:T(8,128)S(1)}) custom-call(s32[3]{0:T(128)S(1)} %pad_add_fusion.here, bf16[1024,1024]{1,0:T(8,128)(2,1)S(1)} %get-tuple-element.12.left_high, bf16[1024,1024]{1,0:T(8,128)(2,1)S(1)} %get-tuple-element.13.left_low, bf16[1024,1024]{1,0:T(8,128)(2,1)S(1)} %get-tuple-element.14.right_high, ...), custom_call_target="tpu_custom_call" | custom-call | tf_op jit(solution)/shard_map/rest_products/pallas_call | solution.py:249
  26.0 0.1 collective-permute-start.4
  26.1 1.9 %collective-permute-done.4 = f32[16,16,512]{2,1,0:T(8,128)S(1)} collective-permute-done((f32[16,16,512]{2,1,0:T(8,128)S(1)}, f32[16,16,512]{2,1,0:T(8,128)S(1)}, u32[]{:S(2)}, u32[]{:S(2)}) %collective-permute-start.4) | collective-permute-done | bytes 524320 | tf_op jit(solution)/shard_map/ppermute | solution.py:268
  28.0 0.1 add.31
  28.1 1.6 %collective-permute-start.5 = (f32[8,16,512]{2,1,0:T(8,128)S(1)}, f32[8,16,512]{2,1,0:T(8,128)S(1)}, u32[]{:S(2)}, u32[]{:S(2)}) collective-permute-start(f32[8,16,512]{2,1,0:T(8,128)S(1)} %slice.71), channel_id=1, source_target_pairs={{0,8},{1,9},{2,10},{3,11},{4,12},{5,13},{6,14},{7,15},{8,0},{9,1},... | collective-permute-start | bytes 786440 | tf_op jit(solution)/shard_map/ppermute | solution.py:195
  29.7 3.9 %collective-permute-done.1 = f32[8,48,512]{2,1,0:T(8,128)S(1)} collective-permute-done((f32[8,48,512]{2,1,0:T(8,128)S(1)}, f32[8,48,512]{2,1,0:T(8,128)S(1)}, u32[]{:S(2)}, u32[]{:S(2)}) %collective-permute-start.1) | collective-permute-done | bytes 786464 | tf_op jit(solution)/shard_map/ppermute | solution.py:195
  33.6 0.1 slice_add_fusion
  33.8 2.1 %collective-permute-start.2 = (f32[4,48,512]{2,1,0:T(8,128)S(1)}, f32[4,48,512]{2,1,0:T(8,128)S(1)}, u32[]{:S(2)}, u32[]{:S(2)}) collective-permute-start(f32[4,48,512]{2,1,0:T(8,128)S(1)} %slice.67), channel_id=1, source_target_pairs={{0,4},{1,9},{2,6},{3,11},{4,0},{5,13},{6,2},{7,15},{8,12},{9,1},{1... | collective-permute-start | bytes 1179656 | tf_op jit(solution)/shard_map/ppermute | solution.py:195
  35.8 0.8 %collective-permute-done.5 = f32[8,16,512]{2,1,0:T(8,128)S(1)} collective-permute-done((f32[8,16,512]{2,1,0:T(8,128)S(1)}, f32[8,16,512]{2,1,0:T(8,128)S(1)}, u32[]{:S(2)}, u32[]{:S(2)}) %collective-permute-start.5) | collective-permute-done | bytes 262176 | tf_op jit(solution)/shard_map/ppermute | solution.py:195
  36.8 1.2 %collective-permute-start.6 = (f32[4,16,512]{2,1,0:T(8,128)S(1)}, f32[4,16,512]{2,1,0:T(8,128)S(1)}, u32[]{:S(2)}, u32[]{:S(2)}) collective-permute-start(f32[4,16,512]{2,1,0:T(8,128)S(1)} %slice.73), channel_id=1, source_target_pairs={{0,2},{1,3},{2,0},{3,1},{4,6},{5,7},{6,4},{7,5},{8,10},{9,11},{10,... | collective-permute-start | bytes 393224 | tf_op jit(solution)/shard_map/ppermute | solution.py:195
  38.0 3.8 %collective-permute-done.6 = f32[4,16,512]{2,1,0:T(8,128)S(1)} collective-permute-done((f32[4,16,512]{2,1,0:T(8,128)S(1)}, f32[4,16,512]{2,1,0:T(8,128)S(1)}, u32[]{:S(2)}, u32[]{:S(2)}) %collective-permute-start.6) | collective-permute-done | bytes 131104 | tf_op jit(solution)/shard_map/ppermute | solution.py:195
  41.8 1.4 %collective-permute-start.7 = (f32[2,16,512]{2,1,0:T(8,128)S(1)}, f32[2,16,512]{2,1,0:T(8,128)S(1)}, u32[]{:S(2)}, u32[]{:S(2)}) collective-permute-start(f32[2,16,512]{2,1,0:T(8,128)S(1)} %slice.75), channel_id=1, source_target_pairs={{0,4},{1,5},{2,6},{3,7},{4,0},{5,1},{6,2},{7,3},{8,12},{9,13},{10,... | collective-permute-start | bytes 196616 | tf_op jit(solution)/shard_map/ppermute | solution.py:195
  43.3 0.0 collective-permute-done.2
  43.3 0.1 slice_add_fusion.1
  43.3 1.6 %collective-permute-start.3 = (f32[2,48,512]{2,1,0:T(8,128)S(1)}, f32[2,48,512]{2,1,0:T(8,128)S(1)}, u32[]{:S(2)}, u32[]{:S(2)}) collective-permute-start(f32[2,48,512]{2,1,0:T(8,128)S(1)} %slice.69), channel_id=1, source_target_pairs={{0,8},{1,3},{2,10},{3,1},{4,12},{5,7},{6,14},{7,5},{8,0},{9,11},{1... | collective-permute-start | bytes 589832 | tf_op jit(solution)/shard_map/ppermute | solution.py:195
  45.0 1.2 %collective-permute-done.7 = f32[2,16,512]{2,1,0:T(8,128)S(1)} collective-permute-done((f32[2,16,512]{2,1,0:T(8,128)S(1)}, f32[2,16,512]{2,1,0:T(8,128)S(1)}, u32[]{:S(2)}, u32[]{:S(2)}) %collective-permute-start.7) | collective-permute-done | bytes 65568 | tf_op jit(solution)/shard_map/ppermute | solution.py:195
  46.2 2.9 %collective-permute-done.3 = f32[2,48,512]{2,1,0:T(8,128)S(1)} collective-permute-done((f32[2,48,512]{2,1,0:T(8,128)S(1)}, f32[2,48,512]{2,1,0:T(8,128)S(1)}, u32[]{:S(2)}, u32[]{:S(2)}) %collective-permute-start.3) | collective-permute-done | bytes 196640 | tf_op jit(solution)/shard_map/ppermute | solution.py:195
  49.1 2.9 %collective-permute-start.8 = (f32[1,64,512]{2,1,0:T(8,128)S(1)}, f32[1,64,512]{2,1,0:T(8,128)S(1)}, u32[]{:S(2)}, u32[]{:S(2)}) collective-permute-start(f32[1,64,512]{2,1,0:T(8,128)S(1)} %pad_maximum_fusion.1), channel_id=1, source_target_pairs={{0,16},{1,17},{2,18},{3,19},{4,20},{5,21},{6,22},{7,23},{8,24},{9,... | collective-permute-start | bytes 393224 | tf_op jit(solution)/shard_map/ppermute | solution.py:195
  52.0 4.4 %collective-permute-done.8 = f32[1,64,512]{2,1,0:T(8,128)S(1)} collective-permute-done((f32[1,64,512]{2,1,0:T(8,128)S(1)}, f32[1,64,512]{2,1,0:T(8,128)S(1)}, u32[]{:S(2)}, u32[]{:S(2)}) %collective-permute-start.8) | collective-permute-done | bytes 131104 | tf_op jit(solution)/shard_map/ppermute | solution.py:195
  56.5 2.0 %all_gather.3 = f32[2,64,512]{2,1,0:T(8,128)S(1)} all-gather(f32[1,64,512]{2,1,0:T(8,128)S(1)} %fusion.1), channel_id=1, replica_groups=mesh['row'=8,'col'=2,'seq'=2] {'seq'}, dimensions={0}, use_global_device_ids=true | all-gather | bytes 393216 | tf_op jit(solution)/shard_map/all_gather | solution.py:284
  58.5 0.7 %pad_maximum_fusion = f32[2,1,64,512]{3,2,0,1:T(8,128)} fusion(f32[2,1,16,512]{3,2,0,1:T(8,128)S(1)} %slice_bitcast_fusion.1, f32[2,1,48,512]{3,2,0,1:T(8,128)S(1)} %slice_bitcast_fusion), kind=kLoop, calls=%fused_computation.5 | loop fusion | flops 65536 | bytes 524288 | tf_op jit(solution)/shard_map/concatenate | solution.py:281
  (14 shorter events, 0.2 us)
Async XLA Ops:
  0.1 0.7 %copy-start = (s32[16]{0:T(128)S(1)}, s32[16]{0:T(128)}, u32[]{:S(2)}) copy-start(s32[16]{0:T(128)} %row_blocks.1) | copy-start | bytes 196
  0.7 0.7 %copy-start.1 = (s32[8]{0:T(128)S(1)}, s32[8]{0:T(128)}, u32[]{:S(2)}) copy-start(s32[8]{0:T(128)} %col_blocks.1) | copy-start | bytes 100
  16.7 3.7 %collective-permute-start = (f32[16,48,512]{2,1,0:T(8,128)S(1)}, f32[16,48,512]{2,1,0:T(8,128)S(1)}, u32[]{:S(2)}, u32[]{:S(2)}) collective-permute-start(f32[16,48,512]{2,1,0:T(8,128)S(1)} %get-tuple-element.16), channel_id=1, source_target_pairs={{0,1},{1,0},{2,3},{3,2},{4,5},{5,4},{6,7},{7,6},{8,9},{9,8},{10,11... | collective-permute-start | bytes 4718600 | tf_op jit(solution)/shard_map/ppermute | solution.py:262
  20.8 12.8 %collective-permute-start.1 = (f32[8,48,512]{2,1,0:T(8,128)S(1)}, f32[8,48,512]{2,1,0:T(8,128)S(1)}, u32[]{:S(2)}, u32[]{:S(2)}) collective-permute-start(f32[8,48,512]{2,1,0:T(8,128)S(1)} %slice.65), channel_id=1, source_target_pairs={{0,2},{1,5},{2,0},{3,7},{4,6},{5,1},{6,4},{7,3},{8,10},{9,13},{10,... | collective-permute-start | bytes 2359304 | tf_op jit(solution)/shard_map/ppermute | solution.py:195
  26.0 2.0 %collective-permute-start.4 = (f32[16,16,512]{2,1,0:T(8,128)S(1)}, f32[16,16,512]{2,1,0:T(8,128)S(1)}, u32[]{:S(2)}, u32[]{:S(2)}) collective-permute-start(f32[16,16,512]{2,1,0:T(8,128)S(1)} %get-tuple-element.18), channel_id=1, source_target_pairs={{0,1},{1,0},{2,3},{3,2},{4,5},{5,4},{6,7},{7,6},{8,9},{9,8},{10,11... | collective-permute-start | bytes 1572872 | tf_op jit(solution)/shard_map/ppermute | solution.py:268
  28.1 8.6 %collective-permute-start.5 = (f32[8,16,512]{2,1,0:T(8,128)S(1)}, f32[8,16,512]{2,1,0:T(8,128)S(1)}, u32[]{:S(2)}, u32[]{:S(2)}) collective-permute-start(f32[8,16,512]{2,1,0:T(8,128)S(1)} %slice.71), channel_id=1, source_target_pairs={{0,8},{1,9},{2,10},{3,11},{4,12},{5,13},{6,14},{7,15},{8,0},{9,1},... | collective-permute-start | bytes 786440 | tf_op jit(solution)/shard_map/ppermute | solution.py:195
  33.8 9.5 %collective-permute-start.2 = (f32[4,48,512]{2,1,0:T(8,128)S(1)}, f32[4,48,512]{2,1,0:T(8,128)S(1)}, u32[]{:S(2)}, u32[]{:S(2)}) collective-permute-start(f32[4,48,512]{2,1,0:T(8,128)S(1)} %slice.67), channel_id=1, source_target_pairs={{0,4},{1,9},{2,6},{3,11},{4,0},{5,13},{6,2},{7,15},{8,12},{9,1},{1... | collective-permute-start | bytes 1179656 | tf_op jit(solution)/shard_map/ppermute | solution.py:195
  36.8 5.0 %collective-permute-start.6 = (f32[4,16,512]{2,1,0:T(8,128)S(1)}, f32[4,16,512]{2,1,0:T(8,128)S(1)}, u32[]{:S(2)}, u32[]{:S(2)}) collective-permute-start(f32[4,16,512]{2,1,0:T(8,128)S(1)} %slice.73), channel_id=1, source_target_pairs={{0,2},{1,3},{2,0},{3,1},{4,6},{5,7},{6,4},{7,5},{8,10},{9,11},{10,... | collective-permute-start | bytes 393224 | tf_op jit(solution)/shard_map/ppermute | solution.py:195
  41.8 4.3 %collective-permute-start.7 = (f32[2,16,512]{2,1,0:T(8,128)S(1)}, f32[2,16,512]{2,1,0:T(8,128)S(1)}, u32[]{:S(2)}, u32[]{:S(2)}) collective-permute-start(f32[2,16,512]{2,1,0:T(8,128)S(1)} %slice.75), channel_id=1, source_target_pairs={{0,4},{1,5},{2,6},{3,7},{4,0},{5,1},{6,2},{7,3},{8,12},{9,13},{10,... | collective-permute-start | bytes 196616 | tf_op jit(solution)/shard_map/ppermute | solution.py:195
  43.3 5.7 %collective-permute-start.3 = (f32[2,48,512]{2,1,0:T(8,128)S(1)}, f32[2,48,512]{2,1,0:T(8,128)S(1)}, u32[]{:S(2)}, u32[]{:S(2)}) collective-permute-start(f32[2,48,512]{2,1,0:T(8,128)S(1)} %slice.69), channel_id=1, source_target_pairs={{0,8},{1,3},{2,10},{3,1},{4,12},{5,7},{6,14},{7,5},{8,0},{9,11},{1... | collective-permute-start | bytes 589832 | tf_op jit(solution)/shard_map/ppermute | solution.py:195
  49.1 7.3 %collective-permute-start.8 = (f32[1,64,512]{2,1,0:T(8,128)S(1)}, f32[1,64,512]{2,1,0:T(8,128)S(1)}, u32[]{:S(2)}, u32[]{:S(2)}) collective-permute-start(f32[1,64,512]{2,1,0:T(8,128)S(1)} %pad_maximum_fusion.1), channel_id=1, source_target_pairs={{0,16},{1,17},{2,18},{3,19},{4,20},{5,21},{6,22},{7,23},{8,24},{9,... | collective-permute-start | bytes 393224 | tf_op jit(solution)/shard_map/ppermute | solution.py:195

commit v3 on v2

--- a/solution.py
+++ b/solution.py
@@ -59,21 +59,35 @@
     low_ref[where] = (values - high.astype(jnp.float32)).astype(jnp.bfloat16)
 
 
-def product_blocks(plan, here, left_high, left_low, right_high, right_low, out_ref, first_row, orders):
-    rows, width = out_ref.shape[1], out_ref.shape[2]
+def product_blocks(plan, here, factors, out_ref, first_row, orders, begin):
+    left_high, left_low, right_high, right_low = factors
+    count, rows, width = out_ref.shape
     tile = min(CHUNK, width)
-    span = pl.ds(first_row, plan.rows * rows)
-    seq = here[2] % 2
-    for start in range(0, plan.cols * width, tile):
-        lanes = pl.ds(start, tile)
-        total = jnp.dot(left_high[span, :], right_high[:, lanes], preferred_element_type=jnp.float32)
-        total += jnp.dot(left_high[span, :], right_low[:, lanes], preferred_element_type=jnp.float32)
-        total += jnp.dot(left_low[span, :], right_high[:, lanes], preferred_element_type=jnp.float32)
-        col = start // width
-        for row in range(plan.rows):
-            places = [plan.place(order, row, col) for order in orders]
-            place = jnp.where(seq == 0, places[0], places[1]) if places[0] != places[1] else places[0]
-            out_ref[place, :, pl.ds(start % width, tile)] = total[row * rows : (row + 1) * rows, :]
+
+    def run(order):
+        for start in range(0, plan.cols * width, tile):
+            col = start // width
+            places = [plan.place(order, row, col) - begin for row in plan.row_sequence]
+            wanted = [spot for spot, place in enumerate(places) if 0 <= place < count]
+            while wanted:
+                length = 1
+                while length < len(wanted) and wanted[length] == wanted[0] + length:
+                    length += 1
+                span = pl.ds(first_row + wanted[0] * rows, length * rows)
+                lanes = pl.ds(start, tile)
+                total = jnp.dot(left_high[span, :], right_high[:, lanes], preferred_element_type=jnp.float32)
+                total += jnp.dot(left_high[span, :], right_low[:, lanes], preferred_element_type=jnp.float32)
+                total += jnp.dot(left_low[span, :], right_high[:, lanes], preferred_element_type=jnp.float32)
+                for at in range(length):
+                    piece = total[at * rows : (at + 1) * rows, :]
+                    out_ref[places[wanted[at]], :, pl.ds(start % width, tile)] = piece
+                wanted = wanted[length:]
+
+    if orders[0] == orders[1]:
+        run(orders[0])
+    else:
+        for seq, order in enumerate(orders):
+            pl.when(here[2] % 2 == seq)(functools.partial(run, order))
 
 
 def mix_kernel(
@@ -113,7 +127,7 @@
     cut = BR * 3 // 4
     for part in range(plan.split):
         base = part * plan.rows * inner * BR
-        for row in range(plan.rows):
+        for order, row in enumerate(plan.row_sequence):
             for at in range(inner):
                 kept = (here[0] ^ row) * plan.per_row + at * plan.split
                 if plan.split == 2:
@@ -121,7 +135,7 @@
                 block = row_blocks[kept]
                 sign = (1 - 2 * scalar_parity(block // row_slots, here[0])).astype(jnp.float32) * scale
                 values = kept_sum(row_mixed, block % row_slots, sign, BR, tokens, 0)
-                spot = row * inner + at
+                spot = order * inner + at
                 first = base + spot * cut
                 store_pieces(values[:cut], left_high, left_low, (pl.ds(first, cut), now))
                 first = base + plan.rows * inner * cut + spot * (BR - cut)
@@ -136,13 +150,14 @@
 
     @pl.when(step == pl.num_programs(0) - 1)
     def _():
-        first, orders = plan.first_product()
-        product_blocks(plan, here, left_high, left_low, right_high, right_low, out, first, orders)
+        factors = (left_high, left_low, right_high, right_low)
+        product_blocks(plan, here, factors, out, *plan.first_product())
 
 
 def product_kernel(plan, wanted, here, left_high, left_low, right_high, right_low, *outs):
-    for (first, orders), out in zip(wanted, outs):
-        product_blocks(plan, here, left_high, left_low, right_high, right_low, out, first, orders)
+    factors = (left_high, left_low, right_high, right_low)
+    for args, out in zip(wanted, outs):
+        product_blocks(plan, here, factors, out, *args)
 
 
 class Plan:
@@ -151,6 +166,10 @@
         self.split = self.seqs if self.seqs == 2 and (row_kept // self.rows) % 2 == 0 else 1
         self.per_row = row_kept // self.rows
         self.per_col = col_kept // self.cols
+        low_first = range(self.rows.bit_length() - 2, -1, -1)
+        self.row_sequence = [
+            sum(((spot >> (self.rows.bit_length() - 2 - bit)) & 1) << bit for bit in low_first) for spot in range(self.rows)
+        ]
         row_bits = [("row", 1 << bit) for bit in range(self.rows.bit_length() - 1)]
         col_bits = [("col", 1 << bit) for bit in range(self.cols.bit_length() - 1)]
         last = row_bits[-1:]
@@ -185,14 +204,18 @@
         return spot
 
     def first_product(self):
+        half = self.rows * self.cols // 2
         if self.split == 1:
-            return 0, self.main
-        return self.rows * self.per_row // 2 * BR, self.main[1:] + self.main[:1]
+            return 0, self.main, half
+        return self.rows * self.per_row // 2 * BR, self.main[1:] + self.main[:1], half
+
+    def cross(self, part, orders, step):
+        bits = (orders[0][step], orders[1][step])
+        return lax.ppermute(part, ("row", "col", "seq"), self.pairs(bits))
 
     def halve(self, part, orders, step):
         half = part.shape[0] // 2
-        bits = (orders[0][step], orders[1][step])
-        return part[:half] + lax.ppermute(part[half:], ("row", "col", "seq"), self.pairs(bits))
+        return part[:half] + self.cross(part[half:], orders, step)
 
 
 def body(plan, out_grads, layer_inputs, row_bits, col_bits, row_blocks, col_blocks):
@@ -209,7 +232,7 @@
     blocks = plan.rows * plan.cols
     smem = pl.BlockSpec(memory_space=pltpu.SMEM)
     vmem = pl.BlockSpec(memory_space=pltpu.VMEM)
-    main_shape = jax.ShapeDtypeStruct((blocks, inner * cut, cols_each), jnp.float32)
+    main_shape = jax.ShapeDtypeStruct((blocks // 2, inner * cut, cols_each), jnp.float32)
     rest_shape = jax.ShapeDtypeStruct((blocks, inner * (BR - cut), cols_each), jnp.float32)
     first_out, *factors = pl.pallas_call(
         functools.partial(mix_kernel, plan, scale),
@@ -255,34 +278,45 @@
             name=name,
         )(here, *factors)
 
-    swap = [(0, 1), (1, 0)]
+    half = blocks // 2
     half_rows = plan.rows * inner * BR
     main_rows = plan.rows * inner * cut
+
+    def swap(values):
+        return lax.ppermute(values, "seq", [(0, 1), (1, 0)])
+
     if plan.split == 2:
-        arrived = lax.ppermute(first_out, "seq", swap)
-        (mine,) = products([(0, plan.main)], [main_shape], "main_product")
-        rest_mine, rest_other = products(
-            [(main_rows, plan.rest), (half_rows + main_rows, plan.rest)], [rest_shape] * 2, "rest_products"
+        (sent,) = products([(0, plan.main, half)], [main_shape], "sent_product")
+        sent = sent + swap(first_out)
+        rest, rest_other = products(
+            [(main_rows, plan.rest, 0), (half_rows + main_rows, plan.rest, 0)], [rest_shape] * 2, "rest_products"
         )
-        main = mine + arrived
-        rest = rest_mine + lax.ppermute(rest_other, "seq", swap)
+        rest = rest + swap(rest_other)
+        (kept_other,) = products([(half_rows, plan.main[1:] + plan.main[:1], 0)], [main_shape], "kept_other_product")
+        (kept,) = products([(0, plan.main, 0)], [main_shape], "kept_product")
+        kept = kept + swap(kept_other)
     else:
-        main = first_out
-        (rest,) = products([(main_rows, plan.rest)], [rest_shape], "rest_product")
+        sent = first_out
+        (rest,) = products([(main_rows, plan.rest, 0)], [rest_shape], "rest_product")
+        (kept,) = products([(0, plan.main, 0)], [main_shape], "kept_product")
     steps = len(plan.main[0])
-    for step in range(steps - 1):
+    main = kept + plan.cross(sent, plan.main, 0)
+    rest = plan.halve(rest, plan.rest, 0)
+    for step in range(1, steps - 1):
         main = plan.halve(main, plan.main, step)
         rest = plan.halve(rest, plan.rest, step)
     both = plan.halve(jnp.concatenate([main, rest], axis=1), plan.rest, steps - 1)[0]
 
     def in_rows(values):
-        first = values[..., : inner * cut, :].reshape(*values.shape[:-2], inner, cut, cols_each)
-        second = values[..., inner * cut :, :].reshape(*values.shape[:-2], inner, BR - cut, cols_each)
-        return jnp.concatenate([first, second], axis=-2)
+        first = values[: inner * cut].reshape(inner, cut, cols_each)
+        second = values[inner * cut :].reshape(inner, BR - cut, cols_each)
+        return jnp.concatenate([first, second], axis=1)
 
     if plan.split == 2:
-        both = in_rows(lax.all_gather(both, "seq", axis=0))
-        return both.transpose(1, 0, 2, 3).reshape(1, plan.per_row * BR, cols_each)
+        mine, other = in_rows(both), in_rows(swap(both))
+        first = lax.axis_index("seq") == 0
+        pair = jnp.stack([jnp.where(first, mine, other), jnp.where(first, other, mine)], axis=1)
+        return pair.reshape(1, plan.per_row * BR, cols_each)
     return in_rows(lax.psum(both, "seq")).reshape(1, plan.per_row * BR, cols_each)
 
 

time: 59.5 us -> 59.3 us (level)
  blocking collectives: 1.99 us -> 0 us
  Pallas kernels: 20.8 us -> 22.3 us
  waiting for transfers between devices: 19 us -> 19.6 us
    pallas_call x2 -> x4, Pallas kernels: 5.49 us -> 8.19 us  [products(): pl.pallas_call(functools.partial(product_kernel, plan, wanted), in_specs=...]
    all_gather x1 -> x0, blocking collectives: 1.99 us -> none  [body(): both = in_rows(lax.all_gather(both, 'seq', axis=0))]
    pallas_call x1, Pallas kernels: 15.3 us -> 14.2 us  [body(): pl.pallas_call(functools.partial(mix_kernel, plan, scale), grid=(tokens /...]
    another operation x0 -> x1, other arithmetic: none -> 0.72 us  [body(): jnp.stack([jnp.where(first, mine, other), jnp.where(first, other, mine)],...]
    concatenate x1 -> x0, other arithmetic: 0.72 us -> none  [in_rows(): return jnp.concatenate([first, second], axis=-2)]
    ppermute x9 -> x11, waiting for transfers between devices: 19 us -> 19.6 us  [the longest x7 18.2 us: cross(): return lax.ppermute(part, ('row', 'col', 'seq'), self.pairs(bits))]
    ppermute x9 -> x11, starting transfers between devices: 14.3 us -> 14.1 us  [the longest x7 13.3 us: cross(): return lax.ppermute(part, ('row', 'col', 'seq'), self.pairs(bits))]
  transfers between devices with their start and end apart: 9 -> 11, of which waited for: 7 -> 7; matrix products, arithmetic and copies ran while one was open for 1% -> 1% of each run, Pallas kernels for 9% -> 14%
where the time goes in v3:
time: 59.3 us; the launch traced here: 59.1 us
  Pallas kernels  22.3 us (38%)
  waiting for transfers between devices  19.6 us (33%)
  starting transfers between devices  14.1 us (24%)
  other arithmetic  1.48 us (2%)
  local copies, waits for them, and re-layouts  1.41 us (2%)
    ppermute x7, waiting for transfers between devices, cross(): return lax.ppermute(part, ('row', 'col', 'seq'), self.pairs(bits))  18.2 us
    pallas_call x1, Pallas kernels, body(): pl.pallas_call(functools.partial(mix_kernel, plan, scale), grid=(tokens /...  14.2 us
    ppermute x7, starting transfers between devices, cross(): return lax.ppermute(part, ('row', 'col', 'seq'), self.pairs(bits))  13.3 us
    pallas_call x4, Pallas kernels, products(): pl.pallas_call(functools.partial(product_kernel, plan, wanted), in_specs=...  8.19 us
    ppermute x4, waiting for transfers between devices, swap(): return lax.ppermute(values, 'seq', [(0, 1), (1, 0)])  1.33 us
    unnamed x4, local copies, waits for them, and re-layouts  1.31 us
  transfers between devices with their start and end apart: 11, of which 7 were waited for; matrix products, arithmetic and copies ran while one was open for 1% of the time, Pallas kernels for 14%

profile of v3, /device:TPU:0, one launch (start us, length us, event | category | flops | bytes accessed | tf_op | source)
XLA Modules:
  0.0 59.1 jit_solution(12283543540710661591)
XLA Ops:
  0.0 0.1 pad_add_fusion.here
  0.1 0.7 %copy-done = s32[16]{0:T(128)S(1)} copy-done((s32[16]{0:T(128)S(1)}, s32[16]{0:T(128)}, u32[]{:S(2)}) %copy-start) | copy-done | bytes 88
  0.7 0.7 %copy-done.1 = s32[8]{0:T(128)S(1)} copy-done((s32[8]{0:T(128)S(1)}, s32[8]{0:T(128)}, u32[]{:S(2)}) %copy-start.1) | copy-done | bytes 56
  1.4 14.2 %mix.1 = (f32[8,48,512]{2,1,0:T(8,128)S(1)}, bf16[1024,1024]{1,0:T(8,128)(2,1)S(1)}, bf16[1024,1024]{1,0:T(8,128)(2,1)S(1)}, bf16[1024,1024]{1,0:T(8,128)(2,1)S(1)}, bf16[1024,1024]{1,0:T(8,128)(2,1)S(1)}) custom-call(s32[3]{0:T(128)S(1)} %pad_add_fusion.here, s32[16]{0:T(128)S(1)} %copy-done, s32[8]{0:T(128)S(1)} %copy-done.1, bf16[1024,4096]{1,0:T(8,128)(2,1)} %bitcast.17, ...), custom_call_target="tpu_custom_call" | custom-call | tf_op jit(solution)/shard_map/mix/pallas_call | solution.py:237
  15.6 0.5 collective-permute-start.1
  16.0 2.0 %kept_other_product.1 = f32[8,48,512]{2,1,0:T(8,128)S(1)} custom-call(s32[3]{0:T(128)S(1)} %pad_add_fusion.here, bf16[1024,1024]{1,0:T(8,128)(2,1)S(1)} %get-tuple-element.12.left_high, bf16[1024,1024]{1,0:T(8,128)(2,1)S(1)} %get-tuple-element.13.left_low, bf16[1024,1024]{1,0:T(8,128)(2,1)S(1)} %get-tuple-element.14.right_high, ...), custom_call_target="tpu_custom_call" | custom-call | tf_op jit(solution)/shard_map/kept_other_product/pallas_call | solution.py:272
  18.0 0.1 collective-permute-start
  18.1 1.9 %sent_product.1 = f32[8,48,512]{2,1,0:T(8,128)S(1)} custom-call(s32[3]{0:T(128)S(1)} %pad_add_fusion.here, bf16[1024,1024]{1,0:T(8,128)(2,1)S(1)} %get-tuple-element.12.left_high, bf16[1024,1024]{1,0:T(8,128)(2,1)S(1)} %get-tuple-element.13.left_low, bf16[1024,1024]{1,0:T(8,128)(2,1)S(1)} %get-tuple-element.14.right_high, ...), custom_call_target="tpu_custom_call" | custom-call | tf_op jit(solution)/shard_map/sent_product/pallas_call | solution.py:272
  20.1 0.0 collective-permute-done.1
  20.1 0.1 add.31
  20.2 3.0 %collective-permute-start.2 = (f32[8,48,512]{2,1,0:T(8,128)S(1)}, f32[8,48,512]{2,1,0:T(8,128)S(1)}, u32[]{:S(2)}, u32[]{:S(2)}) collective-permute-start(f32[8,48,512]{2,1,0:T(8,128)S(1)} %add.31), channel_id=1, source_target_pairs={{0,2},{1,5},{2,0},{3,7},{4,6},{5,1},{6,4},{7,3},{8,10},{9,13},{10,... | collective-permute-start | bytes 2359304 | tf_op jit(solution)/shard_map/ppermute | solution.py:214
  23.3 2.3 %rest_products.1 = (f32[16,16,512]{2,1,0:T(8,128)S(1)}, f32[16,16,512]{2,1,0:T(8,128)S(1)}) custom-call(s32[3]{0:T(128)S(1)} %pad_add_fusion.here, bf16[1024,1024]{1,0:T(8,128)(2,1)S(1)} %get-tuple-element.12.left_high, bf16[1024,1024]{1,0:T(8,128)(2,1)S(1)} %get-tuple-element.13.left_low, bf16[1024,1024]{1,0:T(8,128)(2,1)S(1)} %get-tuple-element.14.right_high, ...), custom_call_target="tpu_custom_call" | custom-call | tf_op jit(solution)/shard_map/rest_products/pallas_call | solution.py:272
  25.6 0.1 collective-permute-start.5
  25.7 1.9 %kept_product.1 = f32[8,48,512]{2,1,0:T(8,128)S(1)} custom-call(s32[3]{0:T(128)S(1)} %pad_add_fusion.here, bf16[1024,1024]{1,0:T(8,128)(2,1)S(1)} %get-tuple-element.12.left_high, bf16[1024,1024]{1,0:T(8,128)(2,1)S(1)} %get-tuple-element.13.left_low, bf16[1024,1024]{1,0:T(8,128)(2,1)S(1)} %get-tuple-element.14.right_high, ...), custom_call_target="tpu_custom_call" | custom-call | tf_op jit(solution)/shard_map/kept_product/pallas_call | solution.py:272
  27.7 0.1 add.35
  27.8 1.6 %collective-permute-start.6 = (f32[8,16,512]{2,1,0:T(8,128)S(1)}, f32[8,16,512]{2,1,0:T(8,128)S(1)}, u32[]{:S(2)}, u32[]{:S(2)}) collective-permute-start(f32[8,16,512]{2,1,0:T(8,128)S(1)} %slice.71), channel_id=1, source_target_pairs={{0,8},{1,9},{2,10},{3,11},{4,12},{5,13},{6,14},{7,15},{8,0},{9,1},... | collective-permute-start | bytes 786440 | tf_op jit(solution)/shard_map/ppermute | solution.py:214
  29.4 3.8 %collective-permute-done.2 = f32[8,48,512]{2,1,0:T(8,128)S(1)} collective-permute-done((f32[8,48,512]{2,1,0:T(8,128)S(1)}, f32[8,48,512]{2,1,0:T(8,128)S(1)}, u32[]{:S(2)}, u32[]{:S(2)}) %collective-permute-start.2) | collective-permute-done | bytes 786464 | tf_op jit(solution)/shard_map/ppermute | solution.py:214
  33.2 0.2 add_add_fusion
  33.5 2.1 %collective-permute-start.3 = (f32[4,48,512]{2,1,0:T(8,128)S(1)}, f32[4,48,512]{2,1,0:T(8,128)S(1)}, u32[]{:S(2)}, u32[]{:S(2)}) collective-permute-start(f32[4,48,512]{2,1,0:T(8,128)S(1)} %slice.67), channel_id=1, source_target_pairs={{0,4},{1,9},{2,6},{3,11},{4,0},{5,13},{6,2},{7,15},{8,12},{9,1},{1... | collective-permute-start | bytes 1179656 | tf_op jit(solution)/shard_map/ppermute | solution.py:214
  35.6 1.4 %collective-permute-done.6 = f32[8,16,512]{2,1,0:T(8,128)S(1)} collective-permute-done((f32[8,16,512]{2,1,0:T(8,128)S(1)}, f32[8,16,512]{2,1,0:T(8,128)S(1)}, u32[]{:S(2)}, u32[]{:S(2)}) %collective-permute-start.6) | collective-permute-done | bytes 262176 | tf_op jit(solution)/shard_map/ppermute | solution.py:214
  37.0 0.5 collective-permute-start.7
  37.5 4.6 %collective-permute-done.7 = f32[4,16,512]{2,1,0:T(8,128)S(1)} collective-permute-done((f32[4,16,512]{2,1,0:T(8,128)S(1)}, f32[4,16,512]{2,1,0:T(8,128)S(1)}, u32[]{:S(2)}, u32[]{:S(2)}) %collective-permute-start.7) | collective-permute-done | bytes 131104 | tf_op jit(solution)/shard_map/ppermute | solution.py:214
  42.1 1.6 %collective-permute-start.8 = (f32[2,16,512]{2,1,0:T(8,128)S(1)}, f32[2,16,512]{2,1,0:T(8,128)S(1)}, u32[]{:S(2)}, u32[]{:S(2)}) collective-permute-start(f32[2,16,512]{2,1,0:T(8,128)S(1)} %slice.75), channel_id=1, source_target_pairs={{0,4},{1,5},{2,6},{3,7},{4,0},{5,1},{6,2},{7,3},{8,12},{9,13},{10,... | collective-permute-start | bytes 196616 | tf_op jit(solution)/shard_map/ppermute | solution.py:214
  43.7 0.1 slice_add_fusion
  43.7 1.6 %collective-permute-start.4 = (f32[2,48,512]{2,1,0:T(8,128)S(1)}, f32[2,48,512]{2,1,0:T(8,128)S(1)}, u32[]{:S(2)}, u32[]{:S(2)}) collective-permute-start(f32[2,48,512]{2,1,0:T(8,128)S(1)} %slice.69), channel_id=1, source_target_pairs={{0,8},{1,3},{2,10},{3,1},{4,12},{5,7},{6,14},{7,5},{8,0},{9,11},{1... | collective-permute-start | bytes 589832 | tf_op jit(solution)/shard_map/ppermute | solution.py:214
  45.4 1.0 %collective-permute-done.8 = f32[2,16,512]{2,1,0:T(8,128)S(1)} collective-permute-done((f32[2,16,512]{2,1,0:T(8,128)S(1)}, f32[2,16,512]{2,1,0:T(8,128)S(1)}, u32[]{:S(2)}, u32[]{:S(2)}) %collective-permute-start.8) | collective-permute-done | bytes 65568 | tf_op jit(solution)/shard_map/ppermute | solution.py:214
  46.4 3.0 %collective-permute-done.4 = f32[2,48,512]{2,1,0:T(8,128)S(1)} collective-permute-done((f32[2,48,512]{2,1,0:T(8,128)S(1)}, f32[2,48,512]{2,1,0:T(8,128)S(1)}, u32[]{:S(2)}, u32[]{:S(2)}) %collective-permute-start.4) | collective-permute-done | bytes 196640 | tf_op jit(solution)/shard_map/ppermute | solution.py:214
  49.5 2.9 %collective-permute-start.9 = (f32[1,64,512]{2,1,0:T(8,128)S(1)}, f32[1,64,512]{2,1,0:T(8,128)S(1)}, u32[]{:S(2)}, u32[]{:S(2)}) collective-permute-start(f32[1,64,512]{2,1,0:T(8,128)S(1)} %pad_maximum_fusion.1), channel_id=1, source_target_pairs={{0,16},{1,17},{2,18},{3,19},{4,20},{5,21},{6,22},{7,23},{8,24},{9,... | collective-permute-start | bytes 393224 | tf_op jit(solution)/shard_map/ppermute | solution.py:214
  52.4 4.4 %collective-permute-done.9 = f32[1,64,512]{2,1,0:T(8,128)S(1)} collective-permute-done((f32[1,64,512]{2,1,0:T(8,128)S(1)}, f32[1,64,512]{2,1,0:T(8,128)S(1)}, u32[]{:S(2)}, u32[]{:S(2)}) %collective-permute-start.9) | collective-permute-done | bytes 131104 | tf_op jit(solution)/shard_map/ppermute | solution.py:214
  56.9 0.1 collective-permute-start.10
  57.0 1.3 %collective-permute-done.10 = f32[64,512]{1,0:T(8,128)S(1)} collective-permute-done((f32[64,512]{1,0:T(8,128)S(1)}, f32[64,512]{1,0:T(8,128)S(1)}, u32[]{:S(2)}, u32[]{:S(2)}) %collective-permute-start.10) | collective-permute-done | bytes 131104 | tf_op jit(solution)/shard_map/ppermute | solution.py:286
  58.4 0.7 %pad_maximum_fusion = f32[1,2,64,512]{3,2,1,0:T(8,128)} fusion(f32[1,1,64,512]{3,2,1,0:T(8,128)S(1)} %get-tuple-element.20, f32[1,1,64,512]{3,2,1,0:T(8,128)S(1)} %get-tuple-element.19), kind=kLoop, calls=%fused_computation.5 | loop fusion | flops 65536 | bytes 524288 | tf_op jit(solution)/shard_map/stack | solution.py:318
  (21 shorter events, 0.3 us)
Async XLA Ops:
  0.1 0.7 %copy-start = (s32[16]{0:T(128)S(1)}, s32[16]{0:T(128)}, u32[]{:S(2)}) copy-start(s32[16]{0:T(128)} %row_blocks.1) | copy-start | bytes 196
  0.7 0.7 %copy-start.1 = (s32[8]{0:T(128)S(1)}, s32[8]{0:T(128)}, u32[]{:S(2)}) copy-start(s32[8]{0:T(128)} %col_blocks.1) | copy-start | bytes 100
  15.6 4.5 %collective-permute-start.1 = (f32[8,48,512]{2,1,0:T(8,128)S(1)}, f32[8,48,512]{2,1,0:T(8,128)S(1)}, u32[]{:S(2)}, u32[]{:S(2)}) collective-permute-start(f32[8,48,512]{2,1,0:T(8,128)S(1)} %get-tuple-element.16), channel_id=1, source_target_pairs={{0,1},{1,0},{2,3},{3,2},{4,5},{5,4},{6,7},{7,6},{8,9},{9,8},{10,11... | collective-permute-start | bytes 2359304 | tf_op jit(solution)/shard_map/ppermute | solution.py:286
  18.0 11.4 %collective-permute-start = (f32[8,48,512]{2,1,0:T(8,128)S(1)}, f32[8,48,512]{2,1,0:T(8,128)S(1)}, u32[]{:S(2)}, u32[]{:S(2)}) collective-permute-start(f32[8,48,512]{2,1,0:T(8,128)S(1)} %kept_other_product.1), channel_id=1, source_target_pairs={{0,1},{1,0},{2,3},{3,2},{4,5},{5,4},{6,7},{7,6},{8,9},{9,8},{10,11... | collective-permute-start | bytes 2359304 | tf_op jit(solution)/shard_map/ppermute | solution.py:286
  20.2 13.0 %collective-permute-start.2 = (f32[8,48,512]{2,1,0:T(8,128)S(1)}, f32[8,48,512]{2,1,0:T(8,128)S(1)}, u32[]{:S(2)}, u32[]{:S(2)}) collective-permute-start(f32[8,48,512]{2,1,0:T(8,128)S(1)} %add.31), channel_id=1, source_target_pairs={{0,2},{1,5},{2,0},{3,7},{4,6},{5,1},{6,4},{7,3},{8,10},{9,13},{10,... | collective-permute-start | bytes 2359304 | tf_op jit(solution)/shard_map/ppermute | solution.py:214
  25.6 2.0 %collective-permute-start.5 = (f32[16,16,512]{2,1,0:T(8,128)S(1)}, f32[16,16,512]{2,1,0:T(8,128)S(1)}, u32[]{:S(2)}, u32[]{:S(2)}) collective-permute-start(f32[16,16,512]{2,1,0:T(8,128)S(1)} %get-tuple-element.18), channel_id=1, source_target_pairs={{0,1},{1,0},{2,3},{3,2},{4,5},{5,4},{6,7},{7,6},{8,9},{9,8},{10,11... | collective-permute-start | bytes 1572872 | tf_op jit(solution)/shard_map/ppermute | solution.py:286
  27.8 9.2 %collective-permute-start.6 = (f32[8,16,512]{2,1,0:T(8,128)S(1)}, f32[8,16,512]{2,1,0:T(8,128)S(1)}, u32[]{:S(2)}, u32[]{:S(2)}) collective-permute-start(f32[8,16,512]{2,1,0:T(8,128)S(1)} %slice.71), channel_id=1, source_target_pairs={{0,8},{1,9},{2,10},{3,11},{4,12},{5,13},{6,14},{7,15},{8,0},{9,1},... | collective-permute-start | bytes 786440 | tf_op jit(solution)/shard_map/ppermute | solution.py:214
  33.5 10.1 %collective-permute-start.3 = (f32[4,48,512]{2,1,0:T(8,128)S(1)}, f32[4,48,512]{2,1,0:T(8,128)S(1)}, u32[]{:S(2)}, u32[]{:S(2)}) collective-permute-start(f32[4,48,512]{2,1,0:T(8,128)S(1)} %slice.67), channel_id=1, source_target_pairs={{0,4},{1,9},{2,6},{3,11},{4,0},{5,13},{6,2},{7,15},{8,12},{9,1},{1... | collective-permute-start | bytes 1179656 | tf_op jit(solution)/shard_map/ppermute | solution.py:214
  37.0 5.0 %collective-permute-start.7 = (f32[4,16,512]{2,1,0:T(8,128)S(1)}, f32[4,16,512]{2,1,0:T(8,128)S(1)}, u32[]{:S(2)}, u32[]{:S(2)}) collective-permute-start(f32[4,16,512]{2,1,0:T(8,128)S(1)} %slice.73), channel_id=1, source_target_pairs={{0,2},{1,3},{2,0},{3,1},{4,6},{5,7},{6,4},{7,5},{8,10},{9,11},{10,... | collective-permute-start | bytes 393224 | tf_op jit(solution)/shard_map/ppermute | solution.py:214
  42.1 4.3 %collective-permute-start.8 = (f32[2,16,512]{2,1,0:T(8,128)S(1)}, f32[2,16,512]{2,1,0:T(8,128)S(1)}, u32[]{:S(2)}, u32[]{:S(2)}) collective-permute-start(f32[2,16,512]{2,1,0:T(8,128)S(1)} %slice.75), channel_id=1, source_target_pairs={{0,4},{1,5},{2,6},{3,7},{4,0},{5,1},{6,2},{7,3},{8,12},{9,13},{10,... | collective-permute-start | bytes 196616 | tf_op jit(solution)/shard_map/ppermute | solution.py:214
  43.7 5.7 %collective-permute-start.4 = (f32[2,48,512]{2,1,0:T(8,128)S(1)}, f32[2,48,512]{2,1,0:T(8,128)S(1)}, u32[]{:S(2)}, u32[]{:S(2)}) collective-permute-start(f32[2,48,512]{2,1,0:T(8,128)S(1)} %slice.69), channel_id=1, source_target_pairs={{0,8},{1,3},{2,10},{3,1},{4,12},{5,7},{6,14},{7,5},{8,0},{9,11},{1... | collective-permute-start | bytes 589832 | tf_op jit(solution)/shard_map/ppermute | solution.py:214
  49.5 7.3 %collective-permute-start.9 = (f32[1,64,512]{2,1,0:T(8,128)S(1)}, f32[1,64,512]{2,1,0:T(8,128)S(1)}, u32[]{:S(2)}, u32[]{:S(2)}) collective-permute-start(f32[1,64,512]{2,1,0:T(8,128)S(1)} %pad_maximum_fusion.1), channel_id=1, source_target_pairs={{0,16},{1,17},{2,18},{3,19},{4,20},{5,21},{6,22},{7,23},{8,24},{9,... | collective-permute-start | bytes 393224 | tf_op jit(solution)/shard_map/ppermute | solution.py:214
  56.9 1.4 %collective-permute-start.10 = (f32[64,512]{1,0:T(8,128)S(1)}, f32[64,512]{1,0:T(8,128)S(1)}, u32[]{:S(2)}, u32[]{:S(2)}) collective-permute-start(f32[64,512]{1,0:T(8,128)S(1)} %bitcast.19), channel_id=1, source_target_pairs={{0,1},{1,0},{2,3},{3,2},{4,5},{5,4},{6,7},{7,6},{8,9},{9,8},{10,11... | collective-permute-start | bytes 393224 | tf_op jit(solution)/shard_map/ppermute | solution.py:286

commit v4 on v3

--- a/solution.py
+++ b/solution.py
@@ -92,7 +92,7 @@
 
 def mix_kernel(
     plan, scale, here, row_blocks, col_blocks, grads, inputs, row_bits, col_bits,
-    out, left_high, left_low, right_high, right_low, row_mixed, col_mixed,
+    sent_out, kept_out, left_high, left_low, right_high, right_low, row_mixed, col_mixed,
 ):
     step = pl.program_id(0)
     tokens, row_local = grads.shape
@@ -151,7 +151,9 @@
     @pl.when(step == pl.num_programs(0) - 1)
     def _():
         factors = (left_high, left_low, right_high, right_low)
-        product_blocks(plan, here, factors, out, *plan.first_product())
+        first_row, orders = plan.first_product()
+        product_blocks(plan, here, factors, sent_out, first_row, orders, sent_out.shape[0])
+        product_blocks(plan, here, factors, kept_out, first_row, orders, 0)
 
 
 def product_kernel(plan, wanted, here, left_high, left_low, right_high, right_low, *outs):
@@ -204,10 +206,9 @@
         return spot
 
     def first_product(self):
-        half = self.rows * self.cols // 2
         if self.split == 1:
-            return 0, self.main, half
-        return self.rows * self.per_row // 2 * BR, self.main[1:] + self.main[:1], half
+            return 0, self.main
+        return self.rows * self.per_row // 2 * BR, self.main[1:] + self.main[:1]
 
     def cross(self, part, orders, step):
         bits = (orders[0][step], orders[1][step])
@@ -234,7 +235,7 @@
     vmem = pl.BlockSpec(memory_space=pltpu.VMEM)
     main_shape = jax.ShapeDtypeStruct((blocks // 2, inner * cut, cols_each), jnp.float32)
     rest_shape = jax.ShapeDtypeStruct((blocks, inner * (BR - cut), cols_each), jnp.float32)
-    first_out, *factors = pl.pallas_call(
+    first_sent, first_kept, *factors = pl.pallas_call(
         functools.partial(mix_kernel, plan, scale),
         grid=(tokens // tile,),
         in_specs=[
@@ -246,8 +247,9 @@
             pl.BlockSpec((1, row_local), lambda step: (0, 0)),
             pl.BlockSpec((1, col_local), lambda step: (0, 0)),
         ],
-        out_specs=[vmem] * 5,
+        out_specs=[vmem] * 6,
         out_shape=[
+            main_shape,
             main_shape,
             pltpu.VMEM((left_rows, tokens), jnp.bfloat16),
             pltpu.VMEM((left_rows, tokens), jnp.bfloat16),
@@ -262,13 +264,13 @@
         name="mix",
     )(
         here,
-        row_blocks,
-        col_blocks,
+        pltpu.with_memory_space_constraint(row_blocks, pltpu.HBM),
+        pltpu.with_memory_space_constraint(col_blocks, pltpu.HBM),
         *(pltpu.with_memory_space_constraint(array, pltpu.HBM) for array in (out_grads[0], layer_inputs[0])),
         *(pltpu.with_memory_space_constraint(bits[None], pltpu.HBM) for bits in (row_bits, col_bits)),
     )
 
-    def products(wanted, shapes, name):
+    def products(wanted, shapes, name, here=here):
         return pl.pallas_call(
             functools.partial(product_kernel, plan, wanted),
             in_specs=[smem] + [vmem] * 4,
@@ -286,25 +288,27 @@
         return lax.ppermute(values, "seq", [(0, 1), (1, 0)])
 
     if plan.split == 2:
+        arrived_sent, arrived_kept = swap(first_sent), swap(first_kept)
         (sent,) = products([(0, plan.main, half)], [main_shape], "sent_product")
-        sent = sent + swap(first_out)
+        sent = sent + arrived_sent
+        later, sent = lax.optimization_barrier((here, sent))
         rest, rest_other = products(
-            [(main_rows, plan.rest, 0), (half_rows + main_rows, plan.rest, 0)], [rest_shape] * 2, "rest_products"
+            [(main_rows, plan.rest, 0), (half_rows + main_rows, plan.rest, 0)], [rest_shape] * 2, "rest_products", later
         )
         rest = rest + swap(rest_other)
-        (kept_other,) = products([(half_rows, plan.main[1:] + plan.main[:1], 0)], [main_shape], "kept_other_product")
-        (kept,) = products([(0, plan.main, 0)], [main_shape], "kept_product")
-        kept = kept + swap(kept_other)
+        (kept,) = products([(0, plan.main, 0)], [main_shape], "kept_product", later)
+        kept = kept + arrived_kept
     else:
-        sent = first_out
+        sent, kept = first_sent, first_kept
         (rest,) = products([(main_rows, plan.rest, 0)], [rest_shape], "rest_product")
-        (kept,) = products([(0, plan.main, 0)], [main_shape], "kept_product")
     steps = len(plan.main[0])
     main = kept + plan.cross(sent, plan.main, 0)
     rest = plan.halve(rest, plan.rest, 0)
     for step in range(1, steps - 1):
         main = plan.halve(main, plan.main, step)
-        rest = plan.halve(rest, plan.rest, step)
+        arrived = plan.cross(rest[rest.shape[0] // 2 :], plan.rest, step)
+        main, arrived = lax.optimization_barrier((main, arrived))
+        rest = rest[: rest.shape[0] // 2] + arrived
     both = plan.halve(jnp.concatenate([main, rest], axis=1), plan.rest, steps - 1)[0]
 
     def in_rows(values):

time: 59.3 us -> 55.9 us (0.943)
  local copies, waits for them, and re-layouts: 1.41 us -> 0.1 us
  waiting for transfers between devices: 19.6 us -> 18.4 us
    pallas_call x4 -> x3, Pallas kernels: 8.19 us -> 6.22 us  [products(): pl.pallas_call(functools.partial(product_kernel, plan, wanted), in_specs=...]
    pallas_call x1, Pallas kernels: 14.2 us -> 15.6 us  [body(): pl.pallas_call(functools.partial(mix_kernel, plan, scale), grid=(tokens /...]
    unnamed x4 -> x0, local copies, waits for them, and re-layouts: 1.31 us -> none
    ppermute x7, waiting for transfers between devices: 18.2 us -> 17 us  [cross(): return lax.ppermute(part, ('row', 'col', 'seq'), self.pairs(bits))]
  transfers between devices with their start and end apart: 11 -> 11, of which waited for: 7 -> 8; matrix products, arithmetic and copies ran while one was open for 1% -> 1% of each run, Pallas kernels for 14% -> 11%
where the time goes in v4:
time: 55.9 us; the launch traced here: 55.8 us
  Pallas kernels  21.8 us (39%)
  waiting for transfers between devices  18.4 us (33%)
  starting transfers between devices  13.8 us (25%)
  other arithmetic  1.48 us (3%)
    ppermute x7, waiting for transfers between devices, cross(): return lax.ppermute(part, ('row', 'col', 'seq'), self.pairs(bits))  17 us
    pallas_call x1, Pallas kernels, body(): pl.pallas_call(functools.partial(mix_kernel, plan, scale), grid=(tokens /...  15.6 us
    ppermute x7, starting transfers between devices, cross(): return lax.ppermute(part, ('row', 'col', 'seq'), self.pairs(bits))  13.1 us
    pallas_call x3, Pallas kernels, products(): pl.pallas_call(functools.partial(product_kernel, plan, wanted), in_specs=...  6.22 us
    ppermute x4, waiting for transfers between devices, swap(): return lax.ppermute(values, 'seq', [(0, 1), (1, 0)])  1.33 us
  transfers between devices with their start and end apart: 11, of which 8 were waited for; matrix products, arithmetic and copies ran while one was open for 1% of the time, Pallas kernels for 11%

profile of v4, /device:TPU:0, one launch (start us, length us, event | category | flops | bytes accessed | tf_op | source)
XLA Modules:
  0.0 55.8 jit_solution(10877991455173237884)
XLA Ops:
  0.0 0.1 pad_add_fusion.here
  0.1 15.6 %mix.1 = (f32[8,48,512]{2,1,0:T(8,128)S(1)}, f32[8,48,512]{2,1,0:T(8,128)S(1)}, bf16[1024,1024]{1,0:T(8,128)(2,1)S(1)}, bf16[1024,1024]{1,0:T(8,128)(2,1)S(1)}, ...) custom-call(s32[3]{0:T(128)S(1)} %pad_add_fusion.here, s32[16]{0:T(128)} %row_blocks.1, s32[8]{0:T(128)} %col_blocks.1, ...), custom_call_target="tpu_custom_call" | custom-call | tf_op jit(solution)/shard_map/mix/pallas_call | solution.py:238
  15.7 0.5 collective-permute-start
  16.2 0.1 collective-permute-start.1
  16.3 1.9 %sent_product.1 = f32[8,48,512]{2,1,0:T(8,128)S(1)} custom-call(s32[3]{0:T(128)S(1)} %pad_add_fusion.here, bf16[1024,1024]{1,0:T(8,128)(2,1)S(1)} %get-tuple-element.19.left_high, bf16[1024,1024]{1,0:T(8,128)(2,1)S(1)} %get-tuple-element.20.left_low, bf16[1024,1024]{1,0:T(8,128)(2,1)S(1)} %get-tuple-element.21.right_high, ...), custom_call_target="tpu_custom_call" | custom-call | tf_op jit(solution)/shard_map/sent_product/pallas_call | solution.py:274
  18.2 0.0 collective-permute-done
  18.2 0.1 add.30
  18.4 3.0 %collective-permute-start.2 = (f32[8,48,512]{2,1,0:T(8,128)S(1)}, f32[8,48,512]{2,1,0:T(8,128)S(1)}, u32[]{:S(2)}, u32[]{:S(2)}) collective-permute-start(f32[8,48,512]{2,1,0:T(8,128)S(1)} %add.30), channel_id=1, source_target_pairs={{0,2},{1,5},{2,0},{3,7},{4,6},{5,1},{6,4},{7,3},{8,10},{9,13},{10,... | collective-permute-start | bytes 2359304 | tf_op jit(solution)/shard_map/ppermute | solution.py:215
  21.4 2.3 %rest_products.1 = (f32[16,16,512]{2,1,0:T(8,128)S(1)}, f32[16,16,512]{2,1,0:T(8,128)S(1)}) custom-call(s32[3]{0:T(128)S(1)} %pad_add_fusion.here, bf16[1024,1024]{1,0:T(8,128)(2,1)S(1)} %get-tuple-element.19.left_high, bf16[1024,1024]{1,0:T(8,128)(2,1)S(1)} %get-tuple-element.20.left_low, bf16[1024,1024]{1,0:T(8,128)(2,1)S(1)} %get-tuple-element.21.right_high, ...), custom_call_target="tpu_custom_call" | custom-call | tf_op jit(solution)/shard_map/rest_products/pallas_call | solution.py:274
  23.8 0.1 collective-permute-start.4
  23.8 1.9 %kept_product.1 = f32[8,48,512]{2,1,0:T(8,128)S(1)} custom-call(s32[3]{0:T(128)S(1)} %pad_add_fusion.here, bf16[1024,1024]{1,0:T(8,128)(2,1)S(1)} %get-tuple-element.19.left_high, bf16[1024,1024]{1,0:T(8,128)(2,1)S(1)} %get-tuple-element.20.left_low, bf16[1024,1024]{1,0:T(8,128)(2,1)S(1)} %get-tuple-element.21.right_high, ...), custom_call_target="tpu_custom_call" | custom-call | tf_op jit(solution)/shard_map/kept_product/pallas_call | solution.py:274
  25.8 0.0 collective-permute-done.4
  25.8 0.1 add.34
  25.9 1.6 %collective-permute-start.5 = (f32[8,16,512]{2,1,0:T(8,128)S(1)}, f32[8,16,512]{2,1,0:T(8,128)S(1)}, u32[]{:S(2)}, u32[]{:S(2)}) collective-permute-start(f32[8,16,512]{2,1,0:T(8,128)S(1)} %slice.69), channel_id=1, source_target_pairs={{0,8},{1,9},{2,10},{3,11},{4,12},{5,13},{6,14},{7,15},{8,0},{9,1},... | collective-permute-start | bytes 786440 | tf_op jit(solution)/shard_map/ppermute | solution.py:215
  27.6 0.0 collective-permute-done.1
  27.6 3.8 %collective-permute-done.2 = f32[8,48,512]{2,1,0:T(8,128)S(1)} collective-permute-done((f32[8,48,512]{2,1,0:T(8,128)S(1)}, f32[8,48,512]{2,1,0:T(8,128)S(1)}, u32[]{:S(2)}, u32[]{:S(2)}) %collective-permute-start.2) | collective-permute-done | bytes 786464 | tf_op jit(solution)/shard_map/ppermute | solution.py:215
  31.4 0.2 add_add_fusion
  31.7 2.1 %collective-permute-start.3 = (f32[4,48,512]{2,1,0:T(8,128)S(1)}, f32[4,48,512]{2,1,0:T(8,128)S(1)}, u32[]{:S(2)}, u32[]{:S(2)}) collective-permute-start(f32[4,48,512]{2,1,0:T(8,128)S(1)} %slice.67), channel_id=1, source_target_pairs={{0,4},{1,9},{2,6},{3,11},{4,0},{5,13},{6,2},{7,15},{8,12},{9,1},{1... | collective-permute-start | bytes 1179656 | tf_op jit(solution)/shard_map/ppermute | solution.py:215
  33.7 1.4 %collective-permute-done.5 = f32[8,16,512]{2,1,0:T(8,128)S(1)} collective-permute-done((f32[8,16,512]{2,1,0:T(8,128)S(1)}, f32[8,16,512]{2,1,0:T(8,128)S(1)}, u32[]{:S(2)}, u32[]{:S(2)}) %collective-permute-start.5) | collective-permute-done | bytes 262176 | tf_op jit(solution)/shard_map/ppermute | solution.py:215
  35.1 0.5 collective-permute-start.6
  35.7 3.8 %collective-permute-done.3 = f32[4,48,512]{2,1,0:T(8,128)S(1)} collective-permute-done((f32[4,48,512]{2,1,0:T(8,128)S(1)}, f32[4,48,512]{2,1,0:T(8,128)S(1)}, u32[]{:S(2)}, u32[]{:S(2)}) %collective-permute-start.3) | collective-permute-done | bytes 393248 | tf_op jit(solution)/shard_map/ppermute | solution.py:215
  39.5 0.1 slice_add_fusion
  39.6 0.6 %collective-permute-done.6 = f32[4,16,512]{2,1,0:T(8,128)S(1)} collective-permute-done((f32[4,16,512]{2,1,0:T(8,128)S(1)}, f32[4,16,512]{2,1,0:T(8,128)S(1)}, u32[]{:S(2)}, u32[]{:S(2)}) %collective-permute-start.6) | collective-permute-done | bytes 131104 | tf_op jit(solution)/shard_map/ppermute | solution.py:215
  40.2 1.6 %collective-permute-start.7 = (f32[2,48,512]{2,1,0:T(8,128)S(1)}, f32[2,48,512]{2,1,0:T(8,128)S(1)}, u32[]{:S(2)}, u32[]{:S(2)}) collective-permute-start(f32[2,48,512]{2,1,0:T(8,128)S(1)} %slice.56), channel_id=1, source_target_pairs={{0,8},{1,3},{2,10},{3,1},{4,12},{5,7},{6,14},{7,5},{8,0},{9,11},{1... | collective-permute-start | bytes 589832 | tf_op jit(solution)/shard_map/ppermute | solution.py:215
  41.9 1.6 %collective-permute-start.8 = (f32[2,16,512]{2,1,0:T(8,128)S(1)}, f32[2,16,512]{2,1,0:T(8,128)S(1)}, u32[]{:S(2)}, u32[]{:S(2)}) collective-permute-start(f32[2,16,512]{2,1,0:T(8,128)S(1)} %slice.72), channel_id=1, source_target_pairs={{0,4},{1,5},{2,6},{3,7},{4,0},{5,1},{6,2},{7,3},{8,12},{9,13},{10,... | collective-permute-start | bytes 196616 | tf_op jit(solution)/shard_map/ppermute | solution.py:215
  43.4 2.5 %collective-permute-done.7 = f32[2,48,512]{2,1,0:T(8,128)S(1)} collective-permute-done((f32[2,48,512]{2,1,0:T(8,128)S(1)}, f32[2,48,512]{2,1,0:T(8,128)S(1)}, u32[]{:S(2)}, u32[]{:S(2)}) %collective-permute-start.7) | collective-permute-done | bytes 196640 | tf_op jit(solution)/shard_map/ppermute | solution.py:215
  46.0 0.2 collective-permute-done.8
  46.2 2.7 %collective-permute-start.9 = (f32[1,64,512]{2,1,0:T(8,128)S(1)}, f32[1,64,512]{2,1,0:T(8,128)S(1)}, u32[]{:S(2)}, u32[]{:S(2)}) collective-permute-start(f32[1,64,512]{2,1,0:T(8,128)S(1)} %pad_maximum_fusion.1), channel_id=1, source_target_pairs={{0,16},{1,17},{2,18},{3,19},{4,20},{5,21},{6,22},{7,23},{8,24},{9,... | collective-permute-start | bytes 393224 | tf_op jit(solution)/shard_map/ppermute | solution.py:215
  48.9 4.7 %collective-permute-done.9 = f32[1,64,512]{2,1,0:T(8,128)S(1)} collective-permute-done((f32[1,64,512]{2,1,0:T(8,128)S(1)}, f32[1,64,512]{2,1,0:T(8,128)S(1)}, u32[]{:S(2)}, u32[]{:S(2)}) %collective-permute-start.9) | collective-permute-done | bytes 131104 | tf_op jit(solution)/shard_map/ppermute | solution.py:215
  53.6 0.1 collective-permute-start.10
  53.7 1.3 %collective-permute-done.10 = f32[64,512]{1,0:T(8,128)S(1)} collective-permute-done((f32[64,512]{1,0:T(8,128)S(1)}, f32[64,512]{1,0:T(8,128)S(1)}, u32[]{:S(2)}, u32[]{:S(2)}) %collective-permute-start.10) | collective-permute-done | bytes 131104 | tf_op jit(solution)/shard_map/ppermute | solution.py:288
  55.1 0.7 %pad_maximum_fusion = f32[1,2,64,512]{3,2,1,0:T(8,128)} fusion(f32[1,1,64,512]{3,2,1,0:T(8,128)S(1)} %get-tuple-element.34, f32[1,1,64,512]{3,2,1,0:T(8,128)S(1)} %get-tuple-element.33), kind=kLoop, calls=%fused_computation.5 | loop fusion | flops 65536 | bytes 524288 | tf_op jit(solution)/shard_map/stack | solution.py:322
  (16 shorter events, 0.2 us)
Async XLA Ops:
  15.7 2.5 %collective-permute-start = (f32[8,48,512]{2,1,0:T(8,128)S(1)}, f32[8,48,512]{2,1,0:T(8,128)S(1)}, u32[]{:S(2)}, u32[]{:S(2)}) collective-permute-start(f32[8,48,512]{2,1,0:T(8,128)S(1)} %get-tuple-element.23), channel_id=1, source_target_pairs={{0,1},{1,0},{2,3},{3,2},{4,5},{5,4},{6,7},{7,6},{8,9},{9,8},{10,11... | collective-permute-start | bytes 2359304 | tf_op jit(solution)/shard_map/ppermute | solution.py:288
  16.2 11.4 %collective-permute-start.1 = (f32[8,48,512]{2,1,0:T(8,128)S(1)}, f32[8,48,512]{2,1,0:T(8,128)S(1)}, u32[]{:S(2)}, u32[]{:S(2)}) collective-permute-start(f32[8,48,512]{2,1,0:T(8,128)S(1)} %get-tuple-element.25), channel_id=1, source_target_pairs={{0,1},{1,0},{2,3},{3,2},{4,5},{5,4},{6,7},{7,6},{8,9},{9,8},{10,11... | collective-permute-start | bytes 2359304 | tf_op jit(solution)/shard_map/ppermute | solution.py:288
  18.4 13.0 %collective-permute-start.2 = (f32[8,48,512]{2,1,0:T(8,128)S(1)}, f32[8,48,512]{2,1,0:T(8,128)S(1)}, u32[]{:S(2)}, u32[]{:S(2)}) collective-permute-start(f32[8,48,512]{2,1,0:T(8,128)S(1)} %add.30), channel_id=1, source_target_pairs={{0,2},{1,5},{2,0},{3,7},{4,6},{5,1},{6,4},{7,3},{8,10},{9,13},{10,... | collective-permute-start | bytes 2359304 | tf_op jit(solution)/shard_map/ppermute | solution.py:215
  23.8 2.0 %collective-permute-start.4 = (f32[16,16,512]{2,1,0:T(8,128)S(1)}, f32[16,16,512]{2,1,0:T(8,128)S(1)}, u32[]{:S(2)}, u32[]{:S(2)}) collective-permute-start(f32[16,16,512]{2,1,0:T(8,128)S(1)} %get-tuple-element.28), channel_id=1, source_target_pairs={{0,1},{1,0},{2,3},{3,2},{4,5},{5,4},{6,7},{7,6},{8,9},{9,8},{10,11... | collective-permute-start | bytes 1572872 | tf_op jit(solution)/shard_map/ppermute | solution.py:288
  25.9 9.2 %collective-permute-start.5 = (f32[8,16,512]{2,1,0:T(8,128)S(1)}, f32[8,16,512]{2,1,0:T(8,128)S(1)}, u32[]{:S(2)}, u32[]{:S(2)}) collective-permute-start(f32[8,16,512]{2,1,0:T(8,128)S(1)} %slice.69), channel_id=1, source_target_pairs={{0,8},{1,9},{2,10},{3,11},{4,12},{5,13},{6,14},{7,15},{8,0},{9,1},... | collective-permute-start | bytes 786440 | tf_op jit(solution)/shard_map/ppermute | solution.py:215
  31.7 7.8 %collective-permute-start.3 = (f32[4,48,512]{2,1,0:T(8,128)S(1)}, f32[4,48,512]{2,1,0:T(8,128)S(1)}, u32[]{:S(2)}, u32[]{:S(2)}) collective-permute-start(f32[4,48,512]{2,1,0:T(8,128)S(1)} %slice.67), channel_id=1, source_target_pairs={{0,4},{1,9},{2,6},{3,11},{4,0},{5,13},{6,2},{7,15},{8,12},{9,1},{1... | collective-permute-start | bytes 1179656 | tf_op jit(solution)/shard_map/ppermute | solution.py:215
  35.1 5.0 %collective-permute-start.6 = (f32[4,16,512]{2,1,0:T(8,128)S(1)}, f32[4,16,512]{2,1,0:T(8,128)S(1)}, u32[]{:S(2)}, u32[]{:S(2)}) collective-permute-start(f32[4,16,512]{2,1,0:T(8,128)S(1)} %slice.70), channel_id=1, source_target_pairs={{0,2},{1,3},{2,0},{3,1},{4,6},{5,7},{6,4},{7,5},{8,10},{9,11},{10,... | collective-permute-start | bytes 393224 | tf_op jit(solution)/shard_map/ppermute | solution.py:215
  40.2 5.7 %collective-permute-start.7 = (f32[2,48,512]{2,1,0:T(8,128)S(1)}, f32[2,48,512]{2,1,0:T(8,128)S(1)}, u32[]{:S(2)}, u32[]{:S(2)}) collective-permute-start(f32[2,48,512]{2,1,0:T(8,128)S(1)} %slice.56), channel_id=1, source_target_pairs={{0,8},{1,3},{2,10},{3,1},{4,12},{5,7},{6,14},{7,5},{8,0},{9,11},{1... | collective-permute-start | bytes 589832 | tf_op jit(solution)/shard_map/ppermute | solution.py:215
  41.9 4.3 %collective-permute-start.8 = (f32[2,16,512]{2,1,0:T(8,128)S(1)}, f32[2,16,512]{2,1,0:T(8,128)S(1)}, u32[]{:S(2)}, u32[]{:S(2)}) collective-permute-start(f32[2,16,512]{2,1,0:T(8,128)S(1)} %slice.72), channel_id=1, source_target_pairs={{0,4},{1,5},{2,6},{3,7},{4,0},{5,1},{6,2},{7,3},{8,12},{9,13},{10,... | collective-permute-start | bytes 196616 | tf_op jit(solution)/shard_map/ppermute | solution.py:215
  46.2 7.3 %collective-permute-start.9 = (f32[1,64,512]{2,1,0:T(8,128)S(1)}, f32[1,64,512]{2,1,0:T(8,128)S(1)}, u32[]{:S(2)}, u32[]{:S(2)}) collective-permute-start(f32[1,64,512]{2,1,0:T(8,128)S(1)} %pad_maximum_fusion.1), channel_id=1, source_target_pairs={{0,16},{1,17},{2,18},{3,19},{4,20},{5,21},{6,22},{7,23},{8,24},{9,... | collective-permute-start | bytes 393224 | tf_op jit(solution)/shard_map/ppermute | solution.py:215
  53.6 1.4 %collective-permute-start.10 = (f32[64,512]{1,0:T(8,128)S(1)}, f32[64,512]{1,0:T(8,128)S(1)}, u32[]{:S(2)}, u32[]{:S(2)}) collective-permute-start(f32[64,512]{1,0:T(8,128)S(1)} %bitcast.19), channel_id=1, source_target_pairs={{0,1},{1,0},{2,3},{3,2},{4,5},{5,4},{6,7},{7,6},{8,9},{9,8},{10,11... | collective-permute-start | bytes 393224 | tf_op jit(solution)/shard_map/ppermute | solution.py:288

commit v5 on v4

--- a/solution.py
+++ b/solution.py
@@ -92,16 +92,23 @@
 
 def mix_kernel(
     plan, scale, here, row_blocks, col_blocks, grads, inputs, row_bits, col_bits,
-    sent_out, kept_out, left_high, left_low, right_high, right_low, row_mixed, col_mixed,
+    sent_out, rest_out, left_high, left_low, right_high, right_low, row_mixed, col_mixed,
+    signs, mixing_here,
 ):
     step = pl.program_id(0)
     tokens, row_local = grads.shape
     col_local = inputs.shape[1]
-    mixing = hadamard_table(CHUNK)
-    index = lax.broadcasted_iota(jnp.int32, (1, row_local), 1) + here[0] * row_local
-    row_sign = jnp.where(index < FF, 1 - 2 * row_bits[...], 0).astype(jnp.float32).astype(jnp.bfloat16)
-    col_sign = (1 - 2 * col_bits[...]).astype(jnp.float32).astype(jnp.bfloat16)
-
+
+    @pl.when(step == 0)
+    def _():
+        mixing_here[...] = hadamard_table(CHUNK)
+        index = lax.broadcasted_iota(jnp.int32, (1, row_local), 1) + here[0] * row_local
+        signs[0:1, :row_local] = jnp.where(index < FF, 1 - 2 * row_bits[...], 0).astype(jnp.float32)
+        signs[1:2, :col_local] = (1 - 2 * col_bits[...]).astype(jnp.float32)
+
+    mixing = mixing_here[...]
+    row_sign = signs[0:1, :row_local].astype(jnp.bfloat16)
+    col_sign = signs[1:2, :col_local].astype(jnp.bfloat16)
     for group in range(row_local // CHUNK // 4):
         parts = []
         for chunk in range(4 * group, 4 * group + 4):
@@ -153,7 +160,7 @@
         factors = (left_high, left_low, right_high, right_low)
         first_row, orders = plan.first_product()
         product_blocks(plan, here, factors, sent_out, first_row, orders, sent_out.shape[0])
-        product_blocks(plan, here, factors, kept_out, first_row, orders, 0)
+        product_blocks(plan, here, factors, rest_out, first_row + plan.rows * inner * cut, plan.rest, 0)
 
 
 def product_kernel(plan, wanted, here, left_high, left_low, right_high, right_low, *outs):
@@ -235,7 +242,7 @@
     vmem = pl.BlockSpec(memory_space=pltpu.VMEM)
     main_shape = jax.ShapeDtypeStruct((blocks // 2, inner * cut, cols_each), jnp.float32)
     rest_shape = jax.ShapeDtypeStruct((blocks, inner * (BR - cut), cols_each), jnp.float32)
-    first_sent, first_kept, *factors = pl.pallas_call(
+    first_sent, first_rest, *factors = pl.pallas_call(
         functools.partial(mix_kernel, plan, scale),
         grid=(tokens // tile,),
         in_specs=[
@@ -250,7 +257,7 @@
         out_specs=[vmem] * 6,
         out_shape=[
             main_shape,
-            main_shape,
+            rest_shape,
             pltpu.VMEM((left_rows, tokens), jnp.bfloat16),
             pltpu.VMEM((left_rows, tokens), jnp.bfloat16),
             pltpu.VMEM((tokens, right_cols), jnp.bfloat16),
@@ -259,6 +266,8 @@
         scratch_shapes=[
             pltpu.VMEM((row_local // CHUNK, CHUNK, tile), jnp.float32),
             pltpu.VMEM((col_local // CHUNK, tile, CHUNK), jnp.float32),
+            pltpu.VMEM((8, max(row_local, col_local)), jnp.float32),
+            pltpu.VMEM((CHUNK, CHUNK), jnp.bfloat16),
         ],
         compiler_params=pltpu.CompilerParams(vmem_limit_bytes=MIX_VMEM),
         name="mix",
@@ -288,21 +297,21 @@
         return lax.ppermute(values, "seq", [(0, 1), (1, 0)])
 
     if plan.split == 2:
-        arrived_sent, arrived_kept = swap(first_sent), swap(first_kept)
+        arrived_sent, arrived_rest = swap(first_sent), swap(first_rest)
         (sent,) = products([(0, plan.main, half)], [main_shape], "sent_product")
         sent = sent + arrived_sent
         later, sent = lax.optimization_barrier((here, sent))
-        rest, rest_other = products(
-            [(main_rows, plan.rest, 0), (half_rows + main_rows, plan.rest, 0)], [rest_shape] * 2, "rest_products", later
-        )
-        rest = rest + swap(rest_other)
+        later, arrived_rest = lax.optimization_barrier((later, arrived_rest))
+        (rest,) = products([(main_rows, plan.rest, 0)], [rest_shape], "rest_product", later)
+        rest = rest + arrived_rest
+        (kept_other,) = products([(half_rows, plan.main[1:] + plan.main[:1], 0)], [main_shape], "kept_other_product", later)
         (kept,) = products([(0, plan.main, 0)], [main_shape], "kept_product", later)
-        kept = kept + arrived_kept
+        main = lax.optimization_barrier(kept + plan.cross(sent, plan.main, 0)) + swap(kept_other)
     else:
-        sent, kept = first_sent, first_kept
-        (rest,) = products([(main_rows, plan.rest, 0)], [rest_shape], "rest_product")
+        rest = first_rest
+        (kept,) = products([(0, plan.main, 0)], [main_shape], "kept_product")
+        main = kept + plan.cross(first_sent, plan.main, 0)
     steps = len(plan.main[0])
-    main = kept + plan.cross(sent, plan.main, 0)
     rest = plan.halve(rest, plan.rest, 0)
     for step in range(1, steps - 1):
         main = plan.halve(main, plan.main, step)

time: 55.9 us -> 55.6 us (level)
  waiting for transfers between devices: 18.4 us -> 16.2 us
  starting transfers between devices: 13.8 us -> 15.2 us
  Pallas kernels: 21.8 us -> 22.4 us
    ppermute x7, waiting for transfers between devices: 17 us -> 14.3 us  [cross(): return lax.ppermute(part, ('row', 'col', 'seq'), self.pairs(bits))]
    ppermute x7, starting transfers between devices: 13.1 us -> 14.4 us  [cross(): return lax.ppermute(part, ('row', 'col', 'seq'), self.pairs(bits))]
    pallas_call x3 -> x4, Pallas kernels: 6.22 us -> 7.37 us  [products(): pl.pallas_call(functools.partial(product_kernel, plan, wanted), in_specs=...]
    pallas_call x1, Pallas kernels: 15.6 us -> 15 us  [body(): pl.pallas_call(functools.partial(mix_kernel, plan, scale), grid=(tokens /...]
  transfers between devices with their start and end apart: 11 -> 11, of which waited for: 8 -> 8; matrix products, arithmetic and copies ran while one was open for 1% -> 1% of each run, Pallas kernels for 11% -> 13%
where the time goes in v5:
time: 55.6 us; the launch traced here: 55.5 us
  Pallas kernels  22.4 us (40%)
  waiting for transfers between devices  16.2 us (29%)
  starting transfers between devices  15.2 us (27%)
  other arithmetic  1.52 us (3%)
    pallas_call x1, Pallas kernels, body(): pl.pallas_call(functools.partial(mix_kernel, plan, scale), grid=(tokens /...  15 us
    ppermute x7, starting transfers between devices, cross(): return lax.ppermute(part, ('row', 'col', 'seq'), self.pairs(bits))  14.4 us
    ppermute x7, waiting for transfers between devices, cross(): return lax.ppermute(part, ('row', 'col', 'seq'), self.pairs(bits))  14.3 us
    pallas_call x4, Pallas kernels, products(): pl.pallas_call(functools.partial(product_kernel, plan, wanted), in_specs=...  7.37 us
    ppermute x4, waiting for transfers between devices, swap(): return lax.ppermute(values, 'seq', [(0, 1), (1, 0)])  1.81 us
  transfers between devices with their start and end apart: 11, of which 8 were waited for; matrix products, arithmetic and copies ran while one was open for 1% of the time, Pallas kernels for 13%

profile of v5, /device:TPU:0, one launch (start us, length us, event | category | flops | bytes accessed | tf_op | source)
XLA Modules:
  0.0 55.5 jit_solution(806662934517503351)
XLA Ops:
  0.0 0.1 pad_add_fusion.here
  0.1 15.0 %mix.1 = (f32[8,48,512]{2,1,0:T(8,128)S(1)}, f32[16,16,512]{2,1,0:T(8,128)S(1)}, bf16[1024,1024]{1,0:T(8,128)(2,1)S(1)}, bf16[1024,1024]{1,0:T(8,128)(2,1)S(1)},...) custom-call(s32[3]{0:T(128)S(1)} %pad_add_fusion.here, s32[16]{0:T(128)} %row_blocks.1, s32[8]{0:T(128)} %col_blocks.1, ...), custom_call_target="tpu_custom_call" | custom-call | tf_op jit(solution)/shard_map/mix/pallas_call | solution.py:245
  15.1 0.5 collective-permute-start
  15.6 0.1 collective-permute-start.1
  15.7 1.9 %sent_product.1 = f32[8,48,512]{2,1,0:T(8,128)S(1)} custom-call(s32[3]{0:T(128)S(1)} %pad_add_fusion.here, bf16[1024,1024]{1,0:T(8,128)(2,1)S(1)} %get-tuple-element.19.left_high, bf16[1024,1024]{1,0:T(8,128)(2,1)S(1)} %get-tuple-element.20.left_low, bf16[1024,1024]{1,0:T(8,128)(2,1)S(1)} %get-tuple-element.21.right_high, ...), custom_call_target="tpu_custom_call" | custom-call | tf_op jit(solution)/shard_map/sent_product/pallas_call | solution.py:283
  17.6 0.1 add.30
  17.8 0.5 collective-permute-done.1
  18.2 2.9 %collective-permute-start.2 = (f32[8,48,512]{2,1,0:T(8,128)S(1)}, f32[8,48,512]{2,1,0:T(8,128)S(1)}, u32[]{:S(2)}, u32[]{:S(2)}) collective-permute-start(f32[8,48,512]{2,1,0:T(8,128)S(1)} %add.30), channel_id=1, source_target_pairs={{0,2},{1,5},{2,0},{3,7},{4,6},{5,1},{6,4},{7,3},{8,10},{9,13},{10,... | collective-permute-start | bytes 2359304 | tf_op jit(solution)/shard_map/ppermute | solution.py:222
  21.1 2.0 %kept_other_product.1 = f32[8,48,512]{2,1,0:T(8,128)S(1)} custom-call(s32[3]{0:T(128)S(1)} %pad_add_fusion.here, bf16[1024,1024]{1,0:T(8,128)(2,1)S(1)} %get-tuple-element.19.left_high, bf16[1024,1024]{1,0:T(8,128)(2,1)S(1)} %get-tuple-element.20.left_low, bf16[1024,1024]{1,0:T(8,128)(2,1)S(1)} %get-tuple-element.21.right_high, ...), custom_call_target="tpu_custom_call" | custom-call | tf_op jit(solution)/shard_map/kept_other_product/pallas_call | solution.py:283
  23.1 0.1 collective-permute-start.3
  23.2 1.5 %rest_product.1 = f32[16,16,512]{2,1,0:T(8,128)S(1)} custom-call(s32[3]{0:T(128)S(1)} %pad_add_fusion.here, bf16[1024,1024]{1,0:T(8,128)(2,1)S(1)} %get-tuple-element.19.left_high, bf16[1024,1024]{1,0:T(8,128)(2,1)S(1)} %get-tuple-element.20.left_low, bf16[1024,1024]{1,0:T(8,128)(2,1)S(1)} %get-tuple-element.21.right_high, ...), custom_call_target="tpu_custom_call" | custom-call | tf_op jit(solution)/shard_map/rest_product/pallas_call | solution.py:283
  24.7 0.1 add.34
  24.8 1.6 %collective-permute-start.5 = (f32[8,16,512]{2,1,0:T(8,128)S(1)}, f32[8,16,512]{2,1,0:T(8,128)S(1)}, u32[]{:S(2)}, u32[]{:S(2)}) collective-permute-start(f32[8,16,512]{2,1,0:T(8,128)S(1)} %slice.69), channel_id=1, source_target_pairs={{0,8},{1,9},{2,10},{3,11},{4,12},{5,13},{6,14},{7,15},{8,0},{9,1},... | collective-permute-start | bytes 786440 | tf_op jit(solution)/shard_map/ppermute | solution.py:222
  26.5 1.9 %kept_product.1 = f32[8,48,512]{2,1,0:T(8,128)S(1)} custom-call(s32[3]{0:T(128)S(1)} %pad_add_fusion.here, bf16[1024,1024]{1,0:T(8,128)(2,1)S(1)} %get-tuple-element.19.left_high, bf16[1024,1024]{1,0:T(8,128)(2,1)S(1)} %get-tuple-element.20.left_low, bf16[1024,1024]{1,0:T(8,128)(2,1)S(1)} %get-tuple-element.21.right_high, ...), custom_call_target="tpu_custom_call" | custom-call | tf_op jit(solution)/shard_map/kept_product/pallas_call | solution.py:283
  28.4 2.7 %collective-permute-done.2 = f32[8,48,512]{2,1,0:T(8,128)S(1)} collective-permute-done((f32[8,48,512]{2,1,0:T(8,128)S(1)}, f32[8,48,512]{2,1,0:T(8,128)S(1)}, u32[]{:S(2)}, u32[]{:S(2)}) %collective-permute-start.2) | collective-permute-done | bytes 786464 | tf_op jit(solution)/shard_map/ppermute | solution.py:222
  31.1 0.1 add.31
  31.2 0.0 collective-permute-done.3
  31.2 0.1 add.32
  31.4 2.1 %collective-permute-start.4 = (f32[4,48,512]{2,1,0:T(8,128)S(1)}, f32[4,48,512]{2,1,0:T(8,128)S(1)}, u32[]{:S(2)}, u32[]{:S(2)}) collective-permute-start(f32[4,48,512]{2,1,0:T(8,128)S(1)} %slice.67), channel_id=1, source_target_pairs={{0,4},{1,9},{2,6},{3,11},{4,0},{5,13},{6,2},{7,15},{8,12},{9,1},{1... | collective-permute-start | bytes 1179656 | tf_op jit(solution)/shard_map/ppermute | solution.py:222
  33.5 0.1 collective-permute-done.5
  33.7 1.5 %collective-permute-start.6 = (f32[4,16,512]{2,1,0:T(8,128)S(1)}, f32[4,16,512]{2,1,0:T(8,128)S(1)}, u32[]{:S(2)}, u32[]{:S(2)}) collective-permute-start(f32[4,16,512]{2,1,0:T(8,128)S(1)} %slice.70), channel_id=1, source_target_pairs={{0,2},{1,3},{2,0},{3,1},{4,6},{5,7},{6,4},{7,5},{8,10},{9,11},{10,... | collective-permute-start | bytes 393224 | tf_op jit(solution)/shard_map/ppermute | solution.py:222
  35.1 4.1 %collective-permute-done.4 = f32[4,48,512]{2,1,0:T(8,128)S(1)} collective-permute-done((f32[4,48,512]{2,1,0:T(8,128)S(1)}, f32[4,48,512]{2,1,0:T(8,128)S(1)}, u32[]{:S(2)}, u32[]{:S(2)}) %collective-permute-start.4) | collective-permute-done | bytes 393248 | tf_op jit(solution)/shard_map/ppermute | solution.py:222
  39.3 0.1 slice_add_fusion
  39.4 2.2 %collective-permute-start.7 = (f32[2,48,512]{2,1,0:T(8,128)S(1)}, f32[2,48,512]{2,1,0:T(8,128)S(1)}, u32[]{:S(2)}, u32[]{:S(2)}) collective-permute-start(f32[2,48,512]{2,1,0:T(8,128)S(1)} %slice.56), channel_id=1, source_target_pairs={{0,8},{1,3},{2,10},{3,1},{4,12},{5,7},{6,14},{7,5},{8,0},{9,11},{1... | collective-permute-start | bytes 589832 | tf_op jit(solution)/shard_map/ppermute | solution.py:222
  41.6 1.5 %collective-permute-start.8 = (f32[2,16,512]{2,1,0:T(8,128)S(1)}, f32[2,16,512]{2,1,0:T(8,128)S(1)}, u32[]{:S(2)}, u32[]{:S(2)}) collective-permute-start(f32[2,16,512]{2,1,0:T(8,128)S(1)} %slice.72), channel_id=1, source_target_pairs={{0,4},{1,5},{2,6},{3,7},{4,0},{5,1},{6,2},{7,3},{8,12},{9,13},{10,... | collective-permute-start | bytes 196616 | tf_op jit(solution)/shard_map/ppermute | solution.py:222
  43.1 2.1 %collective-permute-done.7 = f32[2,48,512]{2,1,0:T(8,128)S(1)} collective-permute-done((f32[2,48,512]{2,1,0:T(8,128)S(1)}, f32[2,48,512]{2,1,0:T(8,128)S(1)}, u32[]{:S(2)}, u32[]{:S(2)}) %collective-permute-start.7) | collective-permute-done | bytes 196640 | tf_op jit(solution)/shard_map/ppermute | solution.py:222
  45.2 0.7 %collective-permute-done.8 = f32[2,16,512]{2,1,0:T(8,128)S(1)} collective-permute-done((f32[2,16,512]{2,1,0:T(8,128)S(1)}, f32[2,16,512]{2,1,0:T(8,128)S(1)}, u32[]{:S(2)}, u32[]{:S(2)}) %collective-permute-start.8) | collective-permute-done | bytes 65568 | tf_op jit(solution)/shard_map/ppermute | solution.py:222
  45.9 2.6 %collective-permute-start.9 = (f32[1,64,512]{2,1,0:T(8,128)S(1)}, f32[1,64,512]{2,1,0:T(8,128)S(1)}, u32[]{:S(2)}, u32[]{:S(2)}) collective-permute-start(f32[1,64,512]{2,1,0:T(8,128)S(1)} %pad_maximum_fusion.1), channel_id=1, source_target_pairs={{0,16},{1,17},{2,18},{3,19},{4,20},{5,21},{6,22},{7,23},{8,24},{9,... | collective-permute-start | bytes 393224 | tf_op jit(solution)/shard_map/ppermute | solution.py:222
  48.6 4.7 %collective-permute-done.9 = f32[1,64,512]{2,1,0:T(8,128)S(1)} collective-permute-done((f32[1,64,512]{2,1,0:T(8,128)S(1)}, f32[1,64,512]{2,1,0:T(8,128)S(1)}, u32[]{:S(2)}, u32[]{:S(2)}) %collective-permute-start.9) | collective-permute-done | bytes 131104 | tf_op jit(solution)/shard_map/ppermute | solution.py:222
  53.3 0.1 collective-permute-start.10
  53.4 1.3 %collective-permute-done.10 = f32[64,512]{1,0:T(8,128)S(1)} collective-permute-done((f32[64,512]{1,0:T(8,128)S(1)}, f32[64,512]{1,0:T(8,128)S(1)}, u32[]{:S(2)}, u32[]{:S(2)}) %collective-permute-start.10) | collective-permute-done | bytes 131104 | tf_op jit(solution)/shard_map/ppermute | solution.py:297
  54.8 0.7 %pad_maximum_fusion = f32[1,2,64,512]{3,2,1,0:T(8,128)} fusion(f32[1,1,64,512]{3,2,1,0:T(8,128)S(1)} %get-tuple-element.34, f32[1,1,64,512]{3,2,1,0:T(8,128)S(1)} %get-tuple-element.33), kind=kLoop, calls=%fused_computation.4 | loop fusion | flops 65536 | bytes 524288 | tf_op jit(solution)/shard_map/stack | solution.py:331
  (18 shorter events, 0.3 us)
Async XLA Ops:
  15.1 2.5 %collective-permute-start = (f32[8,48,512]{2,1,0:T(8,128)S(1)}, f32[8,48,512]{2,1,0:T(8,128)S(1)}, u32[]{:S(2)}, u32[]{:S(2)}) collective-permute-start(f32[8,48,512]{2,1,0:T(8,128)S(1)} %get-tuple-element.23), channel_id=1, source_target_pairs={{0,1},{1,0},{2,3},{3,2},{4,5},{5,4},{6,7},{7,6},{8,9},{9,8},{10,11... | collective-permute-start | bytes 2359304 | tf_op jit(solution)/shard_map/ppermute | solution.py:297
  15.6 2.7 %collective-permute-start.1 = (f32[16,16,512]{2,1,0:T(8,128)S(1)}, f32[16,16,512]{2,1,0:T(8,128)S(1)}, u32[]{:S(2)}, u32[]{:S(2)}) collective-permute-start(f32[16,16,512]{2,1,0:T(8,128)S(1)} %get-tuple-element.25), channel_id=1, source_target_pairs={{0,1},{1,0},{2,3},{3,2},{4,5},{5,4},{6,7},{7,6},{8,9},{9,8},{10,11... | collective-permute-start | bytes 1572872 | tf_op jit(solution)/shard_map/ppermute | solution.py:297
  18.2 12.8 %collective-permute-start.2 = (f32[8,48,512]{2,1,0:T(8,128)S(1)}, f32[8,48,512]{2,1,0:T(8,128)S(1)}, u32[]{:S(2)}, u32[]{:S(2)}) collective-permute-start(f32[8,48,512]{2,1,0:T(8,128)S(1)} %add.30), channel_id=1, source_target_pairs={{0,2},{1,5},{2,0},{3,7},{4,6},{5,1},{6,4},{7,3},{8,10},{9,13},{10,... | collective-permute-start | bytes 2359304 | tf_op jit(solution)/shard_map/ppermute | solution.py:222
  23.1 8.2 %collective-permute-start.3 = (f32[8,48,512]{2,1,0:T(8,128)S(1)}, f32[8,48,512]{2,1,0:T(8,128)S(1)}, u32[]{:S(2)}, u32[]{:S(2)}) collective-permute-start(f32[8,48,512]{2,1,0:T(8,128)S(1)} %kept_other_product.1), channel_id=1, source_target_pairs={{0,1},{1,0},{2,3},{3,2},{4,5},{5,4},{6,7},{7,6},{8,9},{9,8},{10,11... | collective-permute-start | bytes 2359304 | tf_op jit(solution)/shard_map/ppermute | solution.py:297
  24.8 8.8 %collective-permute-start.5 = (f32[8,16,512]{2,1,0:T(8,128)S(1)}, f32[8,16,512]{2,1,0:T(8,128)S(1)}, u32[]{:S(2)}, u32[]{:S(2)}) collective-permute-start(f32[8,16,512]{2,1,0:T(8,128)S(1)} %slice.69), channel_id=1, source_target_pairs={{0,8},{1,9},{2,10},{3,11},{4,12},{5,13},{6,14},{7,15},{8,0},{9,1},... | collective-permute-start | bytes 786440 | tf_op jit(solution)/shard_map/ppermute | solution.py:222
  31.4 7.8 %collective-permute-start.4 = (f32[4,48,512]{2,1,0:T(8,128)S(1)}, f32[4,48,512]{2,1,0:T(8,128)S(1)}, u32[]{:S(2)}, u32[]{:S(2)}) collective-permute-start(f32[4,48,512]{2,1,0:T(8,128)S(1)} %slice.67), channel_id=1, source_target_pairs={{0,4},{1,9},{2,6},{3,11},{4,0},{5,13},{6,2},{7,15},{8,12},{9,1},{1... | collective-permute-start | bytes 1179656 | tf_op jit(solution)/shard_map/ppermute | solution.py:222
  33.7 5.7 %collective-permute-start.6 = (f32[4,16,512]{2,1,0:T(8,128)S(1)}, f32[4,16,512]{2,1,0:T(8,128)S(1)}, u32[]{:S(2)}, u32[]{:S(2)}) collective-permute-start(f32[4,16,512]{2,1,0:T(8,128)S(1)} %slice.70), channel_id=1, source_target_pairs={{0,2},{1,3},{2,0},{3,1},{4,6},{5,7},{6,4},{7,5},{8,10},{9,11},{10,... | collective-permute-start | bytes 393224 | tf_op jit(solution)/shard_map/ppermute | solution.py:222
  39.4 5.8 %collective-permute-start.7 = (f32[2,48,512]{2,1,0:T(8,128)S(1)}, f32[2,48,512]{2,1,0:T(8,128)S(1)}, u32[]{:S(2)}, u32[]{:S(2)}) collective-permute-start(f32[2,48,512]{2,1,0:T(8,128)S(1)} %slice.56), channel_id=1, source_target_pairs={{0,8},{1,3},{2,10},{3,1},{4,12},{5,7},{6,14},{7,5},{8,0},{9,11},{1... | collective-permute-start | bytes 589832 | tf_op jit(solution)/shard_map/ppermute | solution.py:222
  41.6 4.3 %collective-permute-start.8 = (f32[2,16,512]{2,1,0:T(8,128)S(1)}, f32[2,16,512]{2,1,0:T(8,128)S(1)}, u32[]{:S(2)}, u32[]{:S(2)}) collective-permute-start(f32[2,16,512]{2,1,0:T(8,128)S(1)} %slice.72), channel_id=1, source_target_pairs={{0,4},{1,5},{2,6},{3,7},{4,0},{5,1},{6,2},{7,3},{8,12},{9,13},{10,... | collective-permute-start | bytes 196616 | tf_op jit(solution)/shard_map/ppermute | solution.py:222
  45.9 7.3 %collective-permute-start.9 = (f32[1,64,512]{2,1,0:T(8,128)S(1)}, f32[1,64,512]{2,1,0:T(8,128)S(1)}, u32[]{:S(2)}, u32[]{:S(2)}) collective-permute-start(f32[1,64,512]{2,1,0:T(8,128)S(1)} %pad_maximum_fusion.1), channel_id=1, source_target_pairs={{0,16},{1,17},{2,18},{3,19},{4,20},{5,21},{6,22},{7,23},{8,24},{9,... | collective-permute-start | bytes 393224 | tf_op jit(solution)/shard_map/ppermute | solution.py:222
  53.3 1.4 %collective-permute-start.10 = (f32[64,512]{1,0:T(8,128)S(1)}, f32[64,512]{1,0:T(8,128)S(1)}, u32[]{:S(2)}, u32[]{:S(2)}) collective-permute-start(f32[64,512]{1,0:T(8,128)S(1)} %bitcast.19), channel_id=1, source_target_pairs={{0,1},{1,0},{2,3},{3,2},{4,5},{5,4},{6,7},{7,6},{8,9},{9,8},{10,11... | collective-permute-start | bytes 393224 | tf_op jit(solution)/shard_map/ppermute | solution.py:297

commit v6 on v5

--- a/solution.py
+++ b/solution.py
@@ -15,6 +15,7 @@
 TILE = 256
 MIX_VMEM = 30 << 20
 PRODUCT_VMEM = 16 << 20
+AHEAD = 20 * 10**9
 
 
 def scalar_parity(first, second):
@@ -90,11 +91,16 @@
             pl.when(here[2] % 2 == seq)(functools.partial(run, order))
 
 
+def device_place():
+    return [lax.axis_index(name) for name in ("row", "col", "seq")]
+
+
 def mix_kernel(
-    plan, scale, here, row_blocks, col_blocks, grads, inputs, row_bits, col_bits,
-    sent_out, rest_out, left_high, left_low, right_high, right_low, row_mixed, col_mixed,
+    plan, scale, row_blocks, col_blocks, grads, inputs, row_bits, col_bits,
+    sent_out, left_high, left_low, right_high, right_low, row_mixed, col_mixed,
     signs, mixing_here,
 ):
+    here = device_place()
     step = pl.program_id(0)
     tokens, row_local = grads.shape
     col_local = inputs.shape[1]
@@ -160,13 +166,30 @@
         factors = (left_high, left_low, right_high, right_low)
         first_row, orders = plan.first_product()
         product_blocks(plan, here, factors, sent_out, first_row, orders, sent_out.shape[0])
-        product_blocks(plan, here, factors, rest_out, first_row + plan.rows * inner * cut, plan.rest, 0)
-
-
-def product_kernel(plan, wanted, here, left_high, left_low, right_high, right_low, *outs):
+
+
+def product_kernel(plan, wanted, after, left_high, left_low, right_high, right_low, *outs):
+    here = device_place()
     factors = (left_high, left_low, right_high, right_low)
     for args, out in zip(wanted, outs):
         product_blocks(plan, here, factors, out, *args)
+
+
+def add_kernel(first, second, out):
+    out[...] = first[...] + second[...]
+
+
+def add_early(first, second):
+    vmem = pl.BlockSpec(memory_space=pltpu.VMEM)
+    return pl.pallas_call(
+        add_kernel,
+        in_specs=[vmem] * 2,
+        out_specs=vmem,
+        out_shape=jax.ShapeDtypeStruct(first.shape, first.dtype),
+        compiler_params=pltpu.CompilerParams(vmem_limit_bytes=PRODUCT_VMEM),
+        cost_estimate=pl.CostEstimate(flops=AHEAD, bytes_accessed=AHEAD // 100, transcendentals=0),
+        name="add_early",
+    )(first, second)
 
 
 class Plan:
@@ -230,7 +253,7 @@
     tokens, row_local = out_grads.shape[1:]
     col_local = layer_inputs.shape[2]
     tile = min(TILE, tokens)
-    here = jnp.stack([lax.axis_index(name) for name in ("row", "col", "seq")]).astype(jnp.int32)
+    start = jnp.zeros((8, 128), jnp.float32)
     scale = 1.0 / math.sqrt(row_local * plan.rows * col_local * plan.cols)
     left_rows = plan.rows * plan.per_row * BR
     right_cols = plan.cols * plan.per_col * BC
@@ -242,11 +265,10 @@
     vmem = pl.BlockSpec(memory_space=pltpu.VMEM)
     main_shape = jax.ShapeDtypeStruct((blocks // 2, inner * cut, cols_each), jnp.float32)
     rest_shape = jax.ShapeDtypeStruct((blocks, inner * (BR - cut), cols_each), jnp.float32)
-    first_sent, first_rest, *factors = pl.pallas_call(
+    first_sent, *factors = pl.pallas_call(
         functools.partial(mix_kernel, plan, scale),
         grid=(tokens // tile,),
         in_specs=[
-            smem,
             smem,
             smem,
             pl.BlockSpec((tile, row_local), lambda step: (step, 0)),
@@ -254,10 +276,9 @@
             pl.BlockSpec((1, row_local), lambda step: (0, 0)),
             pl.BlockSpec((1, col_local), lambda step: (0, 0)),
         ],
-        out_specs=[vmem] * 6,
+        out_specs=[vmem] * 5,
         out_shape=[
             main_shape,
-            rest_shape,
             pltpu.VMEM((left_rows, tokens), jnp.bfloat16),
             pltpu.VMEM((left_rows, tokens), jnp.bfloat16),
             pltpu.VMEM((tokens, right_cols), jnp.bfloat16),
@@ -272,22 +293,21 @@
         compiler_params=pltpu.CompilerParams(vmem_limit_bytes=MIX_VMEM),
         name="mix",
     )(
-        here,
         pltpu.with_memory_space_constraint(row_blocks, pltpu.HBM),
         pltpu.with_memory_space_constraint(col_blocks, pltpu.HBM),
         *(pltpu.with_memory_space_constraint(array, pltpu.HBM) for array in (out_grads[0], layer_inputs[0])),
         *(pltpu.with_memory_space_constraint(bits[None], pltpu.HBM) for bits in (row_bits, col_bits)),
     )
 
-    def products(wanted, shapes, name, here=here):
+    def products(wanted, shapes, name, after=start):
         return pl.pallas_call(
             functools.partial(product_kernel, plan, wanted),
-            in_specs=[smem] + [vmem] * 4,
+            in_specs=[pl.BlockSpec(memory_space=pl.ANY)] + [vmem] * 4,
             out_specs=[vmem] * len(shapes),
             out_shape=shapes,
             compiler_params=pltpu.CompilerParams(vmem_limit_bytes=PRODUCT_VMEM),
             name=name,
-        )(here, *factors)
+        )(after, *factors)
 
     half = blocks // 2
     half_rows = plan.rows * inner * BR
@@ -297,18 +317,20 @@
         return lax.ppermute(values, "seq", [(0, 1), (1, 0)])
 
     if plan.split == 2:
-        arrived_sent, arrived_rest = swap(first_sent), swap(first_rest)
-        (sent,) = products([(0, plan.main, half)], [main_shape], "sent_product")
+        arrived_sent = swap(first_sent)
+        sent, rest_other = products(
+            [(0, plan.main, half), (half_rows + main_rows, plan.rest, 0)], [main_shape, rest_shape], "sent_products"
+        )
         sent = sent + arrived_sent
-        later, sent = lax.optimization_barrier((here, sent))
-        later, arrived_rest = lax.optimization_barrier((later, arrived_rest))
-        (rest,) = products([(main_rows, plan.rest, 0)], [rest_shape], "rest_product", later)
+        later, sent = lax.optimization_barrier((start, sent))
+        after, arrived_rest = lax.optimization_barrier((later, swap(rest_other)))
+        (rest,) = products([(main_rows, plan.rest, 0)], [rest_shape], "rest_product", after)
         rest = rest + arrived_rest
         (kept_other,) = products([(half_rows, plan.main[1:] + plan.main[:1], 0)], [main_shape], "kept_other_product", later)
         (kept,) = products([(0, plan.main, 0)], [main_shape], "kept_product", later)
-        main = lax.optimization_barrier(kept + plan.cross(sent, plan.main, 0)) + swap(kept_other)
+        main = add_early(kept, plan.cross(sent, plan.main, 0)) + swap(kept_other)
     else:
-        rest = first_rest
+        (rest,) = products([(main_rows, plan.rest, 0)], [rest_shape], "rest_product")
         (kept,) = products([(0, plan.main, 0)], [main_shape], "kept_product")
         main = kept + plan.cross(first_sent, plan.main, 0)
     steps = len(plan.main[0])

time: 55.6 us -> 54.1 us (0.973)
  Pallas kernels: 22.4 us -> 20.2 us
  waiting for transfers between devices: 16.2 us -> 17.4 us
    ppermute x7, waiting for transfers between devices: 14.3 us -> 16.1 us  [cross(): return lax.ppermute(part, ('row', 'col', 'seq'), self.pairs(bits))]
    pallas_call x4, Pallas kernels: 7.37 us -> 6.15 us  [products(): pl.pallas_call(functools.partial(product_kernel, plan, wanted), in_specs=...]
    pallas_call x1, Pallas kernels: 15 us -> 14 us  [body(): pl.pallas_call(functools.partial(mix_kernel, plan, scale), grid=(tokens /...]
  transfers between devices with their start and end apart: 11 -> 11, of which waited for: 8 -> 7; matrix products, arithmetic and copies ran while one was open for 1% -> 1% of each run, Pallas kernels for 13% -> 12%
where the time goes in v6:
time: 54.1 us; the launch traced here: 53.9 us
  Pallas kernels  20.2 us (37%)
  waiting for transfers between devices  17.4 us (32%)
  starting transfers between devices  14.7 us (27%)
  other arithmetic  1.29 us (2%)
    ppermute x7, waiting for transfers between devices, cross(): return lax.ppermute(part, ('row', 'col', 'seq'), self.pairs(bits))  16.1 us
    ppermute x7, starting transfers between devices, cross(): return lax.ppermute(part, ('row', 'col', 'seq'), self.pairs(bits))  14 us
    pallas_call x1, Pallas kernels, body(): pl.pallas_call(functools.partial(mix_kernel, plan, scale), grid=(tokens /...  14 us
    pallas_call x4, Pallas kernels, products(): pl.pallas_call(functools.partial(product_kernel, plan, wanted), in_specs=...  6.15 us
    ppermute x4, waiting for transfers between devices, swap(): return lax.ppermute(values, 'seq', [(0, 1), (1, 0)])  1.33 us
  transfers between devices with their start and end apart: 11, of which 7 were waited for; matrix products, arithmetic and copies ran while one was open for 1% of the time, Pallas kernels for 12%

profile of v6, /device:TPU:0, one launch (start us, length us, event | category | flops | bytes accessed | tf_op | source)
XLA Modules:
  0.0 53.9 jit_solution(843453070191025676)
XLA Ops:
  0.0 14.0 %mix.1 = (f32[8,48,512]{2,1,0:T(8,128)S(1)}, bf16[1024,1024]{1,0:T(8,128)(2,1)S(1)}, bf16[1024,1024]{1,0:T(8,128)(2,1)S(1)}, bf16[1024,1024]{1,0:T(8,128)(2,1)S(1)}, bf16[1024,1024]{1,0:T(8,128)(2,1)S(1)}) custom-call(s32[16]{0:T(128)} %row_blocks.1, s32[8]{0:T(128)} %col_blocks.1, bf16[1024,4096]{1,0:T(8,128)(2,1)} %bitcast.14, ...), custom_call_target="tpu_custom_call" | custom-call | tf_op jit(solution)/shard_map/mix/pallas_call | solution.py:268
  14.0 0.5 collective-permute-start
  14.5 2.4 %sent_products.1 = (f32[8,48,512]{2,1,0:T(8,128)S(1)}, f32[16,16,512]{2,1,0:T(8,128)S(1)}) custom-call(f32[8,128]{1,0:T(8,128)S(1)} %broadcast_in_dim.9.after, bf16[1024,1024]{1,0:T(8,128)(2,1)S(1)} %get-tuple-element.20.left_high, bf16[1024,1024]{1,0:T(8,128)(2,1)S(1)} %get-tuple-element.21.left_low, bf16[1024,1024]{1,0:T(8,128)(2,1)S(1)} %get-tuple-element.22.right_high, ...), custom_call_target="tpu_custom_call" | custom-call | tf_op jit(solution)/shard_map/sent_products/pallas_call | solution.py:303
  16.8 0.0 collective-permute-done
  16.8 0.1 add.27
  17.0 2.6 %collective-permute-start.1 = (f32[8,48,512]{2,1,0:T(8,128)S(1)}, f32[8,48,512]{2,1,0:T(8,128)S(1)}, u32[]{:S(2)}, u32[]{:S(2)}) collective-permute-start(f32[8,48,512]{2,1,0:T(8,128)S(1)} %add.27), channel_id=1, source_target_pairs={{0,2},{1,5},{2,0},{3,7},{4,6},{5,1},{6,4},{7,3},{8,10},{9,13},{10,... | collective-permute-start | bytes 2359304 | tf_op jit(solution)/shard_map/ppermute | solution.py:245
  19.6 0.2 collective-permute-start.4
  19.8 1.4 %kept_other_product.1 = f32[8,48,512]{2,1,0:T(8,128)S(1)} custom-call(f32[8,128]{1,0:T(8,128)S(1)} %broadcast_in_dim.9.after, bf16[1024,1024]{1,0:T(8,128)(2,1)S(1)} %get-tuple-element.20.left_high, bf16[1024,1024]{1,0:T(8,128)(2,1)S(1)} %get-tuple-element.21.left_low, bf16[1024,1024]{1,0:T(8,128)(2,1)S(1)} %get-tuple-element.22.right_high, ...), custom_call_target="tpu_custom_call" | custom-call | tf_op jit(solution)/shard_map/kept_other_product/pallas_call | solution.py:303
  21.2 1.4 %kept_product.1.first = f32[8,48,512]{2,1,0:T(8,128)S(1)} custom-call(f32[8,128]{1,0:T(8,128)S(1)} %broadcast_in_dim.9.after, bf16[1024,1024]{1,0:T(8,128)(2,1)S(1)} %get-tuple-element.20.left_high, bf16[1024,1024]{1,0:T(8,128)(2,1)S(1)} %get-tuple-element.21.left_low, bf16[1024,1024]{1,0:T(8,128)(2,1)S(1)} %get-tuple-element.22.right_high, ...), custom_call_target="tpu_custom_call" | custom-call | tf_op jit(solution)/shard_map/kept_product/pallas_call | solution.py:303
  22.6 0.0 collective-permute-done.4
  22.6 1.0 %rest_product.1 = f32[16,16,512]{2,1,0:T(8,128)S(1)} custom-call(f32[8,128]{1,0:T(8,128)S(1)} %broadcast_in_dim.9.after, bf16[1024,1024]{1,0:T(8,128)(2,1)S(1)} %get-tuple-element.20.left_high, bf16[1024,1024]{1,0:T(8,128)(2,1)S(1)} %get-tuple-element.21.left_low, bf16[1024,1024]{1,0:T(8,128)(2,1)S(1)} %get-tuple-element.22.right_high, ...), custom_call_target="tpu_custom_call" | custom-call | tf_op jit(solution)/shard_map/rest_product/pallas_call | solution.py:303
  23.6 0.1 add.30
  23.7 1.6 %collective-permute-start.5 = (f32[8,16,512]{2,1,0:T(8,128)S(1)}, f32[8,16,512]{2,1,0:T(8,128)S(1)}, u32[]{:S(2)}, u32[]{:S(2)}) collective-permute-start(f32[8,16,512]{2,1,0:T(8,128)S(1)} %slice.69), channel_id=1, source_target_pairs={{0,8},{1,9},{2,10},{3,11},{4,12},{5,13},{6,14},{7,15},{8,0},{9,1},... | collective-permute-start | bytes 786440 | tf_op jit(solution)/shard_map/ppermute | solution.py:245
  25.4 0.0 collective-permute-start.2
  25.4 4.2 %collective-permute-done.1.second = f32[8,48,512]{2,1,0:T(8,128)S(1)} collective-permute-done((f32[8,48,512]{2,1,0:T(8,128)S(1)}, f32[8,48,512]{2,1,0:T(8,128)S(1)}, u32[]{:S(2)}, u32[]{:S(2)}) %collective-permute-start.1) | collective-permute-done | bytes 786464 | tf_op jit(solution)/shard_map/ppermute | solution.py:245
  29.6 0.1 add_early.1
  29.7 0.0 collective-permute-done.2
  29.7 0.1 add.28
  29.9 2.1 %collective-permute-start.3 = (f32[4,48,512]{2,1,0:T(8,128)S(1)}, f32[4,48,512]{2,1,0:T(8,128)S(1)}, u32[]{:S(2)}, u32[]{:S(2)}) collective-permute-start(f32[4,48,512]{2,1,0:T(8,128)S(1)} %slice.67), channel_id=1, source_target_pairs={{0,4},{1,9},{2,6},{3,11},{4,0},{5,13},{6,2},{7,15},{8,12},{9,1},{1... | collective-permute-start | bytes 1179656 | tf_op jit(solution)/shard_map/ppermute | solution.py:245
  31.9 0.4 collective-permute-done.5
  32.4 1.3 %collective-permute-start.6 = (f32[4,16,512]{2,1,0:T(8,128)S(1)}, f32[4,16,512]{2,1,0:T(8,128)S(1)}, u32[]{:S(2)}, u32[]{:S(2)}) collective-permute-start(f32[4,16,512]{2,1,0:T(8,128)S(1)} %slice.70), channel_id=1, source_target_pairs={{0,2},{1,3},{2,0},{3,1},{4,6},{5,7},{6,4},{7,5},{8,10},{9,11},{10,... | collective-permute-start | bytes 393224 | tf_op jit(solution)/shard_map/ppermute | solution.py:245
  33.7 4.1 %collective-permute-done.3 = f32[4,48,512]{2,1,0:T(8,128)S(1)} collective-permute-done((f32[4,48,512]{2,1,0:T(8,128)S(1)}, f32[4,48,512]{2,1,0:T(8,128)S(1)}, u32[]{:S(2)}, u32[]{:S(2)}) %collective-permute-start.3) | collective-permute-done | bytes 393248 | tf_op jit(solution)/shard_map/ppermute | solution.py:245
  37.7 0.1 slice_add_fusion
  37.8 2.1 %collective-permute-start.7 = (f32[2,48,512]{2,1,0:T(8,128)S(1)}, f32[2,48,512]{2,1,0:T(8,128)S(1)}, u32[]{:S(2)}, u32[]{:S(2)}) collective-permute-start(f32[2,48,512]{2,1,0:T(8,128)S(1)} %slice.56), channel_id=1, source_target_pairs={{0,8},{1,3},{2,10},{3,1},{4,12},{5,7},{6,14},{7,5},{8,0},{9,11},{1... | collective-permute-start | bytes 589832 | tf_op jit(solution)/shard_map/ppermute | solution.py:245
  40.0 1.6 %collective-permute-start.8 = (f32[2,16,512]{2,1,0:T(8,128)S(1)}, f32[2,16,512]{2,1,0:T(8,128)S(1)}, u32[]{:S(2)}, u32[]{:S(2)}) collective-permute-start(f32[2,16,512]{2,1,0:T(8,128)S(1)} %slice.72), channel_id=1, source_target_pairs={{0,4},{1,5},{2,6},{3,7},{4,0},{5,1},{6,2},{7,3},{8,12},{9,13},{10,... | collective-permute-start | bytes 196616 | tf_op jit(solution)/shard_map/ppermute | solution.py:245
  41.6 2.1 %collective-permute-done.7 = f32[2,48,512]{2,1,0:T(8,128)S(1)} collective-permute-done((f32[2,48,512]{2,1,0:T(8,128)S(1)}, f32[2,48,512]{2,1,0:T(8,128)S(1)}, u32[]{:S(2)}, u32[]{:S(2)}) %collective-permute-start.7) | collective-permute-done | bytes 196640 | tf_op jit(solution)/shard_map/ppermute | solution.py:245
  43.6 0.7 %collective-permute-done.8 = f32[2,16,512]{2,1,0:T(8,128)S(1)} collective-permute-done((f32[2,16,512]{2,1,0:T(8,128)S(1)}, f32[2,16,512]{2,1,0:T(8,128)S(1)}, u32[]{:S(2)}, u32[]{:S(2)}) %collective-permute-start.8) | collective-permute-done | bytes 65568 | tf_op jit(solution)/shard_map/ppermute | solution.py:245
  44.4 2.7 %collective-permute-start.9 = (f32[1,64,512]{2,1,0:T(8,128)S(1)}, f32[1,64,512]{2,1,0:T(8,128)S(1)}, u32[]{:S(2)}, u32[]{:S(2)}) collective-permute-start(f32[1,64,512]{2,1,0:T(8,128)S(1)} %pad_maximum_fusion.1), channel_id=1, source_target_pairs={{0,16},{1,17},{2,18},{3,19},{4,20},{5,21},{6,22},{7,23},{8,24},{9,... | collective-permute-start | bytes 393224 | tf_op jit(solution)/shard_map/ppermute | solution.py:245
  47.0 4.7 %collective-permute-done.9 = f32[1,64,512]{2,1,0:T(8,128)S(1)} collective-permute-done((f32[1,64,512]{2,1,0:T(8,128)S(1)}, f32[1,64,512]{2,1,0:T(8,128)S(1)}, u32[]{:S(2)}, u32[]{:S(2)}) %collective-permute-start.9) | collective-permute-done | bytes 131104 | tf_op jit(solution)/shard_map/ppermute | solution.py:245
  51.7 0.1 collective-permute-start.10
  51.8 1.3 %collective-permute-done.10 = f32[64,512]{1,0:T(8,128)S(1)} collective-permute-done((f32[64,512]{1,0:T(8,128)S(1)}, f32[64,512]{1,0:T(8,128)S(1)}, u32[]{:S(2)}, u32[]{:S(2)}) %collective-permute-start.10) | collective-permute-done | bytes 131104 | tf_op jit(solution)/shard_map/ppermute | solution.py:317
  53.2 0.7 %pad_maximum_fusion = f32[1,2,64,512]{3,2,1,0:T(8,128)} fusion(f32[1,1,64,512]{3,2,1,0:T(8,128)S(1)} %get-tuple-element.36, f32[1,1,64,512]{3,2,1,0:T(8,128)S(1)} %get-tuple-element.35), kind=kLoop, calls=%fused_computation.4 | loop fusion | flops 65536 | bytes 524288 | tf_op jit(solution)/shard_map/stack | solution.py:353
  (18 shorter events, 0.3 us)
Async XLA Ops:
  14.0 2.9 %collective-permute-start = (f32[8,48,512]{2,1,0:T(8,128)S(1)}, f32[8,48,512]{2,1,0:T(8,128)S(1)}, u32[]{:S(2)}, u32[]{:S(2)}) collective-permute-start(f32[8,48,512]{2,1,0:T(8,128)S(1)} %get-tuple-element.25), channel_id=1, source_target_pairs={{0,1},{1,0},{2,3},{3,2},{4,5},{5,4},{6,7},{7,6},{8,9},{9,8},{10,11... | collective-permute-start | bytes 2359304 | tf_op jit(solution)/shard_map/ppermute | solution.py:317
  17.0 12.6 %collective-permute-start.1 = (f32[8,48,512]{2,1,0:T(8,128)S(1)}, f32[8,48,512]{2,1,0:T(8,128)S(1)}, u32[]{:S(2)}, u32[]{:S(2)}) collective-permute-start(f32[8,48,512]{2,1,0:T(8,128)S(1)} %add.27), channel_id=1, source_target_pairs={{0,2},{1,5},{2,0},{3,7},{4,6},{5,1},{6,4},{7,3},{8,10},{9,13},{10,... | collective-permute-start | bytes 2359304 | tf_op jit(solution)/shard_map/ppermute | solution.py:245
  19.6 3.0 %collective-permute-start.4 = (f32[16,16,512]{2,1,0:T(8,128)S(1)}, f32[16,16,512]{2,1,0:T(8,128)S(1)}, u32[]{:S(2)}, u32[]{:S(2)}) collective-permute-start(f32[16,16,512]{2,1,0:T(8,128)S(1)} %get-tuple-element.28), channel_id=1, source_target_pairs={{0,1},{1,0},{2,3},{3,2},{4,5},{5,4},{6,7},{7,6},{8,9},{9,8},{10,11... | collective-permute-start | bytes 1572872 | tf_op jit(solution)/shard_map/ppermute | solution.py:317
  23.7 8.6 %collective-permute-start.5 = (f32[8,16,512]{2,1,0:T(8,128)S(1)}, f32[8,16,512]{2,1,0:T(8,128)S(1)}, u32[]{:S(2)}, u32[]{:S(2)}) collective-permute-start(f32[8,16,512]{2,1,0:T(8,128)S(1)} %slice.69), channel_id=1, source_target_pairs={{0,8},{1,9},{2,10},{3,11},{4,12},{5,13},{6,14},{7,15},{8,0},{9,1},... | collective-permute-start | bytes 786440 | tf_op jit(solution)/shard_map/ppermute | solution.py:245
  25.4 4.3 %collective-permute-start.2 = (f32[8,48,512]{2,1,0:T(8,128)S(1)}, f32[8,48,512]{2,1,0:T(8,128)S(1)}, u32[]{:S(2)}, u32[]{:S(2)}) collective-permute-start(f32[8,48,512]{2,1,0:T(8,128)S(1)} %kept_other_product.1), channel_id=1, source_target_pairs={{0,1},{1,0},{2,3},{3,2},{4,5},{5,4},{6,7},{7,6},{8,9},{9,8},{10,11... | collective-permute-start | bytes 2359304 | tf_op jit(solution)/shard_map/ppermute | solution.py:317
  29.9 7.8 %collective-permute-start.3 = (f32[4,48,512]{2,1,0:T(8,128)S(1)}, f32[4,48,512]{2,1,0:T(8,128)S(1)}, u32[]{:S(2)}, u32[]{:S(2)}) collective-permute-start(f32[4,48,512]{2,1,0:T(8,128)S(1)} %slice.67), channel_id=1, source_target_pairs={{0,4},{1,9},{2,6},{3,11},{4,0},{5,13},{6,2},{7,15},{8,12},{9,1},{1... | collective-permute-start | bytes 1179656 | tf_op jit(solution)/shard_map/ppermute | solution.py:245
  32.4 5.4 %collective-permute-start.6 = (f32[4,16,512]{2,1,0:T(8,128)S(1)}, f32[4,16,512]{2,1,0:T(8,128)S(1)}, u32[]{:S(2)}, u32[]{:S(2)}) collective-permute-start(f32[4,16,512]{2,1,0:T(8,128)S(1)} %slice.70), channel_id=1, source_target_pairs={{0,2},{1,3},{2,0},{3,1},{4,6},{5,7},{6,4},{7,5},{8,10},{9,11},{10,... | collective-permute-start | bytes 393224 | tf_op jit(solution)/shard_map/ppermute | solution.py:245
  37.8 5.8 %collective-permute-start.7 = (f32[2,48,512]{2,1,0:T(8,128)S(1)}, f32[2,48,512]{2,1,0:T(8,128)S(1)}, u32[]{:S(2)}, u32[]{:S(2)}) collective-permute-start(f32[2,48,512]{2,1,0:T(8,128)S(1)} %slice.56), channel_id=1, source_target_pairs={{0,8},{1,3},{2,10},{3,1},{4,12},{5,7},{6,14},{7,5},{8,0},{9,11},{1... | collective-permute-start | bytes 589832 | tf_op jit(solution)/shard_map/ppermute | solution.py:245
  40.0 4.3 %collective-permute-start.8 = (f32[2,16,512]{2,1,0:T(8,128)S(1)}, f32[2,16,512]{2,1,0:T(8,128)S(1)}, u32[]{:S(2)}, u32[]{:S(2)}) collective-permute-start(f32[2,16,512]{2,1,0:T(8,128)S(1)} %slice.72), channel_id=1, source_target_pairs={{0,4},{1,5},{2,6},{3,7},{4,0},{5,1},{6,2},{7,3},{8,12},{9,13},{10,... | collective-permute-start | bytes 196616 | tf_op jit(solution)/shard_map/ppermute | solution.py:245
  44.4 7.3 %collective-permute-start.9 = (f32[1,64,512]{2,1,0:T(8,128)S(1)}, f32[1,64,512]{2,1,0:T(8,128)S(1)}, u32[]{:S(2)}, u32[]{:S(2)}) collective-permute-start(f32[1,64,512]{2,1,0:T(8,128)S(1)} %pad_maximum_fusion.1), channel_id=1, source_target_pairs={{0,16},{1,17},{2,18},{3,19},{4,20},{5,21},{6,22},{7,23},{8,24},{9,... | collective-permute-start | bytes 393224 | tf_op jit(solution)/shard_map/ppermute | solution.py:245
  51.7 1.4 %collective-permute-start.10 = (f32[64,512]{1,0:T(8,128)S(1)}, f32[64,512]{1,0:T(8,128)S(1)}, u32[]{:S(2)}, u32[]{:S(2)}) collective-permute-start(f32[64,512]{1,0:T(8,128)S(1)} %bitcast.16), channel_id=1, source_target_pairs={{0,1},{1,0},{2,3},{3,2},{4,5},{5,4},{6,7},{7,6},{8,9},{9,8},{10,11... | collective-permute-start | bytes 393224 | tf_op jit(solution)/shard_map/ppermute | solution.py:317

commit v7 on v6

--- a/solution.py
+++ b/solution.py
@@ -60,35 +60,39 @@
     low_ref[where] = (values - high.astype(jnp.float32)).astype(jnp.bfloat16)
 
 
-def product_blocks(plan, here, factors, out_ref, first_row, orders, begin):
+def product_blocks(plan, here, factors, wanted):
     left_high, left_low, right_high, right_low = factors
-    count, rows, width = out_ref.shape
+    width = wanted[0][0].shape[2]
     tile = min(CHUNK, width)
 
-    def run(order):
+    def run(seq):
         for start in range(0, plan.cols * width, tile):
-            col = start // width
-            places = [plan.place(order, row, col) - begin for row in plan.row_sequence]
-            wanted = [spot for spot, place in enumerate(places) if 0 <= place < count]
-            while wanted:
+            pieces = []
+            for out_ref, first_row, orders, begin in wanted:
+                count, rows, _ = out_ref.shape
+                for spot, row in enumerate(plan.row_sequence):
+                    place = plan.place(orders[seq], row, start // width) - begin
+                    if 0 <= place < count:
+                        pieces.append((first_row + spot * rows, rows, place, out_ref))
+            pieces.sort(key=lambda piece: piece[0])
+            while pieces:
                 length = 1
-                while length < len(wanted) and wanted[length] == wanted[0] + length:
+                while length < len(pieces) and pieces[length][0] == sum(pieces[length - 1][:2]):
                     length += 1
-                span = pl.ds(first_row + wanted[0] * rows, length * rows)
-                lanes = pl.ds(start, tile)
+                base, end = pieces[0][0], sum(pieces[length - 1][:2])
+                span, lanes = pl.ds(base, end - base), pl.ds(start, tile)
                 total = jnp.dot(left_high[span, :], right_high[:, lanes], preferred_element_type=jnp.float32)
                 total += jnp.dot(left_high[span, :], right_low[:, lanes], preferred_element_type=jnp.float32)
                 total += jnp.dot(left_low[span, :], right_high[:, lanes], preferred_element_type=jnp.float32)
-                for at in range(length):
-                    piece = total[at * rows : (at + 1) * rows, :]
-                    out_ref[places[wanted[at]], :, pl.ds(start % width, tile)] = piece
-                wanted = wanted[length:]
-
-    if orders[0] == orders[1]:
-        run(orders[0])
+                for at, rows, place, out_ref in pieces[:length]:
+                    out_ref[place, :, pl.ds(start % width, tile)] = total[at - base : at - base + rows, :]
+                pieces = pieces[length:]
+
+    if all(orders[0] == orders[1] for _, _, orders, _ in wanted):
+        run(0)
     else:
-        for seq, order in enumerate(orders):
-            pl.when(here[2] % 2 == seq)(functools.partial(run, order))
+        for seq in range(2):
+            pl.when(here[2] % 2 == seq)(functools.partial(run, seq))
 
 
 def device_place():
@@ -139,7 +143,6 @@
     inner = plan.per_row // plan.split
     cut = BR * 3 // 4
     for part in range(plan.split):
-        base = part * plan.rows * inner * BR
         for order, row in enumerate(plan.row_sequence):
             for at in range(inner):
                 kept = (here[0] ^ row) * plan.per_row + at * plan.split
@@ -149,9 +152,9 @@
                 sign = (1 - 2 * scalar_parity(block // row_slots, here[0])).astype(jnp.float32) * scale
                 values = kept_sum(row_mixed, block % row_slots, sign, BR, tokens, 0)
                 spot = order * inner + at
-                first = base + spot * cut
+                first = plan.first_row(part, 0) + spot * cut
                 store_pieces(values[:cut], left_high, left_low, (pl.ds(first, cut), now))
-                first = base + plan.rows * inner * cut + spot * (BR - cut)
+                first = plan.first_row(part, 1) + spot * (BR - cut)
                 store_pieces(values[cut:], left_high, left_low, (pl.ds(first, BR - cut), now))
     col_slots = col_local // BC
     for col in range(plan.cols):
@@ -164,15 +167,15 @@
     @pl.when(step == pl.num_programs(0) - 1)
     def _():
         factors = (left_high, left_low, right_high, right_low)
-        first_row, orders = plan.first_product()
-        product_blocks(plan, here, factors, sent_out, first_row, orders, sent_out.shape[0])
+        orders = plan.main if plan.split == 1 else plan.main[1:] + plan.main[:1]
+        first_row = plan.first_row(plan.split - 1, 0)
+        product_blocks(plan, here, factors, [(sent_out, first_row, orders, sent_out.shape[0])])
 
 
 def product_kernel(plan, wanted, after, left_high, left_low, right_high, right_low, *outs):
     here = device_place()
     factors = (left_high, left_low, right_high, right_low)
-    for args, out in zip(wanted, outs):
-        product_blocks(plan, here, factors, out, *args)
+    product_blocks(plan, here, factors, [(out, *args) for args, out in zip(wanted, outs)])
 
 
 def add_kernel(first, second, out):
@@ -235,10 +238,12 @@
             spot = spot * 2 + int(bool((row if axis == "row" else col) & mask))
         return spot
 
-    def first_product(self):
+    def first_row(self, part, kind):
+        inner = self.per_row // self.split * self.rows
+        main, rest = inner * (BR * 3 // 4), inner * (BR - BR * 3 // 4)
         if self.split == 1:
-            return 0, self.main
-        return self.rows * self.per_row // 2 * BR, self.main[1:] + self.main[:1]
+            return (0, main)[kind]
+        return ((0, main + rest), (main + 2 * rest, main))[part][kind]
 
     def cross(self, part, orders, step):
         bits = (orders[0][step], orders[1][step])
@@ -310,8 +315,6 @@
         )(after, *factors)
 
     half = blocks // 2
-    half_rows = plan.rows * inner * BR
-    main_rows = plan.rows * inner * cut
 
     def swap(values):
         return lax.ppermute(values, "seq", [(0, 1), (1, 0)])
@@ -319,18 +322,18 @@
     if plan.split == 2:
         arrived_sent = swap(first_sent)
         sent, rest_other = products(
-            [(0, plan.main, half), (half_rows + main_rows, plan.rest, 0)], [main_shape, rest_shape], "sent_products"
+            [(0, plan.main, half), (plan.first_row(1, 1), plan.rest, 0)], [main_shape, rest_shape], "sent_products"
         )
         sent = sent + arrived_sent
         later, sent = lax.optimization_barrier((start, sent))
         after, arrived_rest = lax.optimization_barrier((later, swap(rest_other)))
-        (rest,) = products([(main_rows, plan.rest, 0)], [rest_shape], "rest_product", after)
+        (rest,) = products([(plan.first_row(0, 1), plan.rest, 0)], [rest_shape], "rest_product", after)
         rest = rest + arrived_rest
-        (kept_other,) = products([(half_rows, plan.main[1:] + plan.main[:1], 0)], [main_shape], "kept_other_product", later)
+        (kept_other,) = products([(plan.first_row(1, 0), plan.main[1:] + plan.main[:1], 0)], [main_shape], "kept_other_product", later)
         (kept,) = products([(0, plan.main, 0)], [main_shape], "kept_product", later)
         main = add_early(kept, plan.cross(sent, plan.main, 0)) + swap(kept_other)
     else:
-        (rest,) = products([(main_rows, plan.rest, 0)], [rest_shape], "rest_product")
+        (rest,) = products([(plan.first_row(0, 1), plan.rest, 0)], [rest_shape], "rest_product")
         (kept,) = products([(0, plan.main, 0)], [main_shape], "kept_product")
         main = kept + plan.cross(first_sent, plan.main, 0)
     steps = len(plan.main[0])

time: 54.1 us -> 53.9 us (level)
  transfers between devices with their start and end apart: 11 -> 11, of which waited for: 7 -> 7; matrix products, arithmetic and copies ran while one was open for 1% -> 1% of each run, Pallas kernels for 12% -> 11%
where the time goes in v7:
time: 53.9 us; the launch traced here: 53.8 us
  Pallas kernels  20 us (37%)
  waiting for transfers between devices  17.5 us (32%)
  starting transfers between devices  14.7 us (27%)
  other arithmetic  1.29 us (2%)
    ppermute x7, waiting for transfers between devices, cross(): return lax.ppermute(part, ('row', 'col', 'seq'), self.pairs(bits))  16.2 us
    pallas_call x1, Pallas kernels, body(): pl.pallas_call(functools.partial(mix_kernel, plan, scale), grid=(tokens /...  14 us
    ppermute x7, starting transfers between devices, cross(): return lax.ppermute(part, ('row', 'col', 'seq'), self.pairs(bits))  13.9 us
    pallas_call x4, Pallas kernels, products(): pl.pallas_call(functools.partial(product_kernel, plan, wanted), in_specs=...  5.97 us
    ppermute x4, waiting for transfers between devices, swap(): return lax.ppermute(values, 'seq', [(0, 1), (1, 0)])  1.33 us
  transfers between devices with their start and end apart: 11, of which 7 were waited for; matrix products, arithmetic and copies ran while one was open for 1% of the time, Pallas kernels for 11%

profile of v7, /device:TPU:0, one launch (start us, length us, event | category | flops | bytes accessed | tf_op | source)
XLA Modules:
  0.0 53.8 jit_solution(11202998960830536119)
XLA Ops:
  0.0 14.0 %mix.1 = (f32[8,48,512]{2,1,0:T(8,128)S(1)}, bf16[1024,1024]{1,0:T(8,128)(2,1)S(1)}, bf16[1024,1024]{1,0:T(8,128)(2,1)S(1)}, bf16[1024,1024]{1,0:T(8,128)(2,1)S(1)}, bf16[1024,1024]{1,0:T(8,128)(2,1)S(1)}) custom-call(s32[16]{0:T(128)} %row_blocks.1, s32[8]{0:T(128)} %col_blocks.1, bf16[1024,4096]{1,0:T(8,128)(2,1)} %bitcast.14, ...), custom_call_target="tpu_custom_call" | custom-call | tf_op jit(solution)/shard_map/mix/pallas_call | solution.py:273
  14.0 0.5 collective-permute-start
  14.5 2.2 %sent_products.1 = (f32[8,48,512]{2,1,0:T(8,128)S(1)}, f32[16,16,512]{2,1,0:T(8,128)S(1)}) custom-call(f32[8,128]{1,0:T(8,128)S(1)} %broadcast_in_dim.9.after, bf16[1024,1024]{1,0:T(8,128)(2,1)S(1)} %get-tuple-element.20.left_high, bf16[1024,1024]{1,0:T(8,128)(2,1)S(1)} %get-tuple-element.21.left_low, bf16[1024,1024]{1,0:T(8,128)(2,1)S(1)} %get-tuple-element.22.right_high, ...), custom_call_target="tpu_custom_call" | custom-call | tf_op jit(solution)/shard_map/sent_products/pallas_call | solution.py:308
  16.7 0.0 collective-permute-done
  16.7 0.1 add.27
  16.8 2.7 %collective-permute-start.1 = (f32[8,48,512]{2,1,0:T(8,128)S(1)}, f32[8,48,512]{2,1,0:T(8,128)S(1)}, u32[]{:S(2)}, u32[]{:S(2)}) collective-permute-start(f32[8,48,512]{2,1,0:T(8,128)S(1)} %add.27), channel_id=1, source_target_pairs={{0,2},{1,5},{2,0},{3,7},{4,6},{5,1},{6,4},{7,3},{8,10},{9,13},{10,... | collective-permute-start | bytes 2359304 | tf_op jit(solution)/shard_map/ppermute | solution.py:250
  19.5 0.1 collective-permute-start.4
  19.6 1.4 %kept_other_product.1 = f32[8,48,512]{2,1,0:T(8,128)S(1)} custom-call(f32[8,128]{1,0:T(8,128)S(1)} %broadcast_in_dim.9.after, bf16[1024,1024]{1,0:T(8,128)(2,1)S(1)} %get-tuple-element.20.left_high, bf16[1024,1024]{1,0:T(8,128)(2,1)S(1)} %get-tuple-element.21.left_low, bf16[1024,1024]{1,0:T(8,128)(2,1)S(1)} %get-tuple-element.22.right_high, ...), custom_call_target="tpu_custom_call" | custom-call | tf_op jit(solution)/shard_map/kept_other_product/pallas_call | solution.py:308
  21.0 1.4 %kept_product.1.first = f32[8,48,512]{2,1,0:T(8,128)S(1)} custom-call(f32[8,128]{1,0:T(8,128)S(1)} %broadcast_in_dim.9.after, bf16[1024,1024]{1,0:T(8,128)(2,1)S(1)} %get-tuple-element.20.left_high, bf16[1024,1024]{1,0:T(8,128)(2,1)S(1)} %get-tuple-element.21.left_low, bf16[1024,1024]{1,0:T(8,128)(2,1)S(1)} %get-tuple-element.22.right_high, ...), custom_call_target="tpu_custom_call" | custom-call | tf_op jit(solution)/shard_map/kept_product/pallas_call | solution.py:308
  22.4 0.0 collective-permute-done.4
  22.4 1.0 %rest_product.1 = f32[16,16,512]{2,1,0:T(8,128)S(1)} custom-call(f32[8,128]{1,0:T(8,128)S(1)} %broadcast_in_dim.9.after, bf16[1024,1024]{1,0:T(8,128)(2,1)S(1)} %get-tuple-element.20.left_high, bf16[1024,1024]{1,0:T(8,128)(2,1)S(1)} %get-tuple-element.21.left_low, bf16[1024,1024]{1,0:T(8,128)(2,1)S(1)} %get-tuple-element.22.right_high, ...), custom_call_target="tpu_custom_call" | custom-call | tf_op jit(solution)/shard_map/rest_product/pallas_call | solution.py:308
  23.4 0.1 add.30
  23.5 1.7 %collective-permute-start.5 = (f32[8,16,512]{2,1,0:T(8,128)S(1)}, f32[8,16,512]{2,1,0:T(8,128)S(1)}, u32[]{:S(2)}, u32[]{:S(2)}) collective-permute-start(f32[8,16,512]{2,1,0:T(8,128)S(1)} %slice.69), channel_id=1, source_target_pairs={{0,8},{1,9},{2,10},{3,11},{4,12},{5,13},{6,14},{7,15},{8,0},{9,1},... | collective-permute-start | bytes 786440 | tf_op jit(solution)/shard_map/ppermute | solution.py:250
  25.2 0.1 collective-permute-start.2
  25.3 4.2 %collective-permute-done.1.second = f32[8,48,512]{2,1,0:T(8,128)S(1)} collective-permute-done((f32[8,48,512]{2,1,0:T(8,128)S(1)}, f32[8,48,512]{2,1,0:T(8,128)S(1)}, u32[]{:S(2)}, u32[]{:S(2)}) %collective-permute-start.1) | collective-permute-done | bytes 786464 | tf_op jit(solution)/shard_map/ppermute | solution.py:250
  29.5 0.1 add_early.1
  29.6 0.0 collective-permute-done.2
  29.6 0.1 add.28
  29.8 2.0 %collective-permute-start.3 = (f32[4,48,512]{2,1,0:T(8,128)S(1)}, f32[4,48,512]{2,1,0:T(8,128)S(1)}, u32[]{:S(2)}, u32[]{:S(2)}) collective-permute-start(f32[4,48,512]{2,1,0:T(8,128)S(1)} %slice.67), channel_id=1, source_target_pairs={{0,4},{1,9},{2,6},{3,11},{4,0},{5,13},{6,2},{7,15},{8,12},{9,1},{1... | collective-permute-start | bytes 1179656 | tf_op jit(solution)/shard_map/ppermute | solution.py:250
  31.8 0.4 collective-permute-done.5
  32.3 1.2 %collective-permute-start.6 = (f32[4,16,512]{2,1,0:T(8,128)S(1)}, f32[4,16,512]{2,1,0:T(8,128)S(1)}, u32[]{:S(2)}, u32[]{:S(2)}) collective-permute-start(f32[4,16,512]{2,1,0:T(8,128)S(1)} %slice.70), channel_id=1, source_target_pairs={{0,2},{1,3},{2,0},{3,1},{4,6},{5,7},{6,4},{7,5},{8,10},{9,11},{10,... | collective-permute-start | bytes 393224 | tf_op jit(solution)/shard_map/ppermute | solution.py:250
  33.4 4.1 %collective-permute-done.3 = f32[4,48,512]{2,1,0:T(8,128)S(1)} collective-permute-done((f32[4,48,512]{2,1,0:T(8,128)S(1)}, f32[4,48,512]{2,1,0:T(8,128)S(1)}, u32[]{:S(2)}, u32[]{:S(2)}) %collective-permute-start.3) | collective-permute-done | bytes 393248 | tf_op jit(solution)/shard_map/ppermute | solution.py:250
  37.6 0.1 slice_add_fusion
  37.7 2.1 %collective-permute-start.7 = (f32[2,48,512]{2,1,0:T(8,128)S(1)}, f32[2,48,512]{2,1,0:T(8,128)S(1)}, u32[]{:S(2)}, u32[]{:S(2)}) collective-permute-start(f32[2,48,512]{2,1,0:T(8,128)S(1)} %slice.56), channel_id=1, source_target_pairs={{0,8},{1,3},{2,10},{3,1},{4,12},{5,7},{6,14},{7,5},{8,0},{9,11},{1... | collective-permute-start | bytes 589832 | tf_op jit(solution)/shard_map/ppermute | solution.py:250
  39.9 1.5 %collective-permute-start.8 = (f32[2,16,512]{2,1,0:T(8,128)S(1)}, f32[2,16,512]{2,1,0:T(8,128)S(1)}, u32[]{:S(2)}, u32[]{:S(2)}) collective-permute-start(f32[2,16,512]{2,1,0:T(8,128)S(1)} %slice.72), channel_id=1, source_target_pairs={{0,4},{1,5},{2,6},{3,7},{4,0},{5,1},{6,2},{7,3},{8,12},{9,13},{10,... | collective-permute-start | bytes 196616 | tf_op jit(solution)/shard_map/ppermute | solution.py:250
  41.4 2.1 %collective-permute-done.7 = f32[2,48,512]{2,1,0:T(8,128)S(1)} collective-permute-done((f32[2,48,512]{2,1,0:T(8,128)S(1)}, f32[2,48,512]{2,1,0:T(8,128)S(1)}, u32[]{:S(2)}, u32[]{:S(2)}) %collective-permute-start.7) | collective-permute-done | bytes 196640 | tf_op jit(solution)/shard_map/ppermute | solution.py:250
  43.5 0.7 %collective-permute-done.8 = f32[2,16,512]{2,1,0:T(8,128)S(1)} collective-permute-done((f32[2,16,512]{2,1,0:T(8,128)S(1)}, f32[2,16,512]{2,1,0:T(8,128)S(1)}, u32[]{:S(2)}, u32[]{:S(2)}) %collective-permute-start.8) | collective-permute-done | bytes 65568 | tf_op jit(solution)/shard_map/ppermute | solution.py:250
  44.2 2.6 %collective-permute-start.9 = (f32[1,64,512]{2,1,0:T(8,128)S(1)}, f32[1,64,512]{2,1,0:T(8,128)S(1)}, u32[]{:S(2)}, u32[]{:S(2)}) collective-permute-start(f32[1,64,512]{2,1,0:T(8,128)S(1)} %pad_maximum_fusion.1), channel_id=1, source_target_pairs={{0,16},{1,17},{2,18},{3,19},{4,20},{5,21},{6,22},{7,23},{8,24},{9,... | collective-permute-start | bytes 393224 | tf_op jit(solution)/shard_map/ppermute | solution.py:250
  46.9 4.7 %collective-permute-done.9 = f32[1,64,512]{2,1,0:T(8,128)S(1)} collective-permute-done((f32[1,64,512]{2,1,0:T(8,128)S(1)}, f32[1,64,512]{2,1,0:T(8,128)S(1)}, u32[]{:S(2)}, u32[]{:S(2)}) %collective-permute-start.9) | collective-permute-done | bytes 131104 | tf_op jit(solution)/shard_map/ppermute | solution.py:250
  51.6 0.1 collective-permute-start.10
  51.7 1.3 %collective-permute-done.10 = f32[64,512]{1,0:T(8,128)S(1)} collective-permute-done((f32[64,512]{1,0:T(8,128)S(1)}, f32[64,512]{1,0:T(8,128)S(1)}, u32[]{:S(2)}, u32[]{:S(2)}) %collective-permute-start.10) | collective-permute-done | bytes 131104 | tf_op jit(solution)/shard_map/ppermute | solution.py:320
  53.1 0.7 %pad_maximum_fusion = f32[1,2,64,512]{3,2,1,0:T(8,128)} fusion(f32[1,1,64,512]{3,2,1,0:T(8,128)S(1)} %get-tuple-element.36, f32[1,1,64,512]{3,2,1,0:T(8,128)S(1)} %get-tuple-element.35), kind=kLoop, calls=%fused_computation.4 | loop fusion | flops 65536 | bytes 524288 | tf_op jit(solution)/shard_map/stack | solution.py:356
  (18 shorter events, 0.3 us)
Async XLA Ops:
  14.0 2.7 %collective-permute-start = (f32[8,48,512]{2,1,0:T(8,128)S(1)}, f32[8,48,512]{2,1,0:T(8,128)S(1)}, u32[]{:S(2)}, u32[]{:S(2)}) collective-permute-start(f32[8,48,512]{2,1,0:T(8,128)S(1)} %get-tuple-element.25), channel_id=1, source_target_pairs={{0,1},{1,0},{2,3},{3,2},{4,5},{5,4},{6,7},{7,6},{8,9},{9,8},{10,11... | collective-permute-start | bytes 2359304 | tf_op jit(solution)/shard_map/ppermute | solution.py:320
  16.8 12.6 %collective-permute-start.1 = (f32[8,48,512]{2,1,0:T(8,128)S(1)}, f32[8,48,512]{2,1,0:T(8,128)S(1)}, u32[]{:S(2)}, u32[]{:S(2)}) collective-permute-start(f32[8,48,512]{2,1,0:T(8,128)S(1)} %add.27), channel_id=1, source_target_pairs={{0,2},{1,5},{2,0},{3,7},{4,6},{5,1},{6,4},{7,3},{8,10},{9,13},{10,... | collective-permute-start | bytes 2359304 | tf_op jit(solution)/shard_map/ppermute | solution.py:250
  19.5 2.9 %collective-permute-start.4 = (f32[16,16,512]{2,1,0:T(8,128)S(1)}, f32[16,16,512]{2,1,0:T(8,128)S(1)}, u32[]{:S(2)}, u32[]{:S(2)}) collective-permute-start(f32[16,16,512]{2,1,0:T(8,128)S(1)} %get-tuple-element.28), channel_id=1, source_target_pairs={{0,1},{1,0},{2,3},{3,2},{4,5},{5,4},{6,7},{7,6},{8,9},{9,8},{10,11... | collective-permute-start | bytes 1572872 | tf_op jit(solution)/shard_map/ppermute | solution.py:320
  23.5 8.7 %collective-permute-start.5 = (f32[8,16,512]{2,1,0:T(8,128)S(1)}, f32[8,16,512]{2,1,0:T(8,128)S(1)}, u32[]{:S(2)}, u32[]{:S(2)}) collective-permute-start(f32[8,16,512]{2,1,0:T(8,128)S(1)} %slice.69), channel_id=1, source_target_pairs={{0,8},{1,9},{2,10},{3,11},{4,12},{5,13},{6,14},{7,15},{8,0},{9,1},... | collective-permute-start | bytes 786440 | tf_op jit(solution)/shard_map/ppermute | solution.py:250
  25.2 4.4 %collective-permute-start.2 = (f32[8,48,512]{2,1,0:T(8,128)S(1)}, f32[8,48,512]{2,1,0:T(8,128)S(1)}, u32[]{:S(2)}, u32[]{:S(2)}) collective-permute-start(f32[8,48,512]{2,1,0:T(8,128)S(1)} %kept_other_product.1), channel_id=1, source_target_pairs={{0,1},{1,0},{2,3},{3,2},{4,5},{5,4},{6,7},{7,6},{8,9},{9,8},{10,11... | collective-permute-start | bytes 2359304 | tf_op jit(solution)/shard_map/ppermute | solution.py:320
  29.8 7.8 %collective-permute-start.3 = (f32[4,48,512]{2,1,0:T(8,128)S(1)}, f32[4,48,512]{2,1,0:T(8,128)S(1)}, u32[]{:S(2)}, u32[]{:S(2)}) collective-permute-start(f32[4,48,512]{2,1,0:T(8,128)S(1)} %slice.67), channel_id=1, source_target_pairs={{0,4},{1,9},{2,6},{3,11},{4,0},{5,13},{6,2},{7,15},{8,12},{9,1},{1... | collective-permute-start | bytes 1179656 | tf_op jit(solution)/shard_map/ppermute | solution.py:250
  32.3 5.4 %collective-permute-start.6 = (f32[4,16,512]{2,1,0:T(8,128)S(1)}, f32[4,16,512]{2,1,0:T(8,128)S(1)}, u32[]{:S(2)}, u32[]{:S(2)}) collective-permute-start(f32[4,16,512]{2,1,0:T(8,128)S(1)} %slice.70), channel_id=1, source_target_pairs={{0,2},{1,3},{2,0},{3,1},{4,6},{5,7},{6,4},{7,5},{8,10},{9,11},{10,... | collective-permute-start | bytes 393224 | tf_op jit(solution)/shard_map/ppermute | solution.py:250
  37.7 5.8 %collective-permute-start.7 = (f32[2,48,512]{2,1,0:T(8,128)S(1)}, f32[2,48,512]{2,1,0:T(8,128)S(1)}, u32[]{:S(2)}, u32[]{:S(2)}) collective-permute-start(f32[2,48,512]{2,1,0:T(8,128)S(1)} %slice.56), channel_id=1, source_target_pairs={{0,8},{1,3},{2,10},{3,1},{4,12},{5,7},{6,14},{7,5},{8,0},{9,11},{1... | collective-permute-start | bytes 589832 | tf_op jit(solution)/shard_map/ppermute | solution.py:250
  39.9 4.3 %collective-permute-start.8 = (f32[2,16,512]{2,1,0:T(8,128)S(1)}, f32[2,16,512]{2,1,0:T(8,128)S(1)}, u32[]{:S(2)}, u32[]{:S(2)}) collective-permute-start(f32[2,16,512]{2,1,0:T(8,128)S(1)} %slice.72), channel_id=1, source_target_pairs={{0,4},{1,5},{2,6},{3,7},{4,0},{5,1},{6,2},{7,3},{8,12},{9,13},{10,... | collective-permute-start | bytes 196616 | tf_op jit(solution)/shard_map/ppermute | solution.py:250
  44.2 7.3 %collective-permute-start.9 = (f32[1,64,512]{2,1,0:T(8,128)S(1)}, f32[1,64,512]{2,1,0:T(8,128)S(1)}, u32[]{:S(2)}, u32[]{:S(2)}) collective-permute-start(f32[1,64,512]{2,1,0:T(8,128)S(1)} %pad_maximum_fusion.1), channel_id=1, source_target_pairs={{0,16},{1,17},{2,18},{3,19},{4,20},{5,21},{6,22},{7,23},{8,24},{9,... | collective-permute-start | bytes 393224 | tf_op jit(solution)/shard_map/ppermute | solution.py:250
  51.6 1.4 %collective-permute-start.10 = (f32[64,512]{1,0:T(8,128)S(1)}, f32[64,512]{1,0:T(8,128)S(1)}, u32[]{:S(2)}, u32[]{:S(2)}) collective-permute-start(f32[64,512]{1,0:T(8,128)S(1)} %bitcast.16), channel_id=1, source_target_pairs={{0,1},{1,0},{2,3},{3,2},{4,5},{5,4},{6,7},{7,6},{8,9},{9,8},{10,11... | collective-permute-start | bytes 393224 | tf_op jit(solution)/shard_map/ppermute | solution.py:320

commit v8 on v7

--- a/solution.py
+++ b/solution.py
@@ -15,6 +15,7 @@
 TILE = 256
 MIX_VMEM = 30 << 20
 PRODUCT_VMEM = 16 << 20
+PRODUCT_TILE = 512
 AHEAD = 20 * 10**9
 
 
@@ -63,7 +64,7 @@
 def product_blocks(plan, here, factors, wanted):
     left_high, left_low, right_high, right_low = factors
     width = wanted[0][0].shape[2]
-    tile = min(CHUNK, width)
+    tile = min(PRODUCT_TILE, width)
 
     def run(seq):
         for start in range(0, plan.cols * width, tile):

time: 53.9 us -> 54 us (level)
  no operation moved by 1% of the time
where the time goes in v8:
time: 54 us; the launch traced here: 53.8 us
  Pallas kernels  20.1 us (37%)
  waiting for transfers between devices  17.4 us (32%)
  starting transfers between devices  14.7 us (27%)
  other arithmetic  1.29 us (2%)
    ppermute x7, waiting for transfers between devices, cross(): return lax.ppermute(part, ('row', 'col', 'seq'), self.pairs(bits))  16.1 us
    pallas_call x1, Pallas kernels, body(): pl.pallas_call(functools.partial(mix_kernel, plan, scale), grid=(tokens /...  14 us
    ppermute x7, starting transfers between devices, cross(): return lax.ppermute(part, ('row', 'col', 'seq'), self.pairs(bits))  14 us
    pallas_call x4, Pallas kernels, products(): pl.pallas_call(functools.partial(product_kernel, plan, wanted), in_specs=...  5.97 us
    ppermute x4, waiting for transfers between devices, swap(): return lax.ppermute(values, 'seq', [(0, 1), (1, 0)])  1.33 us
  transfers between devices with their start and end apart: 11, of which 7 were waited for; matrix products, arithmetic and copies ran while one was open for 1% of the time, Pallas kernels for 11%

profile of v8, /device:TPU:0, one launch (start us, length us, event | category | flops | bytes accessed | tf_op | source)
XLA Modules:
  0.0 53.8 jit_solution(17390874674313512002)
XLA Ops:
  0.0 14.0 %mix.1 = (f32[8,48,512]{2,1,0:T(8,128)S(1)}, bf16[1024,1024]{1,0:T(8,128)(2,1)S(1)}, bf16[1024,1024]{1,0:T(8,128)(2,1)S(1)}, bf16[1024,1024]{1,0:T(8,128)(2,1)S(1)}, bf16[1024,1024]{1,0:T(8,128)(2,1)S(1)}) custom-call(s32[16]{0:T(128)} %row_blocks.1, s32[8]{0:T(128)} %col_blocks.1, bf16[1024,4096]{1,0:T(8,128)(2,1)} %bitcast.14, ...), custom_call_target="tpu_custom_call" | custom-call | tf_op jit(solution)/shard_map/mix/pallas_call | solution.py:274
  14.0 0.5 collective-permute-start
  14.5 2.2 %sent_products.1 = (f32[8,48,512]{2,1,0:T(8,128)S(1)}, f32[16,16,512]{2,1,0:T(8,128)S(1)}) custom-call(f32[8,128]{1,0:T(8,128)S(1)} %broadcast_in_dim.9.after, bf16[1024,1024]{1,0:T(8,128)(2,1)S(1)} %get-tuple-element.20.left_high, bf16[1024,1024]{1,0:T(8,128)(2,1)S(1)} %get-tuple-element.21.left_low, bf16[1024,1024]{1,0:T(8,128)(2,1)S(1)} %get-tuple-element.22.right_high, ...), custom_call_target="tpu_custom_call" | custom-call | tf_op jit(solution)/shard_map/sent_products/pallas_call | solution.py:309
  16.7 0.0 collective-permute-done
  16.7 0.1 add.27
  16.9 2.6 %collective-permute-start.1 = (f32[8,48,512]{2,1,0:T(8,128)S(1)}, f32[8,48,512]{2,1,0:T(8,128)S(1)}, u32[]{:S(2)}, u32[]{:S(2)}) collective-permute-start(f32[8,48,512]{2,1,0:T(8,128)S(1)} %add.27), channel_id=1, source_target_pairs={{0,2},{1,5},{2,0},{3,7},{4,6},{5,1},{6,4},{7,3},{8,10},{9,13},{10,... | collective-permute-start | bytes 2359304 | tf_op jit(solution)/shard_map/ppermute | solution.py:251
  19.5 0.2 collective-permute-start.4
  19.7 1.4 %kept_other_product.1 = f32[8,48,512]{2,1,0:T(8,128)S(1)} custom-call(f32[8,128]{1,0:T(8,128)S(1)} %broadcast_in_dim.9.after, bf16[1024,1024]{1,0:T(8,128)(2,1)S(1)} %get-tuple-element.20.left_high, bf16[1024,1024]{1,0:T(8,128)(2,1)S(1)} %get-tuple-element.21.left_low, bf16[1024,1024]{1,0:T(8,128)(2,1)S(1)} %get-tuple-element.22.right_high, ...), custom_call_target="tpu_custom_call" | custom-call | tf_op jit(solution)/shard_map/kept_other_product/pallas_call | solution.py:309
  21.1 1.4 %kept_product.1.first = f32[8,48,512]{2,1,0:T(8,128)S(1)} custom-call(f32[8,128]{1,0:T(8,128)S(1)} %broadcast_in_dim.9.after, bf16[1024,1024]{1,0:T(8,128)(2,1)S(1)} %get-tuple-element.20.left_high, bf16[1024,1024]{1,0:T(8,128)(2,1)S(1)} %get-tuple-element.21.left_low, bf16[1024,1024]{1,0:T(8,128)(2,1)S(1)} %get-tuple-element.22.right_high, ...), custom_call_target="tpu_custom_call" | custom-call | tf_op jit(solution)/shard_map/kept_product/pallas_call | solution.py:309
  22.5 0.0 collective-permute-done.4
  22.5 1.0 %rest_product.1 = f32[16,16,512]{2,1,0:T(8,128)S(1)} custom-call(f32[8,128]{1,0:T(8,128)S(1)} %broadcast_in_dim.9.after, bf16[1024,1024]{1,0:T(8,128)(2,1)S(1)} %get-tuple-element.20.left_high, bf16[1024,1024]{1,0:T(8,128)(2,1)S(1)} %get-tuple-element.21.left_low, bf16[1024,1024]{1,0:T(8,128)(2,1)S(1)} %get-tuple-element.22.right_high, ...), custom_call_target="tpu_custom_call" | custom-call | tf_op jit(solution)/shard_map/rest_product/pallas_call | solution.py:309
  23.5 0.1 add.30
  23.6 1.7 %collective-permute-start.5 = (f32[8,16,512]{2,1,0:T(8,128)S(1)}, f32[8,16,512]{2,1,0:T(8,128)S(1)}, u32[]{:S(2)}, u32[]{:S(2)}) collective-permute-start(f32[8,16,512]{2,1,0:T(8,128)S(1)} %slice.69), channel_id=1, source_target_pairs={{0,8},{1,9},{2,10},{3,11},{4,12},{5,13},{6,14},{7,15},{8,0},{9,1},... | collective-permute-start | bytes 786440 | tf_op jit(solution)/shard_map/ppermute | solution.py:251
  25.3 0.0 collective-permute-start.2
  25.3 4.2 %collective-permute-done.1.second = f32[8,48,512]{2,1,0:T(8,128)S(1)} collective-permute-done((f32[8,48,512]{2,1,0:T(8,128)S(1)}, f32[8,48,512]{2,1,0:T(8,128)S(1)}, u32[]{:S(2)}, u32[]{:S(2)}) %collective-permute-start.1) | collective-permute-done | bytes 786464 | tf_op jit(solution)/shard_map/ppermute | solution.py:251
  29.5 0.1 add_early.1
  29.6 0.0 collective-permute-done.2
  29.6 0.1 add.28
  29.8 2.1 %collective-permute-start.3 = (f32[4,48,512]{2,1,0:T(8,128)S(1)}, f32[4,48,512]{2,1,0:T(8,128)S(1)}, u32[]{:S(2)}, u32[]{:S(2)}) collective-permute-start(f32[4,48,512]{2,1,0:T(8,128)S(1)} %slice.67), channel_id=1, source_target_pairs={{0,4},{1,9},{2,6},{3,11},{4,0},{5,13},{6,2},{7,15},{8,12},{9,1},{1... | collective-permute-start | bytes 1179656 | tf_op jit(solution)/shard_map/ppermute | solution.py:251
  31.9 0.4 collective-permute-done.5
  32.3 1.2 %collective-permute-start.6 = (f32[4,16,512]{2,1,0:T(8,128)S(1)}, f32[4,16,512]{2,1,0:T(8,128)S(1)}, u32[]{:S(2)}, u32[]{:S(2)}) collective-permute-start(f32[4,16,512]{2,1,0:T(8,128)S(1)} %slice.70), channel_id=1, source_target_pairs={{0,2},{1,3},{2,0},{3,1},{4,6},{5,7},{6,4},{7,5},{8,10},{9,11},{10,... | collective-permute-start | bytes 393224 | tf_op jit(solution)/shard_map/ppermute | solution.py:251
  33.5 4.1 %collective-permute-done.3 = f32[4,48,512]{2,1,0:T(8,128)S(1)} collective-permute-done((f32[4,48,512]{2,1,0:T(8,128)S(1)}, f32[4,48,512]{2,1,0:T(8,128)S(1)}, u32[]{:S(2)}, u32[]{:S(2)}) %collective-permute-start.3) | collective-permute-done | bytes 393248 | tf_op jit(solution)/shard_map/ppermute | solution.py:251
  37.6 0.1 slice_add_fusion
  37.7 2.2 %collective-permute-start.7 = (f32[2,48,512]{2,1,0:T(8,128)S(1)}, f32[2,48,512]{2,1,0:T(8,128)S(1)}, u32[]{:S(2)}, u32[]{:S(2)}) collective-permute-start(f32[2,48,512]{2,1,0:T(8,128)S(1)} %slice.56), channel_id=1, source_target_pairs={{0,8},{1,3},{2,10},{3,1},{4,12},{5,7},{6,14},{7,5},{8,0},{9,11},{1... | collective-permute-start | bytes 589832 | tf_op jit(solution)/shard_map/ppermute | solution.py:251
  39.9 1.6 %collective-permute-start.8 = (f32[2,16,512]{2,1,0:T(8,128)S(1)}, f32[2,16,512]{2,1,0:T(8,128)S(1)}, u32[]{:S(2)}, u32[]{:S(2)}) collective-permute-start(f32[2,16,512]{2,1,0:T(8,128)S(1)} %slice.72), channel_id=1, source_target_pairs={{0,4},{1,5},{2,6},{3,7},{4,0},{5,1},{6,2},{7,3},{8,12},{9,13},{10,... | collective-permute-start | bytes 196616 | tf_op jit(solution)/shard_map/ppermute | solution.py:251
  41.5 2.1 %collective-permute-done.7 = f32[2,48,512]{2,1,0:T(8,128)S(1)} collective-permute-done((f32[2,48,512]{2,1,0:T(8,128)S(1)}, f32[2,48,512]{2,1,0:T(8,128)S(1)}, u32[]{:S(2)}, u32[]{:S(2)}) %collective-permute-start.7) | collective-permute-done | bytes 196640 | tf_op jit(solution)/shard_map/ppermute | solution.py:251
  43.6 0.7 %collective-permute-done.8 = f32[2,16,512]{2,1,0:T(8,128)S(1)} collective-permute-done((f32[2,16,512]{2,1,0:T(8,128)S(1)}, f32[2,16,512]{2,1,0:T(8,128)S(1)}, u32[]{:S(2)}, u32[]{:S(2)}) %collective-permute-start.8) | collective-permute-done | bytes 65568 | tf_op jit(solution)/shard_map/ppermute | solution.py:251
  44.3 2.7 %collective-permute-start.9 = (f32[1,64,512]{2,1,0:T(8,128)S(1)}, f32[1,64,512]{2,1,0:T(8,128)S(1)}, u32[]{:S(2)}, u32[]{:S(2)}) collective-permute-start(f32[1,64,512]{2,1,0:T(8,128)S(1)} %pad_maximum_fusion.1), channel_id=1, source_target_pairs={{0,16},{1,17},{2,18},{3,19},{4,20},{5,21},{6,22},{7,23},{8,24},{9,... | collective-permute-start | bytes 393224 | tf_op jit(solution)/shard_map/ppermute | solution.py:251
  46.9 4.7 %collective-permute-done.9 = f32[1,64,512]{2,1,0:T(8,128)S(1)} collective-permute-done((f32[1,64,512]{2,1,0:T(8,128)S(1)}, f32[1,64,512]{2,1,0:T(8,128)S(1)}, u32[]{:S(2)}, u32[]{:S(2)}) %collective-permute-start.9) | collective-permute-done | bytes 131104 | tf_op jit(solution)/shard_map/ppermute | solution.py:251
  51.7 0.1 collective-permute-start.10
  51.8 1.3 %collective-permute-done.10 = f32[64,512]{1,0:T(8,128)S(1)} collective-permute-done((f32[64,512]{1,0:T(8,128)S(1)}, f32[64,512]{1,0:T(8,128)S(1)}, u32[]{:S(2)}, u32[]{:S(2)}) %collective-permute-start.10) | collective-permute-done | bytes 131104 | tf_op jit(solution)/shard_map/ppermute | solution.py:321
  53.1 0.7 %pad_maximum_fusion = f32[1,2,64,512]{3,2,1,0:T(8,128)} fusion(f32[1,1,64,512]{3,2,1,0:T(8,128)S(1)} %get-tuple-element.36, f32[1,1,64,512]{3,2,1,0:T(8,128)S(1)} %get-tuple-element.35), kind=kLoop, calls=%fused_computation.4 | loop fusion | flops 65536 | bytes 524288 | tf_op jit(solution)/shard_map/stack | solution.py:357
  (18 shorter events, 0.3 us)
Async XLA Ops:
  14.0 2.7 %collective-permute-start = (f32[8,48,512]{2,1,0:T(8,128)S(1)}, f32[8,48,512]{2,1,0:T(8,128)S(1)}, u32[]{:S(2)}, u32[]{:S(2)}) collective-permute-start(f32[8,48,512]{2,1,0:T(8,128)S(1)} %get-tuple-element.25), channel_id=1, source_target_pairs={{0,1},{1,0},{2,3},{3,2},{4,5},{5,4},{6,7},{7,6},{8,9},{9,8},{10,11... | collective-permute-start | bytes 2359304 | tf_op jit(solution)/shard_map/ppermute | solution.py:321
  16.9 12.6 %collective-permute-start.1 = (f32[8,48,512]{2,1,0:T(8,128)S(1)}, f32[8,48,512]{2,1,0:T(8,128)S(1)}, u32[]{:S(2)}, u32[]{:S(2)}) collective-permute-start(f32[8,48,512]{2,1,0:T(8,128)S(1)} %add.27), channel_id=1, source_target_pairs={{0,2},{1,5},{2,0},{3,7},{4,6},{5,1},{6,4},{7,3},{8,10},{9,13},{10,... | collective-permute-start | bytes 2359304 | tf_op jit(solution)/shard_map/ppermute | solution.py:251
  19.5 3.0 %collective-permute-start.4 = (f32[16,16,512]{2,1,0:T(8,128)S(1)}, f32[16,16,512]{2,1,0:T(8,128)S(1)}, u32[]{:S(2)}, u32[]{:S(2)}) collective-permute-start(f32[16,16,512]{2,1,0:T(8,128)S(1)} %get-tuple-element.28), channel_id=1, source_target_pairs={{0,1},{1,0},{2,3},{3,2},{4,5},{5,4},{6,7},{7,6},{8,9},{9,8},{10,11... | collective-permute-start | bytes 1572872 | tf_op jit(solution)/shard_map/ppermute | solution.py:321
  23.6 8.6 %collective-permute-start.5 = (f32[8,16,512]{2,1,0:T(8,128)S(1)}, f32[8,16,512]{2,1,0:T(8,128)S(1)}, u32[]{:S(2)}, u32[]{:S(2)}) collective-permute-start(f32[8,16,512]{2,1,0:T(8,128)S(1)} %slice.69), channel_id=1, source_target_pairs={{0,8},{1,9},{2,10},{3,11},{4,12},{5,13},{6,14},{7,15},{8,0},{9,1},... | collective-permute-start | bytes 786440 | tf_op jit(solution)/shard_map/ppermute | solution.py:251
  25.3 4.3 %collective-permute-start.2 = (f32[8,48,512]{2,1,0:T(8,128)S(1)}, f32[8,48,512]{2,1,0:T(8,128)S(1)}, u32[]{:S(2)}, u32[]{:S(2)}) collective-permute-start(f32[8,48,512]{2,1,0:T(8,128)S(1)} %kept_other_product.1), channel_id=1, source_target_pairs={{0,1},{1,0},{2,3},{3,2},{4,5},{5,4},{6,7},{7,6},{8,9},{9,8},{10,11... | collective-permute-start | bytes 2359304 | tf_op jit(solution)/shard_map/ppermute | solution.py:321
  29.8 7.8 %collective-permute-start.3 = (f32[4,48,512]{2,1,0:T(8,128)S(1)}, f32[4,48,512]{2,1,0:T(8,128)S(1)}, u32[]{:S(2)}, u32[]{:S(2)}) collective-permute-start(f32[4,48,512]{2,1,0:T(8,128)S(1)} %slice.67), channel_id=1, source_target_pairs={{0,4},{1,9},{2,6},{3,11},{4,0},{5,13},{6,2},{7,15},{8,12},{9,1},{1... | collective-permute-start | bytes 1179656 | tf_op jit(solution)/shard_map/ppermute | solution.py:251
  32.3 5.4 %collective-permute-start.6 = (f32[4,16,512]{2,1,0:T(8,128)S(1)}, f32[4,16,512]{2,1,0:T(8,128)S(1)}, u32[]{:S(2)}, u32[]{:S(2)}) collective-permute-start(f32[4,16,512]{2,1,0:T(8,128)S(1)} %slice.70), channel_id=1, source_target_pairs={{0,2},{1,3},{2,0},{3,1},{4,6},{5,7},{6,4},{7,5},{8,10},{9,11},{10,... | collective-permute-start | bytes 393224 | tf_op jit(solution)/shard_map/ppermute | solution.py:251
  37.7 5.8 %collective-permute-start.7 = (f32[2,48,512]{2,1,0:T(8,128)S(1)}, f32[2,48,512]{2,1,0:T(8,128)S(1)}, u32[]{:S(2)}, u32[]{:S(2)}) collective-permute-start(f32[2,48,512]{2,1,0:T(8,128)S(1)} %slice.56), channel_id=1, source_target_pairs={{0,8},{1,3},{2,10},{3,1},{4,12},{5,7},{6,14},{7,5},{8,0},{9,11},{1... | collective-permute-start | bytes 589832 | tf_op jit(solution)/shard_map/ppermute | solution.py:251
  39.9 4.3 %collective-permute-start.8 = (f32[2,16,512]{2,1,0:T(8,128)S(1)}, f32[2,16,512]{2,1,0:T(8,128)S(1)}, u32[]{:S(2)}, u32[]{:S(2)}) collective-permute-start(f32[2,16,512]{2,1,0:T(8,128)S(1)} %slice.72), channel_id=1, source_target_pairs={{0,4},{1,5},{2,6},{3,7},{4,0},{5,1},{6,2},{7,3},{8,12},{9,13},{10,... | collective-permute-start | bytes 196616 | tf_op jit(solution)/shard_map/ppermute | solution.py:251
  44.3 7.3 %collective-permute-start.9 = (f32[1,64,512]{2,1,0:T(8,128)S(1)}, f32[1,64,512]{2,1,0:T(8,128)S(1)}, u32[]{:S(2)}, u32[]{:S(2)}) collective-permute-start(f32[1,64,512]{2,1,0:T(8,128)S(1)} %pad_maximum_fusion.1), channel_id=1, source_target_pairs={{0,16},{1,17},{2,18},{3,19},{4,20},{5,21},{6,22},{7,23},{8,24},{9,... | collective-permute-start | bytes 393224 | tf_op jit(solution)/shard_map/ppermute | solution.py:251
  51.7 1.4 %collective-permute-start.10 = (f32[64,512]{1,0:T(8,128)S(1)}, f32[64,512]{1,0:T(8,128)S(1)}, u32[]{:S(2)}, u32[]{:S(2)}) collective-permute-start(f32[64,512]{1,0:T(8,128)S(1)} %bitcast.16), channel_id=1, source_target_pairs={{0,1},{1,0},{2,3},{3,2},{4,5},{5,4},{6,7},{7,6},{8,9},{9,8},{10,11... | collective-permute-start | bytes 393224 | tf_op jit(solution)/shard_map/ppermute | solution.py:321
